TPU v7x, 32 devices: a whole 2x2x4 slice. The times are simulated.
32 devices in a mesh: dp: 4 (over y, x), seq: 8 (over z, core).
Axes of the slice: x: 2, y: 2, z: 4, core: 2. Of those that a mesh axis runs over, the one named last changes fastest.
Arguments:
- tokens: int32 [4, 2048], P('dp', 'seq'), may hold values from 0 to 4
- mask_pos: int32 [4, 307], P('dp'), may hold values from 0 to 2047, as said below
- replace_ids: int32 [4, 307], P('dp'), may hold values from 0 to 5
- token_embedding_matrix: bfloat16 [6, 512], replicated, may hold values from -6 to 6
- entry_scale_vector: float32 [512], replicated, may hold values from 0.1 to 1.9
- input_projection_weight: bfloat16 [512, 1152], replicated, may hold values from -0.25 to 0.25
- increment_coefficients: bfloat16 [512, 8], replicated, may hold values from -0.25 to 0.25
- conv_w: float32 [2, 4, 640], replicated, may hold values from -3 to 3
- conv_b: float32 [2, 640], replicated, may hold values from -0.5 to 0.5
- dt_bias: float32 [2, 8], replicated, may hold values from -1 to 1
- decay_rate: float32 [2, 8], replicated, may hold values from 0 to 0.05, as said below
- gain_out: float32 [512], replicated, may hold values from 0.1 to 1.9
- w_out: bfloat16 [512, 512], replicated, may hold values from -0.25 to 0.25
- w_head: bfloat16 [512, 5], replicated, may hold values from -0.25 to 0.25
Outputs:
- layer_out: bfloat16 [4, 2048, 512], P('dp', 'seq')
- grad_w_out: float32 [512, 512], replicated
Inputs may be any that keep to these rules, and one draw needn't show every extreme that they name: `mask_pos`: the 307 positions of one sequence are distinct. `decay_rate`: positive rates.
All inputs are finite; a program needn't handle non-finite values.
Results may differ from a plain program's by a relative error of at most 0.011.
Values may be sent and summed in bfloat16 or wider, within the bound.
No kernel may reach another device: no remote copies, remote signals or barrier semaphores. Data moves between devices by JAX's collectives and lax.ppermute only.
A program may use at most 256 MiB of HBM per device.

v0:
```python
import jax
import jax.numpy as jnp
from jax import lax
from jax.sharding import PartitionSpec as P

HEADS = 8
HEADDIM = 64
STATE = 64
SPAN = 128
KW = 4
INNER = 512


EPSILON = 1e-05


def with_halo(block, sides, width):
    for axis, dim in sides:
        count = lax.axis_size(axis)
        forward = [(i, i + 1) for i in range(count - 1)]
        backward = [(target, source) for source, target in forward]
        low = lax.ppermute(
            lax.slice_in_dim(block, block.shape[dim] - width, None, axis=dim), axis, forward
        )
        high = lax.ppermute(lax.slice_in_dim(block, 0, width, axis=dim), axis, backward)
        block = jnp.concatenate([low, block, high], axis=dim)
    return block


def carried_in(value, axis, join, neutral, backward):
    count, mine = (lax.axis_size(axis), lax.axis_index(axis))
    pieces = jax.tree.map(lambda part: lax.all_gather(part, axis), value)
    if backward:
        pieces = jax.tree.map(lambda part: part[::-1], pieces)
        mine = count - 1 - mine
    so_far = jax.tree.map(
        lambda part, zero: jnp.full_like(part, 0) + jnp.asarray(zero, part.dtype), value, neutral
    )

    def hop(position, so_far):
        longer = join(so_far, jax.tree.map(lambda part: part[position], pieces))
        return jax.tree.map(lambda new, old: jnp.where(position < mine, new, old), longer, so_far)

    return lax.fori_loop(0, count - 1, hop, so_far)


def complement(entry_numbers):
    return jnp.where(entry_numbers < 4, 3 - entry_numbers, entry_numbers)


def row_norm(entry_numbers, gain):
    mean_sq = jnp.mean(entry_numbers * entry_numbers, axis=-1, keepdims=True)
    return entry_numbers * lax.rsqrt(mean_sq + EPSILON) * gain


def silu_slope(entry_numbers):
    sigma = jax.nn.sigmoid(entry_numbers)
    return sigma * (1.0 + entry_numbers * (1.0 - sigma))


def filtered_lines(padded, weights, offset_lines):
    taps = weights.shape[1]
    length = padded.shape[1] - (taps - 1)
    conv_sum = jnp.broadcast_to(
        offset_lines[:, None, :], (padded.shape[0], length, padded.shape[2])
    )
    for offset in range(taps):
        first_row = taps - 1 - offset
        conv_sum = conv_sum + weights[:, offset][:, None, :] * padded[
            :, first_row : first_row + length
        ].astype(jnp.float32)
    return jax.nn.silu(conv_sum).astype(jnp.bfloat16)


def join_states(earlier, later):
    first_decay, first_state = earlier
    second_decay, second_state = later
    return (first_decay * second_decay, second_decay[..., None] * first_state + second_state)


def local_scan(conv_out, step_size, log_decay):
    strands = conv_out.shape[0]
    blocks = conv_out.shape[1] // SPAN
    causal = jnp.arange(SPAN)[:, None] >= jnp.arange(SPAN)[None, :]

    def to_blocks(array_in):
        return jnp.moveaxis(array_in.reshape((strands, blocks, SPAN) + array_in.shape[2:]), 1, 0)

    def from_blocks(array_in):
        moved = jnp.moveaxis(array_in, 0, 1)
        return moved.reshape((strands, blocks * SPAN) + moved.shape[3:])

    def advance(carry_in, block_in):
        carry_state, offset = carry_in
        conv_blk, step_blk, decay_blk = block_in
        x_rows = conv_blk[..., :INNER].reshape(strands, SPAN, HEADS, HEADDIM)
        b_rows = conv_blk[..., INNER : INNER + STATE]
        c_rows = conv_blk[..., INNER + STATE :]
        cum_decay = jnp.swapaxes(jnp.cumsum(decay_blk, axis=1), 1, 2)
        scores = jnp.einsum("sin,sjn->sij", c_rows, b_rows, preferred_element_type=jnp.float32)
        spread = cum_decay[:, :, :, None] - cum_decay[:, :, None, :]
        weights = jnp.where(
            causal,
            scores[:, None]
            * jnp.exp(jnp.where(causal, spread, 0.0))
            * jnp.swapaxes(step_blk, 1, 2)[:, :, None, :],
            0.0,
        ).astype(jnp.bfloat16)
        intra_out = jnp.einsum(
            "shij,sjhp->sihp", weights, x_rows, preferred_element_type=jnp.float32
        )
        cum_rows = jnp.swapaxes(cum_decay, 1, 2)
        carried = jnp.exp(cum_rows)[..., None] * jnp.einsum(
            "sin,shnp->sihp",
            c_rows.astype(jnp.float32),
            carry_state,
            precision=lax.Precision.HIGHEST,
        )
        block_last = cum_decay[:, :, -1]
        scaled = (
            x_rows.astype(jnp.float32)
            * (jnp.exp(block_last[:, None, :] - cum_rows) * step_blk)[..., None]
        ).astype(jnp.bfloat16)
        block_state = jnp.einsum(
            "sjn,sjhp->shnp", b_rows, scaled, preferred_element_type=jnp.float32
        )
        next_state = jnp.exp(block_last)[..., None, None] * carry_state + block_state
        outputs = (intra_out + carried).reshape(strands, SPAN, INNER)
        return ((next_state, offset + block_last), (outputs, offset[:, None, :] + cum_rows))

    initial = (
        jnp.zeros((strands, HEADS, STATE, HEADDIM), jnp.float32),
        jnp.zeros((strands, HEADS), jnp.float32),
    )
    final_carry, stacked = lax.scan(
        advance, initial, (to_blocks(conv_out), to_blocks(step_size), to_blocks(log_decay))
    )
    final_state, final_offset = final_carry
    local_rows, log_rows = stacked
    flat_state = final_state.reshape(strands, HEADS, STATE * HEADDIM)
    return (from_blocks(local_rows), from_blocks(log_rows), flat_state, jnp.exp(final_offset))


def add_incoming(local_rows, log_rows, conv_out, incoming):
    strands = local_rows.shape[0]
    length = local_rows.shape[1]
    c_rows = conv_out[..., INNER + STATE :].astype(jnp.float32)
    state_in = incoming.reshape(strands, HEADS, STATE, HEADDIM)
    extra = jnp.exp(log_rows)[..., None] * jnp.einsum(
        "sln,shnp->slhp", c_rows, state_in, precision=lax.Precision.HIGHEST
    )
    return local_rows + extra.reshape(strands, length, INNER)


def run_strands(both_ids, up_pick, down_pick, weights_all):
    (
        token_embedding_matrix,
        entry_scale_vector,
        input_projection_weight,
        increment_coefficients,
        conv_w,
        conv_b,
        dt_bias,
        decay_rate,
        gain_out,
    ) = weights_all
    strands = both_ids.shape[0]
    length = both_ids.shape[1]
    up_index = jnp.array(up_pick)
    down_index = jnp.array(down_pick)
    one_hot_targets = (
        both_ids[..., None] == jnp.arange(token_embedding_matrix.shape[0])[None, None, :]
    ).astype(jnp.bfloat16)
    embedded = jnp.einsum(
        "kan,nc->kac", one_hot_targets, token_embedding_matrix, preferred_element_type=jnp.float32
    ).astype(jnp.bfloat16)
    rescaled_lines = row_norm(embedded.astype(jnp.float32), entry_scale_vector).astype(jnp.bfloat16)
    projected_rows = jnp.einsum(
        "wrm,mg->wrg", rescaled_lines, input_projection_weight, preferred_element_type=jnp.float32
    ).astype(jnp.bfloat16)
    unactivated_step = jnp.einsum(
        "sym,mi->syi", rescaled_lines, increment_coefficients, preferred_element_type=jnp.float32
    )
    gate_part = projected_rows[..., :INNER]
    mixed_in = projected_rows[..., INNER:]
    rim_width = KW - 1
    padded = with_halo(mixed_in, (("seq", 1),), KW - 1)
    up_conv = filtered_lines(padded[:, : length + rim_width], conv_w[up_index], conv_b[up_index])
    down_conv = filtered_lines(
        jnp.flip(padded, 1)[:, : length + rim_width], conv_w[down_index], conv_b[down_index]
    )
    up_step = jax.nn.softplus(unactivated_step + dt_bias[up_index][:, None, :])
    down_step = jax.nn.softplus(jnp.flip(unactivated_step, 1) + dt_bias[down_index][:, None, :])
    identity = (
        jnp.ones((strands, HEADS), jnp.float32),
        jnp.zeros((strands, HEADS, STATE * HEADDIM), jnp.float32),
    )
    up_local, up_logs, up_state, up_decay = local_scan(
        up_conv, up_step, -up_step * decay_rate[up_index][:, None, :]
    )
    up_in = carried_in((up_decay, up_state), "seq", join_states, identity, False)
    up_out = add_incoming(up_local, up_logs, up_conv, up_in[1])
    down_local, down_logs, down_state, down_decay = local_scan(
        down_conv, down_step, -down_step * decay_rate[down_index][:, None, :]
    )
    down_in = carried_in((down_decay, down_state), "seq", join_states, identity, True)
    down_out = jnp.flip(add_incoming(down_local, down_logs, down_conv, down_in[1]), 1)
    gated_out = (up_out + down_out) * jax.nn.silu(gate_part.astype(jnp.float32))
    per_head = gated_out.reshape(strands, length, HEADS, HEADDIM)
    mean_sq = jnp.mean(per_head * per_head, axis=-1, keepdims=True)
    normed_out = (per_head * lax.rsqrt(mean_sq + EPSILON)).reshape(
        strands, length, INNER
    ) * gain_out
    return normed_out.astype(jnp.bfloat16)


def per_device(
    tokens,
    mask_pos,
    replace_ids,
    token_embedding_matrix,
    entry_scale_vector,
    input_projection_weight,
    increment_coefficients,
    conv_w,
    conv_b,
    dt_bias,
    decay_rate,
    gain_out,
    w_out,
    w_head,
):
    length = tokens.shape[1]
    seq_rank = lax.axis_index("seq")
    own_ids = tokens[0]
    local_pos = mask_pos[0] - seq_rank * length
    inside = (local_pos >= 0) & (local_pos < length)
    target_rows = jnp.where(inside, local_pos, length)
    input_ids = own_ids.at[target_rows].set(replace_ids[0], mode="drop")
    masked = jnp.zeros((length,), jnp.float32).at[target_rows].set(1.0, mode="drop")
    weights_all = (
        token_embedding_matrix,
        entry_scale_vector,
        input_projection_weight,
        increment_coefficients,
        conv_w,
        conv_b,
        dt_bias,
        decay_rate,
        gain_out,
    )
    both_ids = jnp.stack([input_ids, complement(input_ids)])
    strand_out = run_strands(both_ids, (0, 1), (1, 0), weights_all)
    combined = (strand_out[0].astype(jnp.float32) + strand_out[1].astype(jnp.float32)).astype(
        jnp.bfloat16
    )
    layer_out = jnp.dot(combined, w_out, preferred_element_type=jnp.float32).astype(jnp.bfloat16)
    layer_f32 = layer_out.astype(jnp.float32)
    activated = jax.nn.silu(layer_f32)
    class_scores_raw = jnp.dot(
        activated, w_head.astype(jnp.float32), precision=lax.Precision.HIGHEST
    )
    exp_logits = jnp.exp(class_scores_raw)
    prob_rows = exp_logits / jnp.sum(exp_logits, axis=-1, keepdims=True)
    target = (own_ids[:, None] == jnp.arange(w_head.shape[1])[None, :]).astype(jnp.float32)
    total_masked = lax.axis_size("dp") * mask_pos.shape[1]
    grad_logits = masked[:, None] * (prob_rows - target) / total_masked
    grad_act = jnp.dot(grad_logits, w_head.astype(jnp.float32).T, precision=lax.Precision.HIGHEST)
    grad_layer = (grad_act * silu_slope(layer_f32)).astype(jnp.bfloat16)
    local_grad = jnp.einsum("li,ld->id", combined, grad_layer, preferred_element_type=jnp.float32)
    grad_w_out = lax.psum(local_grad, ("dp", "seq"))
    return (layer_out[None], grad_w_out)


def solution(mesh):
    in_specs = (
        P("dp", "seq"),
        P("dp", None),
        P("dp", None),
        P(),
        P(),
        P(),
        P(),
        P(),
        P(),
        P(),
        P(),
        P(),
        P(),
        P(),
    )
    out_specs = (P("dp", "seq", None), P())
    return jax.shard_map(
        per_device, mesh=mesh, in_specs=in_specs, out_specs=out_specs, check_vma=False
    )
```

profile of v0, /device:TPU:0, one launch (start us, length us, event | category | flops | bytes accessed | tf_op | source)
XLA Modules:
  0.0 335.1 jit_solution(6303383522832163228)
XLA Ops:
  9.4 2.9 scatter_fusion
  13.9 1.0 copy-done.22
  15.5 1.3 collective-permute-start.1
  16.8 3.6 %collective-permute-start = (bf16[2,3,640]{2,1,0:T(4,128)(2,1)}, bf16[2,3,640]{2,1,0:T(4,128)(2,1)}, u32[]{:S(2)}, u32[]{:S(2)}) collective-permute-start(bf16[2,3,640]{2,1,0:T(4,128)(2,1)} %get-tuple-element.512), channel_id=1, source_target_pairs={{0,1},{1,2},{2,3},{3,4},{4,5},{5,6},{6,7},{8,9},{9,10},{10,11},{11... | collective-permute-start | bytes 23048 | tf_op jit(solution)/shard_map/ppermute | solution.py:22
  28.3 1.1 slice.179
  29.5 1.1 gather_fusion.6
  30.6 1.1 gather_fusion.2
  33.4 1.6 copy.93
  34.9 1.6 copy.82
  37.3 3.6 %scatter_custom_fusion.1 = f32[256]{0:T(256)} fusion(s32[307]{0:T(512)} %copy-done.37, f32[307]{0:T(512)S(1)} %broadcast.152, f32[]{:T(128)} %constant.120.clone.1), kind=kCustom, calls=%fused_computation.175 | custom fusion | bytes 1536 | tf_op jit(solution)/shard_map/scatter | solution.py:240
  40.9 2.3 fusion.51
  43.3 10.0 %slice.133 = bf16[2,256,640]{2,1,0:T(8,128)(2,1)} reverse(bf16[2,256,640]{2,1,0:T(8,128)(2,1)} %get-tuple-element.515), dimensions={1} | reverse | bytes 1310720 | tf_op jit(solution)/shard_map/slice | solution.py:69
  53.3 10.0 %slice.130 = bf16[2,256,640]{2,1,0:T(8,128)(2,1)} reverse(bf16[2,256,640]{2,1,0:T(8,128)(2,1)} %get-tuple-element.516), dimensions={1} | reverse | bytes 1310720 | tf_op jit(solution)/shard_map/slice | solution.py:69
  63.3 6.4 %slice.127 = bf16[2,256,640]{2,1,0:T(8,128)(2,1)} reverse(bf16[2,256,640]{2,1,0:T(8,128)(2,1)S(1)} %copy-done.20), dimensions={1} | reverse | bytes 1310720 | tf_op jit(solution)/shard_map/slice | solution.py:69
  69.7 2.3 multiply_convert_fusion.4
  72.0 1.1 copy.92
  73.1 1.0 broadcast.145.clone
  74.1 18.7 %while.67 = (s32[]{:T(128)}, f32[2,8,64,64]{2,3,1,0:T(8,128)S(1)}, f32[2,8]{1,0:T(2,128)S(1)}, f32[2,2,128,512]{2,3,1,0:T(8,128)}, f32[2,2,128,8]{2,3,0,1:T(8,12...) while((s32[]{:T(128)}, f32[2,8,64,64]{2,3,1,0:T(8,128)S(1)}, ...), condition=%wide.region_9.10_spmd.clone.clone, body=%wide.region_7.9_spmd.clone.clone.sunk | while | flops 157896736 | bytes 15402852 | solution.py:135
  74.2 1.1 dynamic-slice_bitcast_fusion.18
  77.2 1.2 fusion.160
  80.7 1.7 fusion.162
  83.5 1.1 dynamic-slice_bitcast_fusion.18
  86.6 1.2 fusion.160
  90.0 1.7 fusion.162
  92.8 13.6 %all-gather.3 = f32[8,2,8]{2,1,0:T(2,128)S(1)} all-gather(f32[1,2,8]{2,1,0:T(2,128)S(1)} %exponential_bitcast_fusion.2), channel_id=3, replica_groups=mesh['dp'=4,'seq'=8] {'seq'}, dimensions={0}, use_global_device_ids=true | all-gather | bytes 576 | tf_op jit(solution)/shard_map/all_gather | solution.py:32
  107.0 1.0 copy.96
  108.0 1.9 all_gather_reshape.7
  110.2 1.3 copy.94
  111.6 1.7 multiply_convert_fusion.5
  113.3 1.1 copy.83
  114.4 1.0 broadcast.145.clone.1
  115.5 13.6 %while.66 = (s32[]{:T(128)}, f32[2,8,64,64]{2,3,1,0:T(8,128)S(1)}, f32[2,8]{1,0:T(2,128)S(1)}, f32[2,2,128,512]{2,3,1,0:T(8,128)}, f32[2,2,128,8]{2,3,0,1:T(8,12...) while((s32[]{:T(128)}, f32[2,8,64,64]{2,3,1,0:T(8,128)S(1)}, ...), condition=%wide.region_4.5_spmd.clone.clone, body=%wide.region_2.4_spmd.clone.clone.sunk | while | flops 157896736 | bytes 15271724 | solution.py:135
  115.5 1.0 dynamic-slice_bitcast_fusion.16
  117.2 1.2 fusion.148
  119.5 1.8 fusion.150
  122.3 1.0 dynamic-slice_bitcast_fusion.16
  124.0 1.2 fusion.148
  126.3 1.8 fusion.150
  130.3 1.3 copy.85
  131.6 9.5 %all-gather.2 = f32[8,2,8]{2,1,0:T(2,128)} all-gather(f32[1,2,8]{2,1,0:T(2,128)S(1)} %exponential_bitcast_fusion.3), channel_id=2, replica_groups=mesh['dp'=4,'seq'=8] {'seq'}, dimensions={0}, use_global_device_ids=true | all-gather | bytes 576 | tf_op jit(solution)/shard_map/all_gather | solution.py:32
  142.4 1.7 rev.18
  144.2 5.4 %while.65 = (s32[]{:T(128)}, f32[2,8,4096]{2,1,0:T(8,128)S(1)}, s32[]{:T(128)}, f32[8,2,8]{2,1,0:T(2,128)}, f32[8,2,8,4096]{3,2,1,0:T(8,128)S(1)}, /*index=5*/s32[]{:T(128)}, s32[]{:T(128)}) while((s32[]{:T(128)}, f32[2,8,4096]{2,1,0:T(8,128)S(1)}, s32[]{:T(128)}, f32[8,2,8]{2,1,0:T(2,128)}, f32[8,2,8,4096]{3,2,1,0:T(8,128)S(1)}, ...), condition=%wide.region_11.12_spmd.clone, body=%wide.region_10.11_spmd.clone.sunk | while | flops 262148 | bytes 786737 | solution.py:44
  150.1 1.6 fusion.65
  151.6 1.1 broadcast_multiply_fusion
  152.7 1.6 copy.99
  154.4 1.2 bitcast_add_fusion.4
  155.6 8.9 %rev.19 = f32[2,256,512]{2,1,0:T(8,128)} reverse(f32[2,256,512]{2,1,0:T(8,128)} %bitcast_add_fusion.4), dimensions={1} | reverse | bytes 2097152 | tf_op jit(solution)/shard_map/jit(_flip)/rev | solution.py:207
  164.5 6.5 %all-gather.7.cloned.1.call-done = f32[8,2,8,4096]{3,2,1,0:T(8,128)} async-done(((f32[1,2,8,4096]{3,2,1,0:T(8,128)}), f32[8,2,8,4096]{3,2,1,0:T(8,128)}) %all-gather.7.cloned.1.call-update) | async-done | bytes 2097168 | tf_op jit(solution)/shard_map/all_gather | solution.py:32
  171.0 12.0 %while.64 = (s32[]{:T(128)}, f32[2,8,4096]{2,1,0:T(8,128)S(1)}, s32[]{:T(128)}, f32[8,2,8]{2,1,0:T(2,128)}, f32[8,2,8,4096]{3,2,1,0:T(8,128)}, /*index=5*/s32[]{:T(128)}, s32[]{:T(128)}) while((s32[]{:T(128)}, f32[2,8,4096]{2,1,0:T(8,128)S(1)}, s32[]{:T(128)}, f32[8,2,8]{2,1,0:T(2,128)}, f32[8,2,8,4096]{3,2,1,0:T(8,128)}, ...), condition=%wide.region_6.7_spmd.clone, body=%wide.region_5.6_spmd.clone.sunk | while | flops 262148 | bytes 786737 | solution.py:44
  171.6 1.0 fusion.137
  173.3 1.0 fusion.137
  175.0 1.0 fusion.137
  176.8 1.0 fusion.137
  178.5 1.0 fusion.137
  180.1 1.0 fusion.137
  181.9 1.0 fusion.137
  183.4 1.6 fusion.67
  185.1 1.3 copy.90
  186.4 3.4 %fusion.93 = (f32[2,256,512]{2,1,0:T(8,128)}, f32[2,256,512]{2,1,0:T(8,128)}) fusion(bf16[2,256,1152]{2,1,0:T(8,128)(2,1)} %copy-done.22, f32[2,256,512]{2,1,0:T(8,128)} %rev.19, f32[2,256,512]{2,1,0:T(8,128)} %copy.90, f32[2,2,128,512]{3,2,1,0:T(8,128)S(1)} %copy-done.15), kind=kLoop, calls=%fused_computation.181 | loop fusion | flops 2359296 | bytes 5767168 | tf_op jit(solution)/shard_map/mul | solution.py:210
  189.8 1.6 copy.100
  192.3 1.5 multiply_convert_fusion.6
  195.4 1.3 fusion.69
  196.8 129.5 %all-reduce.2.cloned.1.call-done = f32[512,512]{1,0:T(8,128)} async-done(((f32[512,512]{1,0:T(8,128)}), f32[512,512]{1,0:T(8,128)}) %all-reduce.2.cloned.1.call-update) | async-done | bytes 1048592 | tf_op jit(solution)/shard_map/psum | solution.py:271
  326.3 2.3 copy.200
  (272 shorter events, 47.2 us)
Async XLA Ops:
  7.2 5.7 %copy-start = (bf16[512,1152]{1,0:T(8,128)(2,1)S(1)}, bf16[512,1152]{1,0:T(8,128)(2,1)}, u32[]{:S(2)}) copy-start(bf16[512,1152]{1,0:T(8,128)(2,1)} %param.29) | copy-start | bytes 3538948
  7.2 135.2 %all-gather.9.cloned.1.call-start = ((), (), s32[]{:S(2)}) async-start(), calls=%async_computation.1 | async-start | bytes 2359296 | tf_op jit(solution)/shard_map/all_gather | solution.py:32
  8.7 3.7 %copy-start.37 = (s32[307]{0:T(512)}, s32[307]{0:T(512)S(1)}, u32[]{:S(2)}) copy-start(s32[307]{0:T(512)S(1)} %fusion.86) | copy-start | bytes 3688
  9.4 3.0 copy-start.42
  9.4 3.5 %copy-start.45 = (f32[512]{0:T(512)S(1)}, f32[512]{0:T(512)}, u32[]{:S(2)}) copy-start(f32[512]{0:T(512)} %param.28) | copy-start | bytes 6148
  12.9 7.6 %copy-start.40 = (s32[2]{0:T(128)S(1)}, s32[2]{0:T(128)}, u32[]{:S(2)}) copy-start(s32[2]{0:T(128)} %constant.141) | copy-start | bytes 28
  12.9 7.6 %copy-start.23 = (f32[2,8]{1,0:T(2,128)S(1)}, f32[2,8]{1,0:T(2,128)}, u32[]{:S(2)}) copy-start(f32[2,8]{1,0:T(2,128)} %param.33) | copy-start | bytes 196
  12.9 8.1 %copy-start.24 = (f32[2,8]{1,0:T(2,128)S(1)}, f32[2,8]{1,0:T(2,128)}, u32[]{:S(2)}) copy-start(f32[2,8]{1,0:T(2,128)} %param.34) | copy-start | bytes 196
  12.9 9.8 %copy-start.25 = (f32[2,4,640]{2,1,0:T(4,128)S(1)}, f32[2,4,640]{2,1,0:T(4,128)}, u32[]{:S(2)}) copy-start(f32[2,4,640]{2,1,0:T(4,128)} %param.31) | copy-start | bytes 61444
  12.9 11.0 %copy-start.43 = (bf16[512,8]{0,1:T(8,128)(2,1)S(1)}, bf16[512,8]{0,1:T(8,128)(2,1)}, u32[]{:S(2)}) copy-start(bf16[512,8]{0,1:T(8,128)(2,1)} %param.30) | copy-start | bytes 24580
  13.9 1.0 copy-start.22
  15.5 25.4 %collective-permute-start.1 = (bf16[2,3,640]{2,1,0:T(4,128)(2,1)}, bf16[2,3,640]{2,1,0:T(4,128)(2,1)}, u32[]{:S(2)}, u32[]{:S(2)}) collective-permute-start(bf16[2,3,640]{2,1,0:T(4,128)(2,1)} %get-tuple-element.513), channel_id=1, source_target_pairs={{1,0},{2,1},{3,2},{4,3},{5,4},{6,5},{7,6},{9,8},{10,9},{11,10},{12... | collective-permute-start | bytes 23048 | tf_op jit(solution)/shard_map/ppermute | solution.py:25
  16.8 94.7 %collective-permute-start = (bf16[2,3,640]{2,1,0:T(4,128)(2,1)}, bf16[2,3,640]{2,1,0:T(4,128)(2,1)}, u32[]{:S(2)}, u32[]{:S(2)}) collective-permute-start(bf16[2,3,640]{2,1,0:T(4,128)(2,1)} %get-tuple-element.512), channel_id=1, source_target_pairs={{0,1},{1,2},{2,3},{3,4},{4,5},{5,6},{6,7},{8,9},{9,10},{10,11},{11... | collective-permute-start | bytes 23048 | tf_op jit(solution)/shard_map/ppermute | solution.py:22
  23.9 5.6 %copy-start.21 = (f32[2,640]{1,0:T(2,128)S(1)}, f32[2,640]{1,0:T(2,128)}, u32[]{:S(2)}) copy-start(f32[2,640]{1,0:T(2,128)} %param.32) | copy-start | bytes 15364
  29.4 13.9 %copy-start.1 = (bf16[2,256,640]{2,1,0:T(8,128)(2,1)}, bf16[2,256,640]{2,1,0:T(8,128)(2,1)S(1)}, u32[]{:S(2)}) copy-start(bf16[2,256,640]{2,1,0:T(8,128)(2,1)S(1)} %slice.179) | copy-start | bytes 1966084
  43.3 20.0 %copy-start.20 = (bf16[2,256,640]{2,1,0:T(8,128)(2,1)S(1)}, bf16[2,256,640]{2,1,0:T(8,128)(2,1)}, u32[]{:S(2)}) copy-start(bf16[2,256,640]{2,1,0:T(8,128)(2,1)} %get-tuple-element.514) | copy-start | bytes 1966084
  53.3 16.4 %copy-start.35 = (f32[2,640]{1,0:T(2,128)S(1)}, f32[2,640]{1,0:T(2,128)}, u32[]{:S(2)}) copy-start(f32[2,640]{1,0:T(2,128)} %get-tuple-element.533) | copy-start | bytes 15364
  53.3 16.4 %copy-start.36 = (f32[2,640]{1,0:T(2,128)S(1)}, f32[2,640]{1,0:T(2,128)}, u32[]{:S(2)}) copy-start(f32[2,640]{1,0:T(2,128)} %get-tuple-element.534) | copy-start | bytes 15364
  71.9 2.2 copy-start.19
  72.0 2.2 copy-start.29
  74.1 1.2 copy-start.4
  74.1 1.2 copy-start.17
  74.2 2.0 copy-start.5
  80.6 1.7 copy-start.9
  82.4 1.0 copy-start.10
  83.5 1.2 copy-start.4
  83.5 1.2 copy-start.17
  83.5 2.0 copy-start.5
  90.0 1.7 copy-start.9
  91.7 1.0 copy-start.10
  92.8 17.4 %copy-start.11 = (f32[2,2,128,512]{2,3,1,0:T(8,128)S(1)}, f32[2,2,128,512]{2,3,1,0:T(8,128)}, u32[]{:S(2)}) copy-start(f32[2,2,128,512]{2,3,1,0:T(8,128)} %get-tuple-element.301) | copy-start | bytes 3145732
  109.9 1.6 copy-start.2
  109.9 1.6 copy-start.30
  109.9 1.6 copy-start.31
  109.9 1.6 copy-start.32
  109.9 1.6 copy-start.33
  109.9 1.6 copy-start.34
  110.0 61.0 %all-gather.7.cloned.1.call-start = ((), (), s32[]{:S(2)}) async-start(), calls=%async_computation | async-start | bytes 2359296 | tf_op jit(solution)/shard_map/all_gather | solution.py:32
  113.3 2.2 copy-start.18
  113.3 2.1 copy-start.3
  113.3 2.1 copy-start.28
  115.5 1.1 copy-start.16
  119.5 1.8 copy-start.12
  121.3 1.0 copy-start.13
  122.3 1.1 copy-start.16
  126.3 1.8 copy-start.12
  128.1 1.0 copy-start.13
  129.1 1.2 copy-start.14
  142.3 1.8 copy-start.7
  142.4 183.9 %all-reduce.2.cloned.1.call-start = ((), (), s32[]{:S(2)}) async-start(), calls=%async_computation.2 | async-start | bytes 2097152 | tf_op jit(solution)/shard_map/psum | solution.py:271
  149.9 1.8 copy-start.27
  152.7 1.7 copy-start.8
  155.6 15.4 %copy-start.6 = (f32[2,8,4096]{2,1,0:T(8,128)S(1)}, f32[2,8,4096]{2,1,0:T(8,128)}, u32[]{:S(2)}) copy-start(f32[2,8,4096]{2,1,0:T(8,128)} %custom-call) | copy-start | bytes 786436
  183.2 1.8 copy-start.26
  185.1 1.3 copy-start.15
  191.6 0.7 copy-start.38
  192.3 1.5 copy-start.41
  192.3 1.9 copy-start.44
  194.1 1.3 copy-start.46
  194.2 0.7 copy-start.39
  194.2 0.7 copy-start.47
Sparse Core Ops, SparseCore 0:
  110.1 27.3 all-gather.8
  142.5 28.4 all-gather.6
  196.9 129.3 all-reduce.1
where the time goes:
time: 339 us; the launch traced here: 335 us
  waiting for transfers between devices  136 us (40%)
  local copies, waits for them, and re-layouts  106 us (31%)
  other arithmetic  27.2 us (8%)
  blocking collectives  23.1 us (7%)
  matrix products  22.2 us (7%)
  between operations  14.5 us (4%)
  starting transfers between devices  5.21 us (2%)
    psum x1, waiting for transfers between devices, per_device(): grad_w_out = lax.psum(local_grad, ('dp', 'seq'))  130 us
    slice x4, local copies, waits for them, and re-layouts, filtered_lines(): padded[:, first_row:first_row + length].astype(jnp.float32)  27.2 us
    all_gather x2, blocking collectives, carried_in(): pieces = jax.tree.map(lambda part: lax.all_gather(part, axis), value)  23.1 us
    mul x14, local copies, waits for them, and re-layouts, join_states(): second_decay[..., None] * first_state + second_state  9.12 us
    rev x1, local copies, waits for them, and re-layouts, run_strands(): jnp.flip(add_incoming(down_local, down_logs, down_conv, down_in[1]), 1)  8.9 us
    select_n x14, other arithmetic, hop(): jnp.where(position < mine, new, old)  8.04 us
    unnamed x88, local copies, waits for them, and re-layouts  7.31 us
    reshape x6, local copies, waits for them, and re-layouts, to_blocks(): array_in.reshape((strands, blocks, SPAN) + array_in.shape[2:])  7 us
  transfers between devices with their start and end apart: 5, of which 2 were waited for; matrix products, arithmetic and copies ran while one was open for 35% of the time, Pallas kernels for 0%

commit v1 on v0

v1 whole, which is shorter than its diff:
```python
import functools

import jax
import jax.numpy as jnp
from jax import lax
from jax.experimental import pallas as pl
from jax.experimental.pallas import tpu as pltpu
from jax.sharding import PartitionSpec as P

HEADS = 8
HEADDIM = 64
STATE = 64
SPAN = 128
KW = 4
INNER = 512
CONVW = 640
EPSILON = 1e-05
F32 = jnp.float32
BF16 = jnp.bfloat16
HIGH = lax.Precision.HIGHEST
NN = (((1,), (0,)), ((), ()))
NT = (((1,), (1,)), ((), ()))
TN = (((0,), (0,)), ((), ()))


def mm(a, b, dims=NN, precision=None):
    return lax.dot_general(a, b, dims, precision=precision, preferred_element_type=F32)


def split_two(value):
    high = value.astype(BF16)
    return high, (value - high.astype(F32)).astype(BF16)


def eye(rows, cols, dtype=F32):
    return (
        lax.broadcasted_iota(jnp.int32, (rows, cols), 0)
        == lax.broadcasted_iota(jnp.int32, (rows, cols), 1)
    ).astype(dtype)


def silu_half(half):
    return half + half * jnp.tanh(half)


def tables_kernel(
    emb_ref, scale_ref, win_ref, inc_ref, cw_ref, cb_ref, dtb_ref, rate_ref, gain_ref, head_ref,
    conv_out, gate_out, step_out, decay_out, gain_out, head_out,
):
    emb = emb_ref[...].astype(F32)
    none = jnp.zeros((2, emb.shape[1]), F32)
    rows = jnp.concatenate(
        [emb, none, emb[3:4], emb[2:3], emb[1:2], emb[0:1], emb[4:6], none], axis=0
    )
    mean_sq = jnp.mean(rows * rows, axis=-1, keepdims=True)
    normed = (rows * lax.rsqrt(mean_sq + EPSILON) * scale_ref[...]).astype(BF16)
    projected = mm(normed, win_ref[...]).astype(BF16).astype(F32)
    raw = mm(normed, inc_ref[...])
    raw_t = mm(eye(HEADS, HEADS), raw, NT, HIGH)
    dtb_t = mm(eye(HEADS, HEADS), dtb_ref[...], NT, HIGH)
    rate_t = mm(eye(HEADS, HEADS), rate_ref[...], NT, HIGH)
    gate = projected[:, :INNER] * 0.5
    gate_t = jnp.transpose(silu_half(gate))
    mixed = projected[:, INNER:]
    for strand in range(2):
        high, low = split_two(gate_t[:, strand * 8 : strand * 8 + 8])
        gate_out[strand * INNER : (strand + 1) * INNER, :] = jnp.concatenate([high, low], axis=1)
    for side in range(2):
        for strand in range(2):
            param = side ^ strand
            mine = mixed[strand * 8 : strand * 8 + 8]
            taps = [cw_ref[param, j : j + 1, :] * mine for j in range(KW)]
            taps[0] = taps[0] + cb_ref[param : param + 1, :]
            table = jnp.transpose(jnp.concatenate(taps, axis=0) * 0.5)
            high, low = split_two(table)
            conv_out[side, strand * CONVW : (strand + 1) * CONVW, :] = jnp.concatenate(
                [high, low], axis=1
            )
            step = jax.nn.softplus(
                raw_t[:, strand * 8 : strand * 8 + 8] + dtb_t[:, param : param + 1]
            )
            step_out[side, strand] = step
            decay_out[side, strand] = -step * rate_t[:, param : param + 1]
    gain_out[...] = jnp.transpose(jnp.broadcast_to(gain_ref[...], (128, INNER)))
    head_out[...] = mm(eye(8, head_ref.shape[1], BF16), head_ref[...], NT).astype(BF16)


def pick(table, ids):
    total = jnp.zeros((table.shape[0], ids.shape[1]), F32)
    for entry in range(6):
        total = jnp.where(ids == entry, table[:, entry : entry + 1], total)
    return total


def layer_kernel(
    n, length, masked_total,
    tok_ref, pos_ref, rep_ref, conv_ref, gate_ref, step_ref, decay_ref, gain_ref, headt_ref, wout_ref,
    layer_out, send_out, keep_out,
    pos_s, rep_s, ids_s, val_s, step_s, log_s, cum_s, tot_s, scaled_s, state_s, y_s, comb_s,
):
    me = lax.axis_index("seq")
    nb = length // SPAN
    blocks = n * nb
    masks = pos_ref.shape[1]
    wide = pos_s.shape[1]
    unrolled = n <= 16
    rows = 2 * nb * 8

    def loop(count, body):
        if unrolled:
            for k in range(count):
                body(k)
        else:
            pl.loop(0, count)(body)

    pos_s[...] = jnp.full_like(pos_s, -1)
    rep_s[...] = jnp.zeros_like(rep_s)
    pos_s[:, :masks] = pos_ref[...]
    rep_s[:, :masks] = rep_ref[...]
    pos = pos_s[...]
    block_hit = lax.broadcasted_iota(jnp.int32, (blocks, wide), 0) == (pos >> 7)
    put = jnp.where(block_hit, (rep_s[...] + 1).astype(F32), 0.0).astype(BF16)
    lane_hit = (lax.broadcasted_iota(jnp.int32, (SPAN, wide), 0) == (pos & 127)) & (pos >= 0)
    val_s[...] = mm(put, lane_hit.astype(F32).astype(BF16), NT)
    nothing = jnp.full((1, length), -1.0, F32)
    ids_s[0:1, :] = nothing
    ids_s[n + 1 : n + 2, :] = nothing

    def values_of(unit):
        return jnp.concatenate(
            [val_s[pl.ds(unit * nb + b, 1), :] for b in range(nb)], axis=1
        )

    def place(k):
        unit = me ^ k
        put_here = values_of(unit)
        own = tok_ref[pl.ds(k, 1), :].astype(F32)
        ids_s[pl.ds(unit + 1, 1), :] = jnp.where(put_here > 0.5, put_here - 1.0, own)

    loop(n, place)

    lane = lax.broadcasted_iota(jnp.int32, (1, length), 1)
    sub8 = lax.broadcasted_iota(jnp.int32, (8, length), 0).astype(F32)

    def one_hots(unit, side):
        here = ids_s[pl.ds(unit + 1, 1), :]
        beside = ids_s[pl.ds(unit + 2 * side, 1), :]
        out = [(sub8 == here).astype(F32)]
        for j in range(1, KW):
            if isinstance(side, int):
                shift = j if side == 0 else length - j
                border = (lane < j) if side == 0 else (lane >= length - j)
            else:
                shift = jnp.where(side == 0, j, length - j)
                border = jnp.where(side == 0, lane, length - 1 - lane) < j
            moved = jnp.where(
                border, pltpu.roll(beside, shift, 1), pltpu.roll(here, shift, 1)
            )
            out.append((sub8 == moved).astype(F32))
        hot = jnp.concatenate(out, axis=0).astype(BF16)
        return jnp.concatenate([hot, hot], axis=0)

    def slot_of(k):
        before = k < me
        unit = jnp.where(before, me - 1 - k, k + 1)
        side = jnp.where(before, 0, 1)
        return unit, side

    def fill(slot, unit, side):
        here = ids_s[pl.ds(unit + 1, 1), :]
        for source, target in ((step_ref, step_s), (decay_ref, log_s)):
            parts = []
            for strand in range(2):
                full = pick(source[side, strand], here)
                parts += [full[:, b * SPAN : (b + 1) * SPAN] for b in range(nb)]
            target[slot] = jnp.concatenate(parts, axis=0)

    def fill_other(k):
        unit, side = slot_of(k)
        fill(k, unit, side)

    loop(n - 1, fill_other)
    fill(n - 1, me, 0)
    fill(n, me, 1)
    logs = log_s[...].reshape((n + 1) * rows, SPAN)
    before = (
        lax.broadcasted_iota(jnp.int32, (SPAN, SPAN), 0)
        <= lax.broadcasted_iota(jnp.int32, (SPAN, SPAN), 1)
    ).astype(F32)
    cum = mm(logs, before, NN, HIGH).reshape(n + 1, rows, SPAN)
    cum_s[...] = cum
    tot_s[...] = jnp.broadcast_to(cum[:, :, SPAN - 1 :], cum.shape)

    def part(array, strand, b):
        start = (strand * nb + b) * 8
        return array[start : start + 8]

    def weigh(k, far):
        side_back = k >= me
        far = [jnp.where(k == me, 0.0, value) for value in far]
        steps, cums, logs_k, tots = step_s[k], cum_s[k], log_s[k], tot_s[k]
        new = []
        parts = [None] * (2 * nb)
        for strand in range(2):
            whole = sum(part(tots, strand, b) for b in range(nb))
            ahead = jnp.zeros((8, SPAN), F32)
            for b in range(nb):
                behind = whole - ahead - part(tots, strand, b)
                e_fwd = part(tots, strand, b) - part(cums, strand, b) + behind
                e_bwd = part(cums, strand, b) - part(logs_k, strand, b) + ahead
                e = jnp.where(side_back, e_bwd, e_fwd) + far[strand]
                parts[strand * nb + b] = part(steps, strand, b) * jnp.exp(e)
                ahead = ahead + part(tots, strand, b)
            new.append(far[strand] + whole)
        step_s[k] = jnp.concatenate(parts, axis=0)
        return new

    far = [jnp.zeros((8, SPAN), F32)] * 2
    if unrolled:
        for k in range(n - 1):
            far = weigh(k, far)
    else:
        lax.fori_loop(0, n - 1, lambda k, c: tuple(weigh(k, list(c))), tuple(far))

    state_s[...] = jnp.zeros_like(state_s)

    def across(array, strand):
        return jnp.concatenate([part(array, strand, b) for b in range(nb)], axis=1)

    def per_head(x, row8, first):
        return jnp.concatenate(
            [
                x[h * HEADDIM : (h + 1) * HEADDIM] * row8[first + h : first + h + 1]
                for h in range(x.shape[0] // HEADDIM)
            ],
            axis=0,
        )

    def gather_state(k):
        unit, side = slot_of(k)
        hot = one_hots(unit, side)
        weight = step_s[k]
        for strand in range(2):
            row8 = across(weight, strand)
            base = strand * CONVW
            slot = (k * 2 + strand) % 4
            for c in range(4):
                half = mm(conv_ref[side, base + c * 128 : base + (c + 1) * 128, :], hot)
                scaled_s[slot, c * 128 : (c + 1) * 128, :] = per_head(
                    silu_half(half), row8, 2 * c
                ).astype(BF16)
            b_t = silu_half(mm(conv_ref[side, base + INNER : base + INNER + STATE, :], hot))
            state_s[side, strand] += mm(scaled_s[slot], b_t.astype(BF16), NT)

    loop(n - 1, gather_state)

    row_i = lax.broadcasted_iota(jnp.int32, (SPAN, SPAN), 0)
    col_i = lax.broadcasted_iota(jnp.int32, (SPAN, SPAN), 1)
    for side in range(2):
        hot = one_hots(me, side)
        slot = n - 1 + side
        steps, cums, logs_k, tots = step_s[slot], cum_s[slot], log_s[slot], tot_s[slot]
        if side == 1:
            cums = tots - cums + logs_k
        cols = jnp.transpose(cums)
        for strand in range(2):
            base = strand * CONVW
            row8 = across(steps, strand)
            buf = side * 2 + strand
            for c in range(4):
                half = mm(conv_ref[side, base + c * 128 : base + (c + 1) * 128, :], hot)
                scaled_s[buf, c * 128 : (c + 1) * 128, :] = per_head(
                    silu_half(half), row8, 2 * c
                ).astype(BF16)
            bc_t = silu_half(mm(conv_ref[side, base + INNER : base + CONVW, :], hot))
            state = state_s[side, strand]
            for step_index in range(nb):
                b = step_index if side == 0 else nb - 1 - step_index
                at = slice(b * SPAN, (b + 1) * SPAN)
                bc_blk = bc_t[:, at]
                b_rows = jnp.transpose(bc_blk)[:, :STATE].astype(BF16)
                c_t = bc_blk[STATE:].astype(BF16)
                b_t = bc_blk[:STATE].astype(BF16)
                scores = mm(b_rows, c_t)
                causal = (row_i <= col_i) if side == 0 else (row_i >= col_i)
                scores = jnp.where(causal, scores, 0.0)
                cs = part(cums, strand, b)
                tot = part(tots, strand, b)
                carried = mm(state.astype(BF16), c_t)
                grow = jnp.exp(cs)
                for h in range(HEADS):
                    col = (strand * nb + b) * 8 + h
                    e = cs[h : h + 1] - cols[:, col : col + 1]
                    w = (scores * jnp.exp(jnp.minimum(e, 0.0))).astype(BF16)
                    hs = slice(h * HEADDIM, (h + 1) * HEADDIM)
                    y = mm(scaled_s[buf, hs, at], w) + carried[hs] * grow[h : h + 1]
                    if side == 0:
                        y_s[strand, hs, at] = y
                    else:
                        y_s[strand, hs, at] += y
                if step_index < nb - 1:
                    decayed = per_head(
                        scaled_s[buf, :, at].astype(F32), jnp.exp(tot - cs), 0
                    ).astype(BF16)
                    state = per_head(state, jnp.exp(tot)[:, :STATE], 0) + mm(decayed, b_t, NT)

    hot0 = (sub8 == ids_s[pl.ds(me + 1, 1), :]).astype(F32)
    hot0 = jnp.concatenate([hot0, hot0], axis=0).astype(BF16)
    for h in range(HEADS):
        hs = slice(h * HEADDIM, (h + 1) * HEADDIM)
        gain = gain_ref[hs, :]
        gain = jnp.concatenate([gain] * nb, axis=1)
        total = None
        for strand in range(2):
            at = strand * INNER + h * HEADDIM
            g = y_s[strand, hs, :] * mm(gate_ref[at : at + HEADDIM, :], hot0)
            mean_sq = jnp.mean(g * g, axis=0, keepdims=True)
            out = (g * lax.rsqrt(mean_sq + EPSILON) * gain).astype(BF16).astype(F32)
            total = out if total is None else total + out
        comb_s[hs, :] = total.astype(BF16)

    comb_t = comb_s[...]
    comb = jnp.transpose(comb_t.astype(F32)).astype(BF16)
    layer = mm(comb, wout_ref[...]).astype(BF16)
    layer_out[...] = layer
    layer = layer.astype(F32)
    sigma = 0.5 + 0.5 * jnp.tanh(0.5 * layer)
    act_high, act_low = split_two(layer * sigma)
    head_t = headt_ref[...]
    logits = mm(head_t, act_high, NT) + mm(head_t, act_low, NT)
    classes = 5
    real = lax.broadcasted_iota(jnp.int32, (8, length), 0) < classes
    expo = jnp.where(real, jnp.exp(logits), 0.0)
    prob = expo / jnp.sum(expo, axis=0, keepdims=True)
    target = (sub8 == tok_ref[0:1, :].astype(F32)).astype(F32)
    masked = values_of(me) > 0.5
    grad_logits = jnp.where(masked & real, (prob - target) / masked_total, 0.0)
    high, low = split_two(grad_logits)
    both = jnp.concatenate([high.astype(F32), low.astype(F32)], axis=0)
    head2 = jnp.concatenate([head_t.astype(F32)] * 2, axis=0).astype(BF16)
    grad_act = mm(jnp.transpose(both).astype(BF16), head2)
    slope = sigma * (1.0 + layer * (1.0 - sigma))
    grad_layer = (grad_act * slope).astype(BF16)
    core = me % 2
    half = INNER // 2
    send_out[...] = mm(
        comb_s[pl.ds(pl.multiple_of((1 - core) * half, half), half), :], grad_layer
    ).astype(BF16)
    keep_out[...] = mm(
        comb_s[pl.ds(pl.multiple_of(core * half, half), half), :], grad_layer
    ).astype(BF16)


def swap(value, axis, k):
    return lax.ppermute(value, axis, [(i, i ^ k) for i in range(lax.axis_size(axis))])


def strides(n):
    out, stride = [], 2
    while stride < n:
        radix = 4 if n // stride >= 4 else 2
        out.append((stride, radix))
        stride *= radix
    return out


def row_of(stack, index):
    return lax.dynamic_index_in_dim(stack, index, 0, False)


def tree_sum(parts):
    parts = [p.astype(F32) for p in parts]
    while len(parts) > 1:
        parts = [a + b for a, b in zip(parts[::2], parts[1::2])]
    return parts[0].astype(BF16)


def sum_all(send, keep, n):
    core = lax.axis_index("seq") % 2
    mine = lax.axis_index("dp")
    rows, cols = keep.shape
    part = tree_sum([keep, swap(send, "seq", 1)]).reshape(4, rows // 4, cols)
    got = [swap(row_of(part, mine ^ k), "dp", k) for k in (1, 2, 3)]
    part = tree_sum([row_of(part, mine)] + got)
    for stride, radix in strides(n):
        got = [swap(part, "seq", k * stride) for k in range(1, radix)]
        part = tree_sum([part] + got)
    got = [part] + [swap(part, "dp", k) for k in (1, 2, 3)]
    part = jnp.stack(
        [
            jnp.where(mine == j, got[0], jnp.where(mine == j ^ 1, got[1], jnp.where(mine == j ^ 2, got[2], got[3])))
            for j in range(4)
        ]
    ).reshape(rows, cols)
    other = swap(part, "seq", 1)
    low = jnp.where(core == 0, part, other)
    high = jnp.where(core == 0, other, part)
    return jnp.concatenate([low, high], axis=0).astype(F32)


def per_device(
    n, tokens, mask_pos, replace_ids, token_embedding_matrix, entry_scale_vector,
    input_projection_weight, increment_coefficients, conv_w, conv_b, dt_bias, decay_rate,
    gain_out, w_out, w_head,
):
    length = tokens.shape[1]
    width = w_out.shape[1]
    nb = length // SPAN
    rows = 2 * nb * 8
    gathered = jnp.concatenate([tokens, swap(tokens, "seq", 1)], axis=0)
    for stride, radix in strides(n):
        gathered = jnp.concatenate(
            [gathered] + [swap(gathered, "seq", k * stride) for k in range(1, radix)], axis=0
        )
    shape = jax.ShapeDtypeStruct
    tables = pl.pallas_call(
        tables_kernel,
        out_shape=(
            shape((2, 2 * CONVW, 16 * KW), BF16),
            shape((2 * INNER, 16), BF16),
            shape((2, 2, HEADS, 8), F32),
            shape((2, 2, HEADS, 8), F32),
            shape((INNER, 128), F32),
            shape((8, width), BF16),
        ),
        compiler_params=pltpu.CompilerParams(vmem_limit_bytes=32 << 20),
        cost_estimate=pl.CostEstimate(flops=20_000_000, bytes_accessed=3_000_000, transcendentals=10_000),
        name="tables",
    )(
        token_embedding_matrix, entry_scale_vector[None], input_projection_weight,
        increment_coefficients, conv_w, conv_b, dt_bias, decay_rate, gain_out[None], w_head,
    )
    masks = mask_pos.shape[1]
    wide = -(-masks // 128) * 128
    slots = n + 1
    layer_out, send, keep = pl.pallas_call(
        functools.partial(layer_kernel, n, length, lax.axis_size("dp") * masks),
        out_shape=(
            shape((length, width), BF16),
            shape((INNER // 2, width), BF16),
            shape((INNER // 2, width), BF16),
        ),
        scratch_shapes=[
            pltpu.VMEM((1, wide), jnp.int32),
            pltpu.VMEM((1, wide), jnp.int32),
            pltpu.VMEM((n + 2, length), F32),
            pltpu.VMEM((n * nb, SPAN), F32),
            pltpu.VMEM((slots, rows, SPAN), F32),
            pltpu.VMEM((slots, rows, SPAN), F32),
            pltpu.VMEM((slots, rows, SPAN), F32),
            pltpu.VMEM((slots, rows, SPAN), F32),
            pltpu.VMEM((4, INNER, length), BF16),
            pltpu.VMEM((2, 2, INNER, STATE), F32),
            pltpu.VMEM((2, INNER, length), F32),
            pltpu.VMEM((INNER, length), BF16),
        ],
        compiler_params=pltpu.CompilerParams(vmem_limit_bytes=48 << 20),
        cost_estimate=pl.CostEstimate(flops=2_000_000_000, bytes_accessed=4_000_000, transcendentals=4_000_000),
        name="layer",
    )(gathered, mask_pos, replace_ids, *tables, w_out)
    return (layer_out[None], sum_all(send, keep, n))


def solution(mesh):
    in_specs = (P("dp", "seq"), P("dp", None), P("dp", None)) + (P(),) * 11
    out_specs = (P("dp", "seq", None), P())
    return jax.shard_map(
        functools.partial(per_device, mesh.shape["seq"]),
        mesh=mesh, in_specs=in_specs, out_specs=out_specs, check_vma=False,
    )
```

time: 339 us -> 54.2 us (0.16); the launches traced: 335 us -> 53.7 us
  waiting for transfers between devices: 136 us -> 15 us
  local copies, waits for them, and re-layouts: 106 us -> 7.9 us
  other arithmetic: 27.2 us -> 2.06 us
  blocking collectives: 23.1 us -> 0 us
  matrix products: 22.2 us -> 0 us
  between operations: 14.5 us -> 0.84 us
  starting transfers between devices: 5.21 us -> 17.4 us
  Pallas kernels: 0 us -> 10.5 us
    psum x1 -> x0, waiting for transfers between devices: 130 us -> none  [per_device(): grad_w_out = lax.psum(local_grad, ('dp', 'seq'))]
    slice x16 -> x0, local copies, waits for them, and re-layouts: 29.1 us -> none  [the longest x4 27.2 us: filtered_lines(): padded[:, first_row:first_row + length].astype(jnp.float32)]
    all_gather x2 -> x0, blocking collectives: 23.1 us -> none  [carried_in(): pieces = jax.tree.map(lambda part: lax.all_gather(part, axis), value)]
    ppermute x2 -> x15, waiting for transfers between devices: 0.01 us -> 15 us  [swap(): lax.ppermute(value, axis, [(i, i ^ k) for i in range(lax.axis_size(axis))])]
    dot_general x19 -> x0, matrix products: 14.4 us -> none  [the longest x4 6.88 us: advance(): jnp.einsum('shij,sjhp->sihp', weights, x_rows, preferred_element_type=jnp...]
    ppermute x2 -> x15, starting transfers between devices: 4.91 us -> 17.4 us  [swap(): lax.ppermute(value, axis, [(i, i ^ k) for i in range(lax.axis_size(axis))])]
    rev x4 -> x0, local copies, waits for them, and re-layouts: 11.4 us -> none  [the longest x1 8.9 us: run_strands(): jnp.flip(add_incoming(down_local, down_logs, down_conv, down_in[1]), 1)]
    mul x21 -> x0, local copies, waits for them, and re-layouts: 11.3 us -> none  [the longest x14 9.12 us: join_states(): second_decay[..., None] * first_state + second_state]
  transfers between devices with their start and end apart: 5 -> 15, of which waited for: 2 -> 11; matrix products, arithmetic and copies ran while one was open for 35% -> 3% of each run, Pallas kernels for 0% -> 2%
where the time goes in v1:
time: 54.2 us; the launch traced here: 53.7 us
  starting transfers between devices  17.4 us (32%)
  waiting for transfers between devices  15 us (28%)
  Pallas kernels  10.5 us (19%)
  local copies, waits for them, and re-layouts  7.9 us (15%)
  other arithmetic  2.06 us (4%)
  between operations  0.84 us (2%)
    ppermute x15, starting transfers between devices, swap(): lax.ppermute(value, axis, [(i, i ^ k) for i in range(lax.axis_size(axis))])  17.4 us
    ppermute x15, waiting for transfers between devices, swap(): lax.ppermute(value, axis, [(i, i ^ k) for i in range(lax.axis_size(axis))])  15 us
    pallas_call x1, Pallas kernels, per_device(): pl.pallas_call(functools.partial(layer_kernel, n, length, lax.axis_size('...  9.35 us
    unnamed x26, local copies, waits for them, and re-layouts  7.85 us
    pallas_call x1, Pallas kernels, per_device(): pl.pallas_call(tables_kernel, out_shape=(shape((2, 2 * CONVW, 16 * KW), B...  1.15 us
    convert_element_type x1, other arithmetic, sum_all(): return jnp.concatenate([low, high], axis=0).astype(F32)  1.1 us
  transfers between devices with their start and end apart: 15, of which 11 were waited for; matrix products, arithmetic and copies ran while one was open for 3% of the time, Pallas kernels for 2%

profile of v1, /device:TPU:0, one launch (start us, length us, event | category | flops | bytes accessed | tf_op | source)
XLA Modules:
  0.0 53.7 jit_solution(625430730304026266)
XLA Ops:
  0.6 0.0 copy-start.11
  0.6 0.0 copy-start.9
  0.7 0.0 copy-start.10
  0.7 0.5 collective-permute-start
  1.2 0.9 %copy.16.inc_ref = bf16[512,8]{1,0:T(8,128)(2,1)S(1)} copy(bf16[512,8]{0,1:T(8,128)(2,1)} %param.20) | data formatting | bytes 16384 | tf_op args[6]
  2.0 0.9 %copy.17.head_ref = bf16[512,5]{1,0:T(8,128)(2,1)S(1)} copy(bf16[512,5]{0,1:T(8,128)(2,1)} %param.27) | data formatting | bytes 10240 | tf_op args[13]
  2.9 0.0 collective-permute-done
  2.9 0.7 %pad_add_fusion = s32[2,256]{1,0:T(2,128)S(1)} fusion(s32[1,256]{1,0:T(1,128)S(1)} %collective-permute-done, s32[1,256]{1,0:T(1,128)} %param.14), kind=kLoop, calls=%fused_computation.16 | loop fusion | flops 512 | bytes 4096 | tf_op jit(solution)/shard_map/concatenate | solution.py:410
  3.6 2.6 %collective-permute-start.1 = (s32[2,256]{1,0:T(2,128)S(1)}, s32[2,256]{1,0:T(2,128)S(1)}, u32[]{:S(2)}, u32[]{:S(2)}) collective-permute-start(s32[2,256]{1,0:T(2,128)S(1)} %pad_add_fusion), channel_id=1, source_target_pairs={{0,2},{1,3},{2,0},{3,1},{4,6},{5,7},{6,4},{7,5},{8,10},{9,11},{10,... | collective-permute-start | bytes 6152 | tf_op jit(solution)/shard_map/ppermute | solution.py:355
  6.2 2.6 %collective-permute-start.2 = (s32[2,256]{1,0:T(2,128)S(1)}, s32[2,256]{1,0:T(2,128)S(1)}, u32[]{:S(2)}, u32[]{:S(2)}) collective-permute-start(s32[2,256]{1,0:T(2,128)S(1)} %pad_add_fusion), channel_id=1, source_target_pairs={{0,4},{1,5},{2,6},{3,7},{4,0},{5,1},{6,2},{7,3},{8,12},{9,13},{10,... | collective-permute-start | bytes 6152 | tf_op jit(solution)/shard_map/ppermute | solution.py:355
  8.8 0.0 collective-permute-start.3
  8.8 0.0 copy-start
  8.8 1.3 %copy-done = bf16[512,1152]{1,0:T(8,128)(2,1)S(1)} copy-done((bf16[512,1152]{1,0:T(8,128)(2,1)S(1)}, bf16[512,1152]{1,0:T(8,128)(2,1)}, u32[]{:S(2)}) %copy-start) | copy-done | bytes 1179672
  10.1 0.0 copy-start.1
  10.1 0.7 %copy-done.1 = f32[2,4,640]{2,1,0:T(4,128)S(1)} copy-done((f32[2,4,640]{2,1,0:T(4,128)S(1)}, f32[2,4,640]{2,1,0:T(4,128)}, u32[]{:S(2)}) %copy-start.1) | copy-done | bytes 20504
  10.8 0.0 copy-start.2
  10.8 0.7 %copy-done.2 = bf16[6,512]{1,0:T(8,128)(2,1)S(1)} copy-done((bf16[6,512]{1,0:T(8,128)(2,1)S(1)}, bf16[6,512]{1,0:T(8,128)(2,1)}, u32[]{:S(2)}) %copy-start.2) | copy-done | bytes 6168
  11.5 0.0 copy-start.3
  11.5 0.7 %copy-done.3 = f32[2,640]{1,0:T(2,128)S(1)} copy-done((f32[2,640]{1,0:T(2,128)S(1)}, f32[2,640]{1,0:T(2,128)}, u32[]{:S(2)}) %copy-start.3) | copy-done | bytes 5144
  12.2 0.0 copy-start.4
  12.2 0.7 %copy-done.4 = f32[512]{0:T(512)S(1)} copy-done((f32[512]{0:T(512)S(1)}, f32[512]{0:T(512)}, u32[]{:S(2)}) %copy-start.4) | copy-done | bytes 2072
  12.9 0.0 copy-start.5
  12.9 0.7 %copy-done.5 = f32[512]{0:T(512)S(1)} copy-done((f32[512]{0:T(512)S(1)}, f32[512]{0:T(512)}, u32[]{:S(2)}) %copy-start.5) | copy-done | bytes 2072
  13.6 0.0 copy-start.6
  13.6 0.7 %copy-done.6 = f32[2,8]{1,0:T(2,128)S(1)} copy-done((f32[2,8]{1,0:T(2,128)S(1)}, f32[2,8]{1,0:T(2,128)}, u32[]{:S(2)}) %copy-start.6) | copy-done | bytes 88
  14.2 0.0 copy-start.7
  14.2 0.7 %copy-done.7 = f32[2,8]{1,0:T(2,128)S(1)} copy-done((f32[2,8]{1,0:T(2,128)S(1)}, f32[2,8]{1,0:T(2,128)}, u32[]{:S(2)}) %copy-start.7) | copy-done | bytes 88
  14.9 0.0 copy-start.8
  14.9 1.2 %tables.1 = (bf16[2,1280,64]{2,1,0:T(8,128)(2,1)S(1)}, bf16[1024,16]{1,0:T(8,128)(2,1)S(1)}, f32[2,2,8,8]{3,2,1,0:T(8,128)S(1)}, f32[2,2,8,8]{3,2,1,0:T(8,128)S(...) custom-call(bf16[6,512]{1,0:T(8,128)(2,1)S(1)} %copy-done.2, f32[1,512]{1,0:T(1,128)S(1)} %bitcast.24, ...), custom_call_target="tpu_custom_call" | custom-call | flops 20000000 | bytes 3000000 | tf_op jit(solution)/shard_map/tables/pallas_call | solution.py:416
  16.1 0.0 collective-permute-done.1
  16.1 0.0 collective-permute-done.2
  16.1 0.0 collective-permute-done.3
  16.1 0.0 copy-done.11
  16.1 0.0 copy-done.9
  16.1 0.0 copy-done.10
  16.2 0.0 copy-done.8
  16.2 9.3 %layer.1 = (bf16[256,512]{1,0:T(8,128)(2,1)}, bf16[256,512]{1,0:T(8,128)(2,1)S(1)}, bf16[256,512]{1,0:T(8,128)(2,1)S(1)}) custom-call(s32[8,256]{1,0:T(8,128)S(1)} %concatenate.11.tok_ref, s32[1,307]{1,0:T(1,128)S(1)} %copy-done.9, s32[1,307]{1,0:T(1,128)S(1)} %copy-done.10, bf16[2,1280,64]{2,1,0:T(8,128)(2,1)S(1)} %get-tuple-element.11.conv_ref, ...), custom_call_target="tpu_custom_call" | custom-call | flops 2000000000 | bytes 4000000 | tf_op jit(solution)/shard_map/layer/pallas_call | solution.py:436
  25.5 0.1 collective-permute-start.4
  25.6 1.5 %collective-permute-done.4 = bf16[256,512]{1,0:T(8,128)(2,1)S(1)} collective-permute-done((bf16[256,512]{1,0:T(8,128)(2,1)S(1)}, bf16[256,512]{1,0:T(8,128)(2,1)S(1)}, u32[]{:S(2)}, u32[]{:S(2)}) %collective-permute-start.4) | collective-permute-done | bytes 262176 | tf_op jit(solution)/shard_map/ppermute | solution.py:355
  27.1 0.1 add_convert_fusion
  27.2 1.8 %collective-permute-start.5 = (bf16[64,512]{1,0:T(8,128)(2,1)S(1)}, bf16[64,512]{1,0:T(8,128)(2,1)S(1)}, u32[]{:S(2)}, u32[]{:S(2)}) collective-permute-start(bf16[64,512]{1,0:T(8,128)(2,1)S(1)} %get-tuple-element.26), channel_id=1, source_target_pairs={{0,8},{8,0},{16,24},{24,16},{1,9},{9,1},{17,25},{25,17},{2,10},{10... | collective-permute-start | bytes 196616 | tf_op jit(solution)/shard_map/ppermute | solution.py:355
  29.0 1.5 %collective-permute-start.6 = (bf16[64,512]{1,0:T(8,128)(2,1)S(1)}, bf16[64,512]{1,0:T(8,128)(2,1)S(1)}, u32[]{:S(2)}, u32[]{:S(2)}) collective-permute-start(bf16[64,512]{1,0:T(8,128)(2,1)S(1)} %get-tuple-element.28), channel_id=1, source_target_pairs={{0,16},{8,24},{16,0},{24,8},{1,17},{9,25},{17,1},{25,9},{2,18},{10... | collective-permute-start | bytes 196616 | tf_op jit(solution)/shard_map/ppermute | solution.py:355
  30.5 0.3 collective-permute-start.7
  30.8 0.8 %collective-permute-done.5 = bf16[64,512]{1,0:T(8,128)(2,1)S(1)} collective-permute-done((bf16[64,512]{1,0:T(8,128)(2,1)S(1)}, bf16[64,512]{1,0:T(8,128)(2,1)S(1)}, u32[]{:S(2)}, u32[]{:S(2)}) %collective-permute-start.5) | collective-permute-done | bytes 65568 | tf_op jit(solution)/shard_map/ppermute | solution.py:355
  31.6 1.7 %collective-permute-done.6 = bf16[64,512]{1,0:T(8,128)(2,1)S(1)} collective-permute-done((bf16[64,512]{1,0:T(8,128)(2,1)S(1)}, bf16[64,512]{1,0:T(8,128)(2,1)S(1)}, u32[]{:S(2)}, u32[]{:S(2)}) %collective-permute-start.6) | collective-permute-done | bytes 65568 | tf_op jit(solution)/shard_map/ppermute | solution.py:355
  33.3 2.4 %collective-permute-done.7 = bf16[64,512]{1,0:T(8,128)(2,1)S(1)} collective-permute-done((bf16[64,512]{1,0:T(8,128)(2,1)S(1)}, bf16[64,512]{1,0:T(8,128)(2,1)S(1)}, u32[]{:S(2)}, u32[]{:S(2)}) %collective-permute-start.7) | collective-permute-done | bytes 65568 | tf_op jit(solution)/shard_map/ppermute | solution.py:355
  35.7 3.7 %collective-permute-start.10 = (bf16[64,512]{1,0:T(8,128)(2,1)S(1)}, bf16[64,512]{1,0:T(8,128)(2,1)S(1)}, u32[]{:S(2)}, u32[]{:S(2)}) collective-permute-start(bf16[64,512]{1,0:T(8,128)(2,1)S(1)} %fusion.1), channel_id=1, source_target_pairs={{0,6},{1,7},{2,4},{3,5},{4,2},{5,3},{6,0},{7,1},{8,14},{9,15},{10,... | collective-permute-start | bytes 196616 | tf_op jit(solution)/shard_map/ppermute | solution.py:355
  39.4 0.0 collective-permute-start.8
  39.4 0.8 %collective-permute-start.9 = (bf16[64,512]{1,0:T(8,128)(2,1)S(1)}, bf16[64,512]{1,0:T(8,128)(2,1)S(1)}, u32[]{:S(2)}, u32[]{:S(2)}) collective-permute-start(bf16[64,512]{1,0:T(8,128)(2,1)S(1)} %fusion.1), channel_id=1, source_target_pairs={{0,4},{1,5},{2,6},{3,7},{4,0},{5,1},{6,2},{7,3},{8,12},{9,13},{10,... | collective-permute-start | bytes 196616 | tf_op jit(solution)/shard_map/ppermute | solution.py:355
  40.2 1.8 %collective-permute-done.10 = bf16[64,512]{1,0:T(8,128)(2,1)S(1)} collective-permute-done((bf16[64,512]{1,0:T(8,128)(2,1)S(1)}, bf16[64,512]{1,0:T(8,128)(2,1)S(1)}, u32[]{:S(2)}, u32[]{:S(2)}) %collective-permute-start.10) | collective-permute-done | bytes 65568 | tf_op jit(solution)/shard_map/ppermute | solution.py:355
  41.9 1.7 %collective-permute-done.8 = bf16[64,512]{1,0:T(8,128)(2,1)S(1)} collective-permute-done((bf16[64,512]{1,0:T(8,128)(2,1)S(1)}, bf16[64,512]{1,0:T(8,128)(2,1)S(1)}, u32[]{:S(2)}, u32[]{:S(2)}) %collective-permute-start.8) | collective-permute-done | bytes 65568 | tf_op jit(solution)/shard_map/ppermute | solution.py:355
  43.7 0.9 %collective-permute-done.9 = bf16[64,512]{1,0:T(8,128)(2,1)S(1)} collective-permute-done((bf16[64,512]{1,0:T(8,128)(2,1)S(1)}, bf16[64,512]{1,0:T(8,128)(2,1)S(1)}, u32[]{:S(2)}, u32[]{:S(2)}) %collective-permute-start.9) | collective-permute-done | bytes 65568 | tf_op jit(solution)/shard_map/ppermute | solution.py:355
  44.6 0.6 %collective-permute-start.11 = (bf16[64,512]{1,0:T(8,128)(2,1)S(1)}, bf16[64,512]{1,0:T(8,128)(2,1)S(1)}, u32[]{:S(2)}, u32[]{:S(2)}) collective-permute-start(bf16[64,512]{1,0:T(8,128)(2,1)S(1)} %add_convert_fusion.1), channel_id=1, source_target_pairs={{0,8},{8,0},{16,24},{24,16},{1,9},{9,1},{17,25},{25,17},{2,10},{10... | collective-permute-start | bytes 196616 | tf_op jit(solution)/shard_map/ppermute | solution.py:355
  45.2 0.5 collective-permute-start.12
  45.7 2.4 %collective-permute-start.13 = (bf16[64,512]{1,0:T(8,128)(2,1)S(1)}, bf16[64,512]{1,0:T(8,128)(2,1)S(1)}, u32[]{:S(2)}, u32[]{:S(2)}) collective-permute-start(bf16[64,512]{1,0:T(8,128)(2,1)S(1)} %add_convert_fusion.1), channel_id=1, source_target_pairs={{0,24},{8,16},{16,8},{24,0},{1,25},{9,17},{17,9},{25,1},{2,26},{10... | collective-permute-start | bytes 196616 | tf_op jit(solution)/shard_map/ppermute | solution.py:355
  48.1 0.8 %collective-permute-done.11 = bf16[64,512]{1,0:T(8,128)(2,1)S(1)} collective-permute-done((bf16[64,512]{1,0:T(8,128)(2,1)S(1)}, bf16[64,512]{1,0:T(8,128)(2,1)S(1)}, u32[]{:S(2)}, u32[]{:S(2)}) %collective-permute-start.11) | collective-permute-done | bytes 65568 | tf_op jit(solution)/shard_map/ppermute | solution.py:355
  48.9 0.5 collective-permute-done.12
  49.5 1.4 %collective-permute-done.13 = bf16[64,512]{1,0:T(8,128)(2,1)S(1)} collective-permute-done((bf16[64,512]{1,0:T(8,128)(2,1)S(1)}, bf16[64,512]{1,0:T(8,128)(2,1)S(1)}, u32[]{:S(2)}, u32[]{:S(2)}) %collective-permute-start.13) | collective-permute-done | bytes 65568 | tf_op jit(solution)/shard_map/ppermute | solution.py:355
  51.0 0.1 collective-permute-start.14
  51.0 1.5 %collective-permute-done.14 = bf16[256,512]{1,0:T(8,128)(2,1)S(1)} collective-permute-done((bf16[256,512]{1,0:T(8,128)(2,1)S(1)}, bf16[256,512]{1,0:T(8,128)(2,1)S(1)}, u32[]{:S(2)}, u32[]{:S(2)}) %collective-permute-start.14) | collective-permute-done | bytes 262176 | tf_op jit(solution)/shard_map/ppermute | solution.py:355
  52.6 0.1 broadcast_select_fusion.1
  52.6 1.1 %maximum_convert_fusion = f32[512,512]{1,0:T(8,128)} fusion(bf16[256,512]{1,0:T(8,128)(2,1)S(1)} %get-tuple-element.21, bf16[256,512]{1,0:T(8,128)(2,1)S(1)} %get-tuple-element.20), kind=kLoop, calls=%fused_computation | loop fusion | flops 1048576 | bytes 1572864 | tf_op jit(solution)/shard_map/convert_element_type | solution.py:398
  (6 shorter events, 0.2 us)
Async XLA Ops:
  0.6 15.5 %copy-start.11 = (s32[1,256]{1,0:T(1,128)S(1)}, s32[1,256]{1,0:T(1,128)}, u32[]{:S(2)}) copy-start(s32[1,256]{1,0:T(1,128)} %param.14) | copy-start | bytes 3076
  0.6 15.5 %copy-start.9 = (s32[1,307]{1,0:T(1,128)S(1)}, s32[1,307]{1,0:T(1,128)}, u32[]{:S(2)}) copy-start(s32[1,307]{1,0:T(1,128)} %pos_ref.1) | copy-start | bytes 3688
  0.7 15.5 %copy-start.10 = (s32[1,307]{1,0:T(1,128)S(1)}, s32[1,307]{1,0:T(1,128)}, u32[]{:S(2)}) copy-start(s32[1,307]{1,0:T(1,128)} %rep_ref.1) | copy-start | bytes 3688
  0.7 2.3 %collective-permute-start = (s32[1,256]{1,0:T(1,128)}, s32[1,256]{1,0:T(1,128)S(1)}, u32[]{:S(2)}, u32[]{:S(2)}) collective-permute-start(s32[1,256]{1,0:T(1,128)} %param.14), channel_id=1, source_target_pairs={{0,1},{1,0},{2,3},{3,2},{4,5},{5,4},{6,7},{7,6},{8,9},{9,8},{10,11... | collective-permute-start | bytes 3080 | tf_op jit(solution)/shard_map/ppermute | solution.py:355
  3.6 12.4 %collective-permute-start.1 = (s32[2,256]{1,0:T(2,128)S(1)}, s32[2,256]{1,0:T(2,128)S(1)}, u32[]{:S(2)}, u32[]{:S(2)}) collective-permute-start(s32[2,256]{1,0:T(2,128)S(1)} %pad_add_fusion), channel_id=1, source_target_pairs={{0,2},{1,3},{2,0},{3,1},{4,6},{5,7},{6,4},{7,5},{8,10},{9,11},{10,... | collective-permute-start | bytes 6152 | tf_op jit(solution)/shard_map/ppermute | solution.py:355
  6.2 9.9 %collective-permute-start.2 = (s32[2,256]{1,0:T(2,128)S(1)}, s32[2,256]{1,0:T(2,128)S(1)}, u32[]{:S(2)}, u32[]{:S(2)}) collective-permute-start(s32[2,256]{1,0:T(2,128)S(1)} %pad_add_fusion), channel_id=1, source_target_pairs={{0,4},{1,5},{2,6},{3,7},{4,0},{5,1},{6,2},{7,3},{8,12},{9,13},{10,... | collective-permute-start | bytes 6152 | tf_op jit(solution)/shard_map/ppermute | solution.py:355
  8.8 7.3 %collective-permute-start.3 = (s32[2,256]{1,0:T(2,128)S(1)}, s32[2,256]{1,0:T(2,128)S(1)}, u32[]{:S(2)}, u32[]{:S(2)}) collective-permute-start(s32[2,256]{1,0:T(2,128)S(1)} %pad_add_fusion), channel_id=1, source_target_pairs={{0,6},{1,7},{2,4},{3,5},{4,2},{5,3},{6,0},{7,1},{8,14},{9,15},{10,... | collective-permute-start | bytes 6152 | tf_op jit(solution)/shard_map/ppermute | solution.py:355
  8.8 1.3 %copy-start = (bf16[512,1152]{1,0:T(8,128)(2,1)S(1)}, bf16[512,1152]{1,0:T(8,128)(2,1)}, u32[]{:S(2)}) copy-start(bf16[512,1152]{1,0:T(8,128)(2,1)} %win_ref.1) | copy-start | bytes 3538948
  10.1 0.7 %copy-start.1 = (f32[2,4,640]{2,1,0:T(4,128)S(1)}, f32[2,4,640]{2,1,0:T(4,128)}, u32[]{:S(2)}) copy-start(f32[2,4,640]{2,1,0:T(4,128)} %cw_ref.1) | copy-start | bytes 61444
  10.8 0.7 %copy-start.2 = (bf16[6,512]{1,0:T(8,128)(2,1)S(1)}, bf16[6,512]{1,0:T(8,128)(2,1)}, u32[]{:S(2)}) copy-start(bf16[6,512]{1,0:T(8,128)(2,1)} %emb_ref.1) | copy-start | bytes 18436
  11.5 0.7 %copy-start.3 = (f32[2,640]{1,0:T(2,128)S(1)}, f32[2,640]{1,0:T(2,128)}, u32[]{:S(2)}) copy-start(f32[2,640]{1,0:T(2,128)} %cb_ref.1) | copy-start | bytes 15364
  12.2 0.7 %copy-start.4 = (f32[512]{0:T(512)S(1)}, f32[512]{0:T(512)}, u32[]{:S(2)}) copy-start(f32[512]{0:T(512)} %param.18) | copy-start | bytes 6148
  12.9 0.7 %copy-start.5 = (f32[512]{0:T(512)S(1)}, f32[512]{0:T(512)}, u32[]{:S(2)}) copy-start(f32[512]{0:T(512)} %param.25) | copy-start | bytes 6148
  13.6 0.7 %copy-start.6 = (f32[2,8]{1,0:T(2,128)S(1)}, f32[2,8]{1,0:T(2,128)}, u32[]{:S(2)}) copy-start(f32[2,8]{1,0:T(2,128)} %dtb_ref.1) | copy-start | bytes 196
  14.2 0.7 %copy-start.7 = (f32[2,8]{1,0:T(2,128)S(1)}, f32[2,8]{1,0:T(2,128)}, u32[]{:S(2)}) copy-start(f32[2,8]{1,0:T(2,128)} %rate_ref.1) | copy-start | bytes 196
  14.9 1.2 %copy-start.8 = (bf16[512,512]{1,0:T(8,128)(2,1)S(1)}, bf16[512,512]{1,0:T(8,128)(2,1)}, u32[]{:S(2)}) copy-start(bf16[512,512]{1,0:T(8,128)(2,1)} %wout_ref.1) | copy-start | bytes 1572868
  25.5 1.6 %collective-permute-start.4 = (bf16[256,512]{1,0:T(8,128)(2,1)S(1)}, bf16[256,512]{1,0:T(8,128)(2,1)S(1)}, u32[]{:S(2)}, u32[]{:S(2)}) collective-permute-start(bf16[256,512]{1,0:T(8,128)(2,1)S(1)} %get-tuple-element.19), channel_id=1, source_target_pairs={{0,1},{1,0},{2,3},{3,2},{4,5},{5,4},{6,7},{7,6},{8,9},{9,8},{10,11... | collective-permute-start | bytes 786440 | tf_op jit(solution)/shard_map/ppermute | solution.py:355
  27.2 4.3 %collective-permute-start.5 = (bf16[64,512]{1,0:T(8,128)(2,1)S(1)}, bf16[64,512]{1,0:T(8,128)(2,1)S(1)}, u32[]{:S(2)}, u32[]{:S(2)}) collective-permute-start(bf16[64,512]{1,0:T(8,128)(2,1)S(1)} %get-tuple-element.26), channel_id=1, source_target_pairs={{0,8},{8,0},{16,24},{24,16},{1,9},{9,1},{17,25},{25,17},{2,10},{10... | collective-permute-start | bytes 196616 | tf_op jit(solution)/shard_map/ppermute | solution.py:355
  29.0 4.3 %collective-permute-start.6 = (bf16[64,512]{1,0:T(8,128)(2,1)S(1)}, bf16[64,512]{1,0:T(8,128)(2,1)S(1)}, u32[]{:S(2)}, u32[]{:S(2)}) collective-permute-start(bf16[64,512]{1,0:T(8,128)(2,1)S(1)} %get-tuple-element.28), channel_id=1, source_target_pairs={{0,16},{8,24},{16,0},{24,8},{1,17},{9,25},{17,1},{25,9},{2,18},{10... | collective-permute-start | bytes 196616 | tf_op jit(solution)/shard_map/ppermute | solution.py:355
  30.5 5.2 %collective-permute-start.7 = (bf16[64,512]{1,0:T(8,128)(2,1)S(1)}, bf16[64,512]{1,0:T(8,128)(2,1)S(1)}, u32[]{:S(2)}, u32[]{:S(2)}) collective-permute-start(bf16[64,512]{1,0:T(8,128)(2,1)S(1)} %get-tuple-element.27), channel_id=1, source_target_pairs={{0,24},{8,16},{16,8},{24,0},{1,25},{9,17},{17,9},{25,1},{2,26},{10... | collective-permute-start | bytes 196616 | tf_op jit(solution)/shard_map/ppermute | solution.py:355
  35.7 6.2 %collective-permute-start.10 = (bf16[64,512]{1,0:T(8,128)(2,1)S(1)}, bf16[64,512]{1,0:T(8,128)(2,1)S(1)}, u32[]{:S(2)}, u32[]{:S(2)}) collective-permute-start(bf16[64,512]{1,0:T(8,128)(2,1)S(1)} %fusion.1), channel_id=1, source_target_pairs={{0,6},{1,7},{2,4},{3,5},{4,2},{5,3},{6,0},{7,1},{8,14},{9,15},{10,... | collective-permute-start | bytes 196616 | tf_op jit(solution)/shard_map/ppermute | solution.py:355
  39.4 4.3 %collective-permute-start.8 = (bf16[64,512]{1,0:T(8,128)(2,1)S(1)}, bf16[64,512]{1,0:T(8,128)(2,1)S(1)}, u32[]{:S(2)}, u32[]{:S(2)}) collective-permute-start(bf16[64,512]{1,0:T(8,128)(2,1)S(1)} %fusion.1), channel_id=1, source_target_pairs={{0,2},{1,3},{2,0},{3,1},{4,6},{5,7},{6,4},{7,5},{8,10},{9,11},{10,... | collective-permute-start | bytes 196616 | tf_op jit(solution)/shard_map/ppermute | solution.py:355
  39.4 5.2 %collective-permute-start.9 = (bf16[64,512]{1,0:T(8,128)(2,1)S(1)}, bf16[64,512]{1,0:T(8,128)(2,1)S(1)}, u32[]{:S(2)}, u32[]{:S(2)}) collective-permute-start(bf16[64,512]{1,0:T(8,128)(2,1)S(1)} %fusion.1), channel_id=1, source_target_pairs={{0,4},{1,5},{2,6},{3,7},{4,0},{5,1},{6,2},{7,3},{8,12},{9,13},{10,... | collective-permute-start | bytes 196616 | tf_op jit(solution)/shard_map/ppermute | solution.py:355
  44.6 4.3 %collective-permute-start.11 = (bf16[64,512]{1,0:T(8,128)(2,1)S(1)}, bf16[64,512]{1,0:T(8,128)(2,1)S(1)}, u32[]{:S(2)}, u32[]{:S(2)}) collective-permute-start(bf16[64,512]{1,0:T(8,128)(2,1)S(1)} %add_convert_fusion.1), channel_id=1, source_target_pairs={{0,8},{8,0},{16,24},{24,16},{1,9},{9,1},{17,25},{25,17},{2,10},{10... | collective-permute-start | bytes 196616 | tf_op jit(solution)/shard_map/ppermute | solution.py:355
  45.2 4.3 %collective-permute-start.12 = (bf16[64,512]{1,0:T(8,128)(2,1)S(1)}, bf16[64,512]{1,0:T(8,128)(2,1)S(1)}, u32[]{:S(2)}, u32[]{:S(2)}) collective-permute-start(bf16[64,512]{1,0:T(8,128)(2,1)S(1)} %add_convert_fusion.1), channel_id=1, source_target_pairs={{0,16},{8,24},{16,0},{24,8},{1,17},{9,25},{17,1},{25,9},{2,18},{10... | collective-permute-start | bytes 196616 | tf_op jit(solution)/shard_map/ppermute | solution.py:355
  45.7 5.2 %collective-permute-start.13 = (bf16[64,512]{1,0:T(8,128)(2,1)S(1)}, bf16[64,512]{1,0:T(8,128)(2,1)S(1)}, u32[]{:S(2)}, u32[]{:S(2)}) collective-permute-start(bf16[64,512]{1,0:T(8,128)(2,1)S(1)} %add_convert_fusion.1), channel_id=1, source_target_pairs={{0,24},{8,16},{16,8},{24,0},{1,25},{9,17},{17,9},{25,1},{2,26},{10... | collective-permute-start | bytes 196616 | tf_op jit(solution)/shard_map/ppermute | solution.py:355
  51.0 1.6 %collective-permute-start.14 = (bf16[256,512]{1,0:T(8,128)(2,1)S(1)}, bf16[256,512]{1,0:T(8,128)(2,1)S(1)}, u32[]{:S(2)}, u32[]{:S(2)}) collective-permute-start(bf16[256,512]{1,0:T(8,128)(2,1)S(1)} %bitcast.28), channel_id=1, source_target_pairs={{0,1},{1,0},{2,3},{3,2},{4,5},{5,4},{6,7},{7,6},{8,9},{9,8},{10,11... | collective-permute-start | bytes 786440 | tf_op jit(solution)/shard_map/ppermute | solution.py:355

commit v2 on v1

--- a/solution.py
+++ b/solution.py
@@ -43,10 +43,19 @@
     return half + half * jnp.tanh(half)
 
 
-def tables_kernel(
-    emb_ref, scale_ref, win_ref, inc_ref, cw_ref, cb_ref, dtb_ref, rate_ref, gain_ref, head_ref,
-    conv_out, gate_out, step_out, decay_out, gain_out, head_out,
-):
+def tables_kernel(*refs):
+    count = 10
+    sources, outs, buffers, sem = refs[:count], refs[count:-count - 1], refs[-count - 1 : -1], refs[-1]
+    copies = [
+        pltpu.make_async_copy(source, buffer, sem.at[i])
+        for i, (source, buffer) in enumerate(zip(sources, buffers))
+    ]
+    for copy in copies:
+        copy.start()
+    for copy in copies:
+        copy.wait()
+    emb_ref, scale_ref, win_ref, inc_ref, cw_ref, cb_ref, dtb_ref, rate_ref, gain_ref, head_ref = buffers
+    conv_out, gate_out, step_out, decay_out, gain_out, head_out = outs
     emb = emb_ref[...].astype(F32)
     none = jnp.zeros((2, emb.shape[1]), F32)
     rows = jnp.concatenate(
@@ -55,8 +64,7 @@
     mean_sq = jnp.mean(rows * rows, axis=-1, keepdims=True)
     normed = (rows * lax.rsqrt(mean_sq + EPSILON) * scale_ref[...]).astype(BF16)
     projected = mm(normed, win_ref[...]).astype(BF16).astype(F32)
-    raw = mm(normed, inc_ref[...])
-    raw_t = mm(eye(HEADS, HEADS), raw, NT, HIGH)
+    raw_t = mm(inc_ref[...], normed, NT)
     dtb_t = mm(eye(HEADS, HEADS), dtb_ref[...], NT, HIGH)
     rate_t = mm(eye(HEADS, HEADS), rate_ref[...], NT, HIGH)
     gate = projected[:, :INNER] * 0.5
@@ -82,7 +90,10 @@
             step_out[side, strand] = step
             decay_out[side, strand] = -step * rate_t[:, param : param + 1]
     gain_out[...] = jnp.transpose(jnp.broadcast_to(gain_ref[...], (128, INNER)))
-    head_out[...] = mm(eye(8, head_ref.shape[1], BF16), head_ref[...], NT).astype(BF16)
+    classes, width = head_ref.shape
+    head_out[...] = jnp.concatenate(
+        [head_ref[...].astype(F32), jnp.zeros((8 - classes, width), F32)], axis=0
+    ).astype(BF16)
 
 
 def pick(table, ids):
@@ -134,7 +145,7 @@
     def place(k):
         unit = me ^ k
         put_here = values_of(unit)
-        own = tok_ref[pl.ds(k, 1), :].astype(F32)
+        own = tok_ref[pl.ds(k, 1), :]
         ids_s[pl.ds(unit + 1, 1), :] = jnp.where(put_here > 0.5, put_here - 1.0, own)
 
     loop(n, place)
@@ -332,7 +343,7 @@
     real = lax.broadcasted_iota(jnp.int32, (8, length), 0) < classes
     expo = jnp.where(real, jnp.exp(logits), 0.0)
     prob = expo / jnp.sum(expo, axis=0, keepdims=True)
-    target = (sub8 == tok_ref[0:1, :].astype(F32)).astype(F32)
+    target = (sub8 == tok_ref[0:1, :]).astype(F32)
     masked = values_of(me) > 0.5
     grad_logits = jnp.where(masked & real, (prob - target) / masked_total, 0.0)
     high, low = split_two(grad_logits)
@@ -407,38 +418,45 @@
     width = w_out.shape[1]
     nb = length // SPAN
     rows = 2 * nb * 8
-    gathered = jnp.concatenate([tokens, swap(tokens, "seq", 1)], axis=0)
+    gathered = jnp.concatenate(
+        [tokens.astype(F32), swap(tokens, "seq", 1).astype(F32)], axis=0
+    )
     for stride, radix in strides(n):
         gathered = jnp.concatenate(
             [gathered] + [swap(gathered, "seq", k * stride) for k in range(1, radix)], axis=0
         )
     shape = jax.ShapeDtypeStruct
+    weights = (
+        token_embedding_matrix, entry_scale_vector[None], input_projection_weight,
+        increment_coefficients.T, conv_w, conv_b, dt_bias, decay_rate, gain_out[None], w_head.T,
+    )
     tables = pl.pallas_call(
         tables_kernel,
+        in_specs=[pl.BlockSpec(memory_space=pltpu.HBM)] * len(weights),
+        scratch_shapes=[pltpu.VMEM(w.shape, w.dtype) for w in weights]
+        + [pltpu.SemaphoreType.DMA((len(weights),))],
         out_shape=(
-            shape((2, 2 * CONVW, 16 * KW), BF16),
-            shape((2 * INNER, 16), BF16),
-            shape((2, 2, HEADS, 8), F32),
-            shape((2, 2, HEADS, 8), F32),
-            shape((INNER, 128), F32),
-            shape((8, width), BF16),
+            pltpu.VMEM((2, 2 * CONVW, 16 * KW), BF16),
+            pltpu.VMEM((2 * INNER, 16), BF16),
+            pltpu.VMEM((2, 2, HEADS, 8), F32),
+            pltpu.VMEM((2, 2, HEADS, 8), F32),
+            pltpu.VMEM((INNER, 128), F32),
+            pltpu.VMEM((8, width), BF16),
         ),
         compiler_params=pltpu.CompilerParams(vmem_limit_bytes=32 << 20),
         cost_estimate=pl.CostEstimate(flops=20_000_000, bytes_accessed=3_000_000, transcendentals=10_000),
         name="tables",
-    )(
-        token_embedding_matrix, entry_scale_vector[None], input_projection_weight,
-        increment_coefficients, conv_w, conv_b, dt_bias, decay_rate, gain_out[None], w_head,
-    )
+    )(*[pltpu.with_memory_space_constraint(w, pltpu.HBM) for w in weights])
     masks = mask_pos.shape[1]
     wide = -(-masks // 128) * 128
     slots = n + 1
+    operands = (gathered, mask_pos, replace_ids, *tables, w_out)
     layer_out, send, keep = pl.pallas_call(
         functools.partial(layer_kernel, n, length, lax.axis_size("dp") * masks),
         out_shape=(
             shape((length, width), BF16),
-            shape((INNER // 2, width), BF16),
-            shape((INNER // 2, width), BF16),
+            pltpu.VMEM((INNER // 2, width), BF16),
+            pltpu.VMEM((INNER // 2, width), BF16),
         ),
         scratch_shapes=[
             pltpu.VMEM((1, wide), jnp.int32),
@@ -454,10 +472,10 @@
             pltpu.VMEM((2, INNER, length), F32),
             pltpu.VMEM((INNER, length), BF16),
         ],
-        compiler_params=pltpu.CompilerParams(vmem_limit_bytes=48 << 20),
+        compiler_params=pltpu.CompilerParams(vmem_limit_bytes=32 << 20),
         cost_estimate=pl.CostEstimate(flops=2_000_000_000, bytes_accessed=4_000_000, transcendentals=4_000_000),
         name="layer",
-    )(gathered, mask_pos, replace_ids, *tables, w_out)
+    )(*operands)
     return (layer_out[None], sum_all(send, keep, n))
 
 

time: 54.2 us -> 48.7 us (0.90)
  local copies, waits for them, and re-layouts: 7.9 us -> 0.06 us
  Pallas kernels: 10.5 us -> 11.9 us
  waiting for transfers between devices: 15 us -> 15.9 us
    unnamed x26 -> x6, local copies, waits for them, and re-layouts: 7.85 us -> 0.01 us
    pallas_call x1, Pallas kernels: 1.15 us -> 2.55 us  [per_device(): pl.pallas_call(tables_kernel, in_specs=[pl.BlockSpec(memory_space=pltpu.H...]
    ppermute x15, waiting for transfers between devices: 15 us -> 15.9 us  [swap(): lax.ppermute(value, axis, [(i, i ^ k) for i in range(lax.axis_size(axis))])]
    convert_element_type x0 -> x2, other arithmetic: none -> 0.68 us  [the longest x1 0.68 us: per_device(): tokens.astype(F32)]
    concatenate x1, other arithmetic: 0.69 us -> 0.01 us  [per_device(): jnp.concatenate([tokens.astype(F32), swap(tokens, 'seq', 1).astype(F32)],...]
  transfers between devices with their start and end apart: 15 -> 15, of which waited for: 11 -> 12; matrix products, arithmetic and copies ran while one was open for 3% -> 1% of each run, Pallas kernels for 2% -> 5%
where the time goes in v2:
time: 48.7 us; the launch traced here: 48.5 us
  starting transfers between devices  17.8 us (37%)
  waiting for transfers between devices  15.9 us (33%)
  Pallas kernels  11.9 us (24%)
  other arithmetic  2.06 us (4%)
  between operations  0.8 us (2%)
    ppermute x15, starting transfers between devices, swap(): lax.ppermute(value, axis, [(i, i ^ k) for i in range(lax.axis_size(axis))])  17.8 us
    ppermute x15, waiting for transfers between devices, swap(): lax.ppermute(value, axis, [(i, i ^ k) for i in range(lax.axis_size(axis))])  15.9 us
    pallas_call x1, Pallas kernels, per_device(): pl.pallas_call(functools.partial(layer_kernel, n, length, lax.axis_size('...  9.34 us
    pallas_call x1, Pallas kernels, per_device(): pl.pallas_call(tables_kernel, in_specs=[pl.BlockSpec(memory_space=pltpu.H...  2.55 us
    convert_element_type x1, other arithmetic, sum_all(): return jnp.concatenate([low, high], axis=0).astype(F32)  1.1 us
  transfers between devices with their start and end apart: 15, of which 12 were waited for; matrix products, arithmetic and copies ran while one was open for 1% of the time, Pallas kernels for 5%

profile of v2, /device:TPU:0, one launch (start us, length us, event | category | flops | bytes accessed | tf_op | source)
XLA Modules:
  0.0 48.5 jit_solution(14121073815897445435)
XLA Ops:
  0.6 0.0 copy-start.1
  0.6 0.0 copy-start.2
  0.7 0.0 copy-start
  0.7 0.5 %collective-permute-start = (s32[1,256]{1,0:T(1,128)}, s32[1,256]{1,0:T(1,128)S(1)}, u32[]{:S(2)}, u32[]{:S(2)}) collective-permute-start(s32[1,256]{1,0:T(1,128)} %param.14), channel_id=1, source_target_pairs={{0,1},{1,0},{2,3},{3,2},{4,5},{5,4},{6,7},{7,6},{8,9},{9,8},{10,11... | collective-permute-start | bytes 3080 | tf_op jit(solution)/shard_map/ppermute | solution.py:366
  1.2 0.7 %convert_element_type.51 = f32[1,256]{1,0:T(1,128)S(1)} convert(s32[1,256]{1,0:T(1,128)} %param.14) | non-fusion elementwise | flops 256 | bytes 2048 | tf_op jit(solution)/shard_map/convert_element_type | solution.py:422
  1.9 0.3 collective-permute-done
  2.2 3.0 %collective-permute-start.1 = (f32[2,256]{1,0:T(2,128)S(1)}, f32[2,256]{1,0:T(2,128)S(1)}, u32[]{:S(2)}, u32[]{:S(2)}) collective-permute-start(f32[2,256]{1,0:T(2,128)S(1)} %pad_maximum_fusion.1), channel_id=1, source_target_pairs={{0,2},{1,3},{2,0},{3,1},{4,6},{5,7},{6,4},{7,5},{8,10},{9,11},{10,... | collective-permute-start | bytes 6152 | tf_op jit(solution)/shard_map/ppermute | solution.py:366
  5.2 2.6 %collective-permute-start.2 = (f32[2,256]{1,0:T(2,128)S(1)}, f32[2,256]{1,0:T(2,128)S(1)}, u32[]{:S(2)}, u32[]{:S(2)}) collective-permute-start(f32[2,256]{1,0:T(2,128)S(1)} %pad_maximum_fusion.1), channel_id=1, source_target_pairs={{0,4},{1,5},{2,6},{3,7},{4,0},{5,1},{6,2},{7,3},{8,12},{9,13},{10,... | collective-permute-start | bytes 6152 | tf_op jit(solution)/shard_map/ppermute | solution.py:366
  7.8 0.0 collective-permute-start.3
  7.8 2.5 %tables.1 = (bf16[2,1280,64]{2,1,0:T(8,128)(2,1)S(1)}, bf16[1024,16]{1,0:T(8,128)(2,1)S(1)}, f32[2,2,8,8]{3,2,1,0:T(8,128)S(1)}, f32[2,2,8,8]{3,2,1,0:T(8,128)S(...) custom-call(bf16[6,512]{1,0:T(8,128)(2,1)} %refs_0_.1, f32[1,512]{1,0:T(1,128)} %bitcast.31, ...), custom_call_target="tpu_custom_call" | custom-call | flops 20000000 | bytes 3000000 | tf_op jit(solution)/shard_map/tables/pallas_call | solution.py:433
  10.3 0.0 collective-permute-done.1
  10.3 0.0 collective-permute-done.2
  10.3 2.8 %collective-permute-done.3 = f32[2,256]{1,0:T(2,128)S(1)} collective-permute-done((f32[2,256]{1,0:T(2,128)S(1)}, f32[2,256]{1,0:T(2,128)S(1)}, u32[]{:S(2)}, u32[]{:S(2)}) %collective-permute-start.3) | collective-permute-done | bytes 2080 | tf_op jit(solution)/shard_map/ppermute | solution.py:366
  13.2 0.0 copy-done.1
  13.2 0.0 copy-done.2
  13.2 0.0 copy-done
  13.2 9.3 %layer.1 = (bf16[256,512]{1,0:T(8,128)(2,1)}, bf16[256,512]{1,0:T(8,128)(2,1)S(1)}, bf16[256,512]{1,0:T(8,128)(2,1)S(1)}) custom-call(f32[8,256]{1,0:T(8,128)S(1)} %concatenate.11.tok_ref, s32[1,307]{1,0:T(1,128)S(1)} %copy-done.1, s32[1,307]{1,0:T(1,128)S(1)} %copy-done.2, bf16[2,1280,64]{2,1,0:T(8,128)(2,1)S(1)} %get-tuple-element.11.conv_ref, ...), custom_call_target="tpu_custom_call" | custom-call | flops 2000000000 | bytes 4000000 | tf_op jit(solution)/shard_map/layer/pallas_call | solution.py:454
  22.6 0.1 collective-permute-start.4
  22.7 1.5 %collective-permute-done.4 = bf16[256,512]{1,0:T(8,128)(2,1)S(1)} collective-permute-done((bf16[256,512]{1,0:T(8,128)(2,1)S(1)}, bf16[256,512]{1,0:T(8,128)(2,1)S(1)}, u32[]{:S(2)}, u32[]{:S(2)}) %collective-permute-start.4) | collective-permute-done | bytes 262176 | tf_op jit(solution)/shard_map/ppermute | solution.py:366
  24.2 0.1 add_convert_fusion
  24.3 1.6 %collective-permute-start.5 = (bf16[64,512]{1,0:T(8,128)(2,1)S(1)}, bf16[64,512]{1,0:T(8,128)(2,1)S(1)}, u32[]{:S(2)}, u32[]{:S(2)}) collective-permute-start(bf16[64,512]{1,0:T(8,128)(2,1)S(1)} %get-tuple-element.26), channel_id=1, source_target_pairs={{0,8},{8,0},{16,24},{24,16},{1,9},{9,1},{17,25},{25,17},{2,10},{10... | collective-permute-start | bytes 196616 | tf_op jit(solution)/shard_map/ppermute | solution.py:366
  25.8 1.5 %collective-permute-start.6 = (bf16[64,512]{1,0:T(8,128)(2,1)S(1)}, bf16[64,512]{1,0:T(8,128)(2,1)S(1)}, u32[]{:S(2)}, u32[]{:S(2)}) collective-permute-start(bf16[64,512]{1,0:T(8,128)(2,1)S(1)} %get-tuple-element.28), channel_id=1, source_target_pairs={{0,16},{8,24},{16,0},{24,8},{1,17},{9,25},{17,1},{25,9},{2,18},{10... | collective-permute-start | bytes 196616 | tf_op jit(solution)/shard_map/ppermute | solution.py:366
  27.3 0.5 collective-permute-start.7
  27.8 0.8 %collective-permute-done.5 = bf16[64,512]{1,0:T(8,128)(2,1)S(1)} collective-permute-done((bf16[64,512]{1,0:T(8,128)(2,1)S(1)}, bf16[64,512]{1,0:T(8,128)(2,1)S(1)}, u32[]{:S(2)}, u32[]{:S(2)}) %collective-permute-start.5) | collective-permute-done | bytes 65568 | tf_op jit(solution)/shard_map/ppermute | solution.py:366
  28.6 1.5 %collective-permute-done.6 = bf16[64,512]{1,0:T(8,128)(2,1)S(1)} collective-permute-done((bf16[64,512]{1,0:T(8,128)(2,1)S(1)}, bf16[64,512]{1,0:T(8,128)(2,1)S(1)}, u32[]{:S(2)}, u32[]{:S(2)}) %collective-permute-start.6) | collective-permute-done | bytes 65568 | tf_op jit(solution)/shard_map/ppermute | solution.py:366
  30.1 2.4 %collective-permute-done.7 = bf16[64,512]{1,0:T(8,128)(2,1)S(1)} collective-permute-done((bf16[64,512]{1,0:T(8,128)(2,1)S(1)}, bf16[64,512]{1,0:T(8,128)(2,1)S(1)}, u32[]{:S(2)}, u32[]{:S(2)}) %collective-permute-start.7) | collective-permute-done | bytes 65568 | tf_op jit(solution)/shard_map/ppermute | solution.py:366
  32.5 1.1 %collective-permute-start.10 = (bf16[64,512]{1,0:T(8,128)(2,1)S(1)}, bf16[64,512]{1,0:T(8,128)(2,1)S(1)}, u32[]{:S(2)}, u32[]{:S(2)}) collective-permute-start(bf16[64,512]{1,0:T(8,128)(2,1)S(1)} %fusion.1), channel_id=1, source_target_pairs={{0,6},{1,7},{2,4},{3,5},{4,2},{5,3},{6,0},{7,1},{8,14},{9,15},{10,... | collective-permute-start | bytes 196616 | tf_op jit(solution)/shard_map/ppermute | solution.py:366
  33.6 0.0 collective-permute-start.8
  33.6 3.3 %collective-permute-start.9 = (bf16[64,512]{1,0:T(8,128)(2,1)S(1)}, bf16[64,512]{1,0:T(8,128)(2,1)S(1)}, u32[]{:S(2)}, u32[]{:S(2)}) collective-permute-start(bf16[64,512]{1,0:T(8,128)(2,1)S(1)} %fusion.1), channel_id=1, source_target_pairs={{0,4},{1,5},{2,6},{3,7},{4,0},{5,1},{6,2},{7,3},{8,12},{9,13},{10,... | collective-permute-start | bytes 196616 | tf_op jit(solution)/shard_map/ppermute | solution.py:366
  37.0 1.7 %collective-permute-done.10 = bf16[64,512]{1,0:T(8,128)(2,1)S(1)} collective-permute-done((bf16[64,512]{1,0:T(8,128)(2,1)S(1)}, bf16[64,512]{1,0:T(8,128)(2,1)S(1)}, u32[]{:S(2)}, u32[]{:S(2)}) %collective-permute-start.10) | collective-permute-done | bytes 65568 | tf_op jit(solution)/shard_map/ppermute | solution.py:366
  38.7 0.0 collective-permute-done.8
  38.7 0.7 %collective-permute-done.9 = bf16[64,512]{1,0:T(8,128)(2,1)S(1)} collective-permute-done((bf16[64,512]{1,0:T(8,128)(2,1)S(1)}, bf16[64,512]{1,0:T(8,128)(2,1)S(1)}, u32[]{:S(2)}, u32[]{:S(2)}) %collective-permute-start.9) | collective-permute-done | bytes 65568 | tf_op jit(solution)/shard_map/ppermute | solution.py:366
  39.4 0.6 %collective-permute-start.11 = (bf16[64,512]{1,0:T(8,128)(2,1)S(1)}, bf16[64,512]{1,0:T(8,128)(2,1)S(1)}, u32[]{:S(2)}, u32[]{:S(2)}) collective-permute-start(bf16[64,512]{1,0:T(8,128)(2,1)S(1)} %add_convert_fusion.1), channel_id=1, source_target_pairs={{0,8},{8,0},{16,24},{24,16},{1,9},{9,1},{17,25},{25,17},{2,10},{10... | collective-permute-start | bytes 196616 | tf_op jit(solution)/shard_map/ppermute | solution.py:366
  40.0 0.5 %collective-permute-start.12 = (bf16[64,512]{1,0:T(8,128)(2,1)S(1)}, bf16[64,512]{1,0:T(8,128)(2,1)S(1)}, u32[]{:S(2)}, u32[]{:S(2)}) collective-permute-start(bf16[64,512]{1,0:T(8,128)(2,1)S(1)} %add_convert_fusion.1), channel_id=1, source_target_pairs={{0,16},{8,24},{16,0},{24,8},{1,17},{9,25},{17,1},{25,9},{2,18},{10... | collective-permute-start | bytes 196616 | tf_op jit(solution)/shard_map/ppermute | solution.py:366
  40.5 2.4 %collective-permute-start.13 = (bf16[64,512]{1,0:T(8,128)(2,1)S(1)}, bf16[64,512]{1,0:T(8,128)(2,1)S(1)}, u32[]{:S(2)}, u32[]{:S(2)}) collective-permute-start(bf16[64,512]{1,0:T(8,128)(2,1)S(1)} %add_convert_fusion.1), channel_id=1, source_target_pairs={{0,24},{8,16},{16,8},{24,0},{1,25},{9,17},{17,9},{25,1},{2,26},{10... | collective-permute-start | bytes 196616 | tf_op jit(solution)/shard_map/ppermute | solution.py:366
  43.0 0.8 %collective-permute-done.11 = bf16[64,512]{1,0:T(8,128)(2,1)S(1)} collective-permute-done((bf16[64,512]{1,0:T(8,128)(2,1)S(1)}, bf16[64,512]{1,0:T(8,128)(2,1)S(1)}, u32[]{:S(2)}, u32[]{:S(2)}) %collective-permute-start.11) | collective-permute-done | bytes 65568 | tf_op jit(solution)/shard_map/ppermute | solution.py:366
  43.7 0.5 %collective-permute-done.12 = bf16[64,512]{1,0:T(8,128)(2,1)S(1)} collective-permute-done((bf16[64,512]{1,0:T(8,128)(2,1)S(1)}, bf16[64,512]{1,0:T(8,128)(2,1)S(1)}, u32[]{:S(2)}, u32[]{:S(2)}) %collective-permute-start.12) | collective-permute-done | bytes 65568 | tf_op jit(solution)/shard_map/ppermute | solution.py:366
  44.3 1.4 %collective-permute-done.13 = bf16[64,512]{1,0:T(8,128)(2,1)S(1)} collective-permute-done((bf16[64,512]{1,0:T(8,128)(2,1)S(1)}, bf16[64,512]{1,0:T(8,128)(2,1)S(1)}, u32[]{:S(2)}, u32[]{:S(2)}) %collective-permute-start.13) | collective-permute-done | bytes 65568 | tf_op jit(solution)/shard_map/ppermute | solution.py:366
  45.8 0.1 collective-permute-start.14
  45.9 1.5 %collective-permute-done.14 = bf16[256,512]{1,0:T(8,128)(2,1)S(1)} collective-permute-done((bf16[256,512]{1,0:T(8,128)(2,1)S(1)}, bf16[256,512]{1,0:T(8,128)(2,1)S(1)}, u32[]{:S(2)}, u32[]{:S(2)}) %collective-permute-start.14) | collective-permute-done | bytes 262176 | tf_op jit(solution)/shard_map/ppermute | solution.py:366
  47.4 0.1 broadcast_select_fusion.1
  47.4 1.1 %maximum_convert_fusion = f32[512,512]{1,0:T(8,128)} fusion(bf16[256,512]{1,0:T(8,128)(2,1)S(1)} %get-tuple-element.21, bf16[256,512]{1,0:T(8,128)(2,1)S(1)} %get-tuple-element.20), kind=kLoop, calls=%fused_computation | loop fusion | flops 1048576 | bytes 1572864 | tf_op jit(solution)/shard_map/convert_element_type | solution.py:409
  (8 shorter events, 0.2 us)
Async XLA Ops:
  0.6 12.5 %copy-start.1 = (s32[1,307]{1,0:T(1,128)S(1)}, s32[1,307]{1,0:T(1,128)}, u32[]{:S(2)}) copy-start(s32[1,307]{1,0:T(1,128)} %pos_ref.1) | copy-start | bytes 3688
  0.6 12.5 %copy-start.2 = (s32[1,307]{1,0:T(1,128)S(1)}, s32[1,307]{1,0:T(1,128)}, u32[]{:S(2)}) copy-start(s32[1,307]{1,0:T(1,128)} %rep_ref.1) | copy-start | bytes 3688
  0.7 12.5 %copy-start = (bf16[512,512]{1,0:T(8,128)(2,1)S(1)}, bf16[512,512]{1,0:T(8,128)(2,1)}, u32[]{:S(2)}) copy-start(bf16[512,512]{1,0:T(8,128)(2,1)} %wout_ref.1) | copy-start | bytes 1572868
  0.7 1.5 %collective-permute-start = (s32[1,256]{1,0:T(1,128)}, s32[1,256]{1,0:T(1,128)S(1)}, u32[]{:S(2)}, u32[]{:S(2)}) collective-permute-start(s32[1,256]{1,0:T(1,128)} %param.14), channel_id=1, source_target_pairs={{0,1},{1,0},{2,3},{3,2},{4,5},{5,4},{6,7},{7,6},{8,9},{9,8},{10,11... | collective-permute-start | bytes 3080 | tf_op jit(solution)/shard_map/ppermute | solution.py:366
  2.2 8.1 %collective-permute-start.1 = (f32[2,256]{1,0:T(2,128)S(1)}, f32[2,256]{1,0:T(2,128)S(1)}, u32[]{:S(2)}, u32[]{:S(2)}) collective-permute-start(f32[2,256]{1,0:T(2,128)S(1)} %pad_maximum_fusion.1), channel_id=1, source_target_pairs={{0,2},{1,3},{2,0},{3,1},{4,6},{5,7},{6,4},{7,5},{8,10},{9,11},{10,... | collective-permute-start | bytes 6152 | tf_op jit(solution)/shard_map/ppermute | solution.py:366
  5.2 5.2 %collective-permute-start.2 = (f32[2,256]{1,0:T(2,128)S(1)}, f32[2,256]{1,0:T(2,128)S(1)}, u32[]{:S(2)}, u32[]{:S(2)}) collective-permute-start(f32[2,256]{1,0:T(2,128)S(1)} %pad_maximum_fusion.1), channel_id=1, source_target_pairs={{0,4},{1,5},{2,6},{3,7},{4,0},{5,1},{6,2},{7,3},{8,12},{9,13},{10,... | collective-permute-start | bytes 6152 | tf_op jit(solution)/shard_map/ppermute | solution.py:366
  7.8 5.4 %collective-permute-start.3 = (f32[2,256]{1,0:T(2,128)S(1)}, f32[2,256]{1,0:T(2,128)S(1)}, u32[]{:S(2)}, u32[]{:S(2)}) collective-permute-start(f32[2,256]{1,0:T(2,128)S(1)} %pad_maximum_fusion.1), channel_id=1, source_target_pairs={{0,6},{1,7},{2,4},{3,5},{4,2},{5,3},{6,0},{7,1},{8,14},{9,15},{10,... | collective-permute-start | bytes 6152 | tf_op jit(solution)/shard_map/ppermute | solution.py:366
  22.6 1.6 %collective-permute-start.4 = (bf16[256,512]{1,0:T(8,128)(2,1)S(1)}, bf16[256,512]{1,0:T(8,128)(2,1)S(1)}, u32[]{:S(2)}, u32[]{:S(2)}) collective-permute-start(bf16[256,512]{1,0:T(8,128)(2,1)S(1)} %get-tuple-element.19), channel_id=1, source_target_pairs={{0,1},{1,0},{2,3},{3,2},{4,5},{5,4},{6,7},{7,6},{8,9},{9,8},{10,11... | collective-permute-start | bytes 786440 | tf_op jit(solution)/shard_map/ppermute | solution.py:366
  24.3 4.3 %collective-permute-start.5 = (bf16[64,512]{1,0:T(8,128)(2,1)S(1)}, bf16[64,512]{1,0:T(8,128)(2,1)S(1)}, u32[]{:S(2)}, u32[]{:S(2)}) collective-permute-start(bf16[64,512]{1,0:T(8,128)(2,1)S(1)} %get-tuple-element.26), channel_id=1, source_target_pairs={{0,8},{8,0},{16,24},{24,16},{1,9},{9,1},{17,25},{25,17},{2,10},{10... | collective-permute-start | bytes 196616 | tf_op jit(solution)/shard_map/ppermute | solution.py:366
  25.8 4.3 %collective-permute-start.6 = (bf16[64,512]{1,0:T(8,128)(2,1)S(1)}, bf16[64,512]{1,0:T(8,128)(2,1)S(1)}, u32[]{:S(2)}, u32[]{:S(2)}) collective-permute-start(bf16[64,512]{1,0:T(8,128)(2,1)S(1)} %get-tuple-element.28), channel_id=1, source_target_pairs={{0,16},{8,24},{16,0},{24,8},{1,17},{9,25},{17,1},{25,9},{2,18},{10... | collective-permute-start | bytes 196616 | tf_op jit(solution)/shard_map/ppermute | solution.py:366
  27.3 5.2 %collective-permute-start.7 = (bf16[64,512]{1,0:T(8,128)(2,1)S(1)}, bf16[64,512]{1,0:T(8,128)(2,1)S(1)}, u32[]{:S(2)}, u32[]{:S(2)}) collective-permute-start(bf16[64,512]{1,0:T(8,128)(2,1)S(1)} %get-tuple-element.27), channel_id=1, source_target_pairs={{0,24},{8,16},{16,8},{24,0},{1,25},{9,17},{17,9},{25,1},{2,26},{10... | collective-permute-start | bytes 196616 | tf_op jit(solution)/shard_map/ppermute | solution.py:366
  32.5 6.1 %collective-permute-start.10 = (bf16[64,512]{1,0:T(8,128)(2,1)S(1)}, bf16[64,512]{1,0:T(8,128)(2,1)S(1)}, u32[]{:S(2)}, u32[]{:S(2)}) collective-permute-start(bf16[64,512]{1,0:T(8,128)(2,1)S(1)} %fusion.1), channel_id=1, source_target_pairs={{0,6},{1,7},{2,4},{3,5},{4,2},{5,3},{6,0},{7,1},{8,14},{9,15},{10,... | collective-permute-start | bytes 196616 | tf_op jit(solution)/shard_map/ppermute | solution.py:366
  33.6 5.0 %collective-permute-start.8 = (bf16[64,512]{1,0:T(8,128)(2,1)S(1)}, bf16[64,512]{1,0:T(8,128)(2,1)S(1)}, u32[]{:S(2)}, u32[]{:S(2)}) collective-permute-start(bf16[64,512]{1,0:T(8,128)(2,1)S(1)} %fusion.1), channel_id=1, source_target_pairs={{0,2},{1,3},{2,0},{3,1},{4,6},{5,7},{6,4},{7,5},{8,10},{9,11},{10,... | collective-permute-start | bytes 196616 | tf_op jit(solution)/shard_map/ppermute | solution.py:366
  33.6 5.7 %collective-permute-start.9 = (bf16[64,512]{1,0:T(8,128)(2,1)S(1)}, bf16[64,512]{1,0:T(8,128)(2,1)S(1)}, u32[]{:S(2)}, u32[]{:S(2)}) collective-permute-start(bf16[64,512]{1,0:T(8,128)(2,1)S(1)} %fusion.1), channel_id=1, source_target_pairs={{0,4},{1,5},{2,6},{3,7},{4,0},{5,1},{6,2},{7,3},{8,12},{9,13},{10,... | collective-permute-start | bytes 196616 | tf_op jit(solution)/shard_map/ppermute | solution.py:366
  39.4 4.3 %collective-permute-start.11 = (bf16[64,512]{1,0:T(8,128)(2,1)S(1)}, bf16[64,512]{1,0:T(8,128)(2,1)S(1)}, u32[]{:S(2)}, u32[]{:S(2)}) collective-permute-start(bf16[64,512]{1,0:T(8,128)(2,1)S(1)} %add_convert_fusion.1), channel_id=1, source_target_pairs={{0,8},{8,0},{16,24},{24,16},{1,9},{9,1},{17,25},{25,17},{2,10},{10... | collective-permute-start | bytes 196616 | tf_op jit(solution)/shard_map/ppermute | solution.py:366
  40.0 4.3 %collective-permute-start.12 = (bf16[64,512]{1,0:T(8,128)(2,1)S(1)}, bf16[64,512]{1,0:T(8,128)(2,1)S(1)}, u32[]{:S(2)}, u32[]{:S(2)}) collective-permute-start(bf16[64,512]{1,0:T(8,128)(2,1)S(1)} %add_convert_fusion.1), channel_id=1, source_target_pairs={{0,16},{8,24},{16,0},{24,8},{1,17},{9,25},{17,1},{25,9},{2,18},{10... | collective-permute-start | bytes 196616 | tf_op jit(solution)/shard_map/ppermute | solution.py:366
  40.5 5.2 %collective-permute-start.13 = (bf16[64,512]{1,0:T(8,128)(2,1)S(1)}, bf16[64,512]{1,0:T(8,128)(2,1)S(1)}, u32[]{:S(2)}, u32[]{:S(2)}) collective-permute-start(bf16[64,512]{1,0:T(8,128)(2,1)S(1)} %add_convert_fusion.1), channel_id=1, source_target_pairs={{0,24},{8,16},{16,8},{24,0},{1,25},{9,17},{17,9},{25,1},{2,26},{10... | collective-permute-start | bytes 196616 | tf_op jit(solution)/shard_map/ppermute | solution.py:366
  45.8 1.6 %collective-permute-start.14 = (bf16[256,512]{1,0:T(8,128)(2,1)S(1)}, bf16[256,512]{1,0:T(8,128)(2,1)S(1)}, u32[]{:S(2)}, u32[]{:S(2)}) collective-permute-start(bf16[256,512]{1,0:T(8,128)(2,1)S(1)} %bitcast.28), channel_id=1, source_target_pairs={{0,1},{1,0},{2,3},{3,2},{4,5},{5,4},{6,7},{7,6},{8,9},{9,8},{10,11... | collective-permute-start | bytes 786440 | tf_op jit(solution)/shard_map/ppermute | solution.py:366

commit v3 on v2

--- a/solution.py
+++ b/solution.py
@@ -107,7 +107,7 @@
     n, length, masked_total,
     tok_ref, pos_ref, rep_ref, conv_ref, gate_ref, step_ref, decay_ref, gain_ref, headt_ref, wout_ref,
     layer_out, send_out, keep_out,
-    pos_s, rep_s, ids_s, val_s, step_s, log_s, cum_s, tot_s, scaled_s, state_s, y_s, comb_s,
+    pos_s, rep_s, ids_s, val_s, step_s, log_s, cum_s, tot_s, own_s, from_s, near_s, far_s, farb_s, state_s, y_s, comb_s,
 ):
     me = lax.axis_index("seq")
     nb = length // SPAN
@@ -233,8 +233,6 @@
     else:
         lax.fori_loop(0, n - 1, lambda k, c: tuple(weigh(k, list(c))), tuple(far))
 
-    state_s[...] = jnp.zeros_like(state_s)
-
     def across(array, strand):
         return jnp.concatenate([part(array, strand, b) for b in range(nb)], axis=1)
 
@@ -247,73 +245,108 @@
             axis=0,
         )
 
-    def gather_state(k):
+    def gather_state(k, spot):
         unit, side = slot_of(k)
         hot = one_hots(unit, side)
         weight = step_s[k]
+        at = slice(spot * length, (spot + 1) * length)
         for strand in range(2):
             row8 = across(weight, strand)
             base = strand * CONVW
-            slot = (k * 2 + strand) % 4
             for c in range(4):
                 half = mm(conv_ref[side, base + c * 128 : base + (c + 1) * 128, :], hot)
-                scaled_s[slot, c * 128 : (c + 1) * 128, :] = per_head(
+                far_s[strand, c * 128 : (c + 1) * 128, at] = per_head(
                     silu_half(half), row8, 2 * c
                 ).astype(BF16)
             b_t = silu_half(mm(conv_ref[side, base + INNER : base + INNER + STATE, :], hot))
-            state_s[side, strand] += mm(scaled_s[slot], b_t.astype(BF16), NT)
-
-    loop(n - 1, gather_state)
+            farb_s[strand, :STATE, at] = jnp.where(side == 0, b_t, 0.0).astype(BF16)
+            farb_s[strand, STATE:, at] = jnp.where(side == 0, 0.0, b_t).astype(BF16)
+
+    if unrolled:
+        for k in range(n - 1):
+            gather_state(k, k)
+        for strand in range(2):
+            state_s[strand] = mm(far_s[strand], farb_s[strand], NT)
+    else:
+        state_s[...] = jnp.zeros_like(state_s)
+
+        def add_state(k):
+            gather_state(k, 0)
+            for strand in range(2):
+                state_s[strand] += mm(far_s[strand], farb_s[strand], NT)
+
+        loop(n - 1, add_state)
 
     row_i = lax.broadcasted_iota(jnp.int32, (SPAN, SPAN), 0)
     col_i = lax.broadcasted_iota(jnp.int32, (SPAN, SPAN), 1)
+    sides = []
     for side in range(2):
-        hot = one_hots(me, side)
         slot = n - 1 + side
         steps, cums, logs_k, tots = step_s[slot], cum_s[slot], log_s[slot], tot_s[slot]
         if side == 1:
             cums = tots - cums + logs_k
-        cols = jnp.transpose(cums)
-        for strand in range(2):
-            base = strand * CONVW
+        sides.append((one_hots(me, side), steps, cums, tots, jnp.transpose(cums)))
+    for strand in range(2):
+        base = strand * CONVW
+        states = state_s[strand].astype(BF16)
+        scores, grown, near = {}, {}, {}
+        for side in range(2):
+            hot, steps, cums, tots, _ = sides[side]
             row8 = across(steps, strand)
-            buf = side * 2 + strand
             for c in range(4):
                 half = mm(conv_ref[side, base + c * 128 : base + (c + 1) * 128, :], hot)
-                scaled_s[buf, c * 128 : (c + 1) * 128, :] = per_head(
-                    silu_half(half), row8, 2 * c
-                ).astype(BF16)
+                x = per_head(silu_half(half), row8, 2 * c).astype(BF16)
+                for b in range(nb):
+                    to = (b * 2 + side) * SPAN
+                    own_s[strand, c * 128 : (c + 1) * 128, to : to + SPAN] = x[:, b * SPAN : (b + 1) * SPAN]
             bc_t = silu_half(mm(conv_ref[side, base + INNER : base + CONVW, :], hot))
-            state = state_s[side, strand]
+            c_only = bc_t[STATE:]
+            none = jnp.zeros_like(c_only)
+            c_both = jnp.concatenate([c_only, none] if side == 0 else [none, c_only], axis=0)
+            from_s[strand, side] = mm(states, c_both.astype(BF16))
+            c_t, b_t = c_only.astype(BF16), bc_t[:STATE].astype(BF16)
+            ahead = jnp.zeros((8, SPAN), F32)
+            local = None
             for step_index in range(nb):
                 b = step_index if side == 0 else nb - 1 - step_index
                 at = slice(b * SPAN, (b + 1) * SPAN)
-                bc_blk = bc_t[:, at]
-                b_rows = jnp.transpose(bc_blk)[:, :STATE].astype(BF16)
-                c_t = bc_blk[STATE:].astype(BF16)
-                b_t = bc_blk[:STATE].astype(BF16)
-                scores = mm(b_rows, c_t)
+                b_rows = jnp.transpose(bc_t[:, at])[:, :STATE].astype(BF16)
                 causal = (row_i <= col_i) if side == 0 else (row_i >= col_i)
-                scores = jnp.where(causal, scores, 0.0)
-                cs = part(cums, strand, b)
-                tot = part(tots, strand, b)
-                carried = mm(state.astype(BF16), c_t)
-                grow = jnp.exp(cs)
-                for h in range(HEADS):
+                scores[side, b] = jnp.where(causal, mm(b_rows, c_t[:, at]), 0.0)
+                cs, tot = part(cums, strand, b), part(tots, strand, b)
+                grown[side, b] = (jnp.exp(cs), jnp.exp(cs + ahead))
+                near[side, b] = local is not None
+                if local is not None:
+                    near_s[strand, side, :, at] = mm(local.astype(BF16), c_t[:, at])
+                if step_index < nb - 1:
+                    to = (b * 2 + side) * SPAN
+                    decayed = per_head(
+                        own_s[strand, :, to : to + SPAN].astype(F32), jnp.exp(tot - cs), 0
+                    ).astype(BF16)
+                    fresh = mm(decayed, b_t[:, at], NT)
+                    if local is not None:
+                        fresh = fresh + per_head(local, jnp.exp(tot)[:, :STATE], 0)
+                    local = fresh
+                    ahead = ahead + tot
+        for b in range(nb):
+            at = slice(b * SPAN, (b + 1) * SPAN)
+            for h in range(HEADS):
+                hs = slice(h * HEADDIM, (h + 1) * HEADDIM)
+                both = []
+                for side in range(2):
                     col = (strand * nb + b) * 8 + h
-                    e = cs[h : h + 1] - cols[:, col : col + 1]
-                    w = (scores * jnp.exp(jnp.minimum(e, 0.0))).astype(BF16)
-                    hs = slice(h * HEADDIM, (h + 1) * HEADDIM)
-                    y = mm(scaled_s[buf, hs, at], w) + carried[hs] * grow[h : h + 1]
-                    if side == 0:
-                        y_s[strand, hs, at] = y
-                    else:
-                        y_s[strand, hs, at] += y
-                if step_index < nb - 1:
-                    decayed = per_head(
-                        scaled_s[buf, :, at].astype(F32), jnp.exp(tot - cs), 0
-                    ).astype(BF16)
-                    state = per_head(state, jnp.exp(tot)[:, :STATE], 0) + mm(decayed, b_t, NT)
+                    e = part(sides[side][2], strand, b)[h : h + 1] - sides[side][4][:, col : col + 1]
+                    both.append((scores[side, b] * jnp.exp(jnp.minimum(e, 0.0))).astype(BF16))
+                y = mm(
+                    own_s[strand, hs, b * 2 * SPAN : (b + 1) * 2 * SPAN],
+                    jnp.concatenate(both, axis=0),
+                )
+                for side in range(2):
+                    here, far_grow = grown[side, b]
+                    y = y + from_s[strand, side, hs, at] * far_grow[h : h + 1]
+                    if near[side, b]:
+                        y = y + near_s[strand, side, hs, at] * here[h : h + 1]
+                y_s[strand, hs, at] = y
 
     hot0 = (sub8 == ids_s[pl.ds(me + 1, 1), :]).astype(F32)
     hot0 = jnp.concatenate([hot0, hot0], axis=0).astype(BF16)
@@ -450,6 +483,7 @@
     masks = mask_pos.shape[1]
     wide = -(-masks // 128) * 128
     slots = n + 1
+    spots = n - 1 if n <= 16 else 1
     operands = (gathered, mask_pos, replace_ids, *tables, w_out)
     layer_out, send, keep = pl.pallas_call(
         functools.partial(layer_kernel, n, length, lax.axis_size("dp") * masks),
@@ -467,8 +501,12 @@
             pltpu.VMEM((slots, rows, SPAN), F32),
             pltpu.VMEM((slots, rows, SPAN), F32),
             pltpu.VMEM((slots, rows, SPAN), F32),
-            pltpu.VMEM((4, INNER, length), BF16),
-            pltpu.VMEM((2, 2, INNER, STATE), F32),
+            pltpu.VMEM((2, INNER, 2 * length), BF16),
+            pltpu.VMEM((2, 2, INNER, length), F32),
+            pltpu.VMEM((2, 2, INNER, length), F32),
+            pltpu.VMEM((2, INNER, spots * length), BF16),
+            pltpu.VMEM((2, 2 * STATE, spots * length), BF16),
+            pltpu.VMEM((2, INNER, 2 * STATE), F32),
             pltpu.VMEM((2, INNER, length), F32),
             pltpu.VMEM((INNER, length), BF16),
         ],

time: 48.7 us -> 46.5 us (0.955)
  Pallas kernels: 11.9 us -> 9.67 us
    pallas_call x1, Pallas kernels: 9.34 us -> 7.12 us  [per_device(): pl.pallas_call(functools.partial(layer_kernel, n, length, lax.axis_size('...]
  transfers between devices with their start and end apart: 15 -> 15, of which waited for: 12 -> 12; matrix products, arithmetic and copies ran while one was open for 1% -> 1% of each run, Pallas kernels for 5% -> 6%
where the time goes in v3:
time: 46.5 us; the launch traced here: 46.3 us
  starting transfers between devices  17.8 us (38%)
  waiting for transfers between devices  15.9 us (34%)
  Pallas kernels  9.67 us (21%)
  other arithmetic  2.06 us (4%)
  between operations  0.8 us (2%)
    ppermute x15, starting transfers between devices, swap(): lax.ppermute(value, axis, [(i, i ^ k) for i in range(lax.axis_size(axis))])  17.8 us
    ppermute x15, waiting for transfers between devices, swap(): lax.ppermute(value, axis, [(i, i ^ k) for i in range(lax.axis_size(axis))])  15.9 us
    pallas_call x1, Pallas kernels, per_device(): pl.pallas_call(functools.partial(layer_kernel, n, length, lax.axis_size('...  7.12 us
    pallas_call x1, Pallas kernels, per_device(): pl.pallas_call(tables_kernel, in_specs=[pl.BlockSpec(memory_space=pltpu.H...  2.55 us
    convert_element_type x1, other arithmetic, sum_all(): return jnp.concatenate([low, high], axis=0).astype(F32)  1.1 us
  transfers between devices with their start and end apart: 15, of which 12 were waited for; matrix products, arithmetic and copies ran while one was open for 1% of the time, Pallas kernels for 6%

profile of v3, /device:TPU:0, one launch (start us, length us, event | category | flops | bytes accessed | tf_op | source)
XLA Modules:
  0.0 46.3 jit_solution(8756007389869684335)
XLA Ops:
  0.6 0.0 copy-start.1
  0.6 0.0 copy-start.2
  0.7 0.0 copy-start
  0.7 0.5 %collective-permute-start = (s32[1,256]{1,0:T(1,128)}, s32[1,256]{1,0:T(1,128)S(1)}, u32[]{:S(2)}, u32[]{:S(2)}) collective-permute-start(s32[1,256]{1,0:T(1,128)} %param.14), channel_id=1, source_target_pairs={{0,1},{1,0},{2,3},{3,2},{4,5},{5,4},{6,7},{7,6},{8,9},{9,8},{10,11... | collective-permute-start | bytes 3080 | tf_op jit(solution)/shard_map/ppermute | solution.py:399
  1.2 0.7 %convert_element_type.51 = f32[1,256]{1,0:T(1,128)S(1)} convert(s32[1,256]{1,0:T(1,128)} %param.14) | non-fusion elementwise | flops 256 | bytes 2048 | tf_op jit(solution)/shard_map/convert_element_type | solution.py:455
  1.9 0.3 collective-permute-done
  2.2 3.0 %collective-permute-start.1 = (f32[2,256]{1,0:T(2,128)S(1)}, f32[2,256]{1,0:T(2,128)S(1)}, u32[]{:S(2)}, u32[]{:S(2)}) collective-permute-start(f32[2,256]{1,0:T(2,128)S(1)} %pad_maximum_fusion.1), channel_id=1, source_target_pairs={{0,2},{1,3},{2,0},{3,1},{4,6},{5,7},{6,4},{7,5},{8,10},{9,11},{10,... | collective-permute-start | bytes 6152 | tf_op jit(solution)/shard_map/ppermute | solution.py:399
  5.2 2.6 %collective-permute-start.2 = (f32[2,256]{1,0:T(2,128)S(1)}, f32[2,256]{1,0:T(2,128)S(1)}, u32[]{:S(2)}, u32[]{:S(2)}) collective-permute-start(f32[2,256]{1,0:T(2,128)S(1)} %pad_maximum_fusion.1), channel_id=1, source_target_pairs={{0,4},{1,5},{2,6},{3,7},{4,0},{5,1},{6,2},{7,3},{8,12},{9,13},{10,... | collective-permute-start | bytes 6152 | tf_op jit(solution)/shard_map/ppermute | solution.py:399
  7.8 0.0 collective-permute-start.3
  7.8 2.5 %tables.1 = (bf16[2,1280,64]{2,1,0:T(8,128)(2,1)S(1)}, bf16[1024,16]{1,0:T(8,128)(2,1)S(1)}, f32[2,2,8,8]{3,2,1,0:T(8,128)S(1)}, f32[2,2,8,8]{3,2,1,0:T(8,128)S(...) custom-call(bf16[6,512]{1,0:T(8,128)(2,1)} %refs_0_.1, f32[1,512]{1,0:T(1,128)} %bitcast.31, ...), custom_call_target="tpu_custom_call" | custom-call | flops 20000000 | bytes 3000000 | tf_op jit(solution)/shard_map/tables/pallas_call | solution.py:466
  10.3 0.0 collective-permute-done.1
  10.3 0.0 collective-permute-done.2
  10.3 2.8 %collective-permute-done.3 = f32[2,256]{1,0:T(2,128)S(1)} collective-permute-done((f32[2,256]{1,0:T(2,128)S(1)}, f32[2,256]{1,0:T(2,128)S(1)}, u32[]{:S(2)}, u32[]{:S(2)}) %collective-permute-start.3) | collective-permute-done | bytes 2080 | tf_op jit(solution)/shard_map/ppermute | solution.py:399
  13.2 0.0 copy-done.1
  13.2 0.0 copy-done.2
  13.2 0.0 copy-done
  13.2 7.1 %layer.1 = (bf16[256,512]{1,0:T(8,128)(2,1)}, bf16[256,512]{1,0:T(8,128)(2,1)S(1)}, bf16[256,512]{1,0:T(8,128)(2,1)S(1)}) custom-call(f32[8,256]{1,0:T(8,128)S(1)} %concatenate.11.tok_ref, s32[1,307]{1,0:T(1,128)S(1)} %copy-done.1, s32[1,307]{1,0:T(1,128)S(1)} %copy-done.2, bf16[2,1280,64]{2,1,0:T(8,128)(2,1)S(1)} %get-tuple-element.11.conv_ref, ...), custom_call_target="tpu_custom_call" | custom-call | flops 2000000000 | bytes 4000000 | tf_op jit(solution)/shard_map/layer/pallas_call | solution.py:488
  20.3 0.1 collective-permute-start.4
  20.4 1.5 %collective-permute-done.4 = bf16[256,512]{1,0:T(8,128)(2,1)S(1)} collective-permute-done((bf16[256,512]{1,0:T(8,128)(2,1)S(1)}, bf16[256,512]{1,0:T(8,128)(2,1)S(1)}, u32[]{:S(2)}, u32[]{:S(2)}) %collective-permute-start.4) | collective-permute-done | bytes 262176 | tf_op jit(solution)/shard_map/ppermute | solution.py:399
  21.9 0.1 add_convert_fusion
  22.0 1.6 %collective-permute-start.5 = (bf16[64,512]{1,0:T(8,128)(2,1)S(1)}, bf16[64,512]{1,0:T(8,128)(2,1)S(1)}, u32[]{:S(2)}, u32[]{:S(2)}) collective-permute-start(bf16[64,512]{1,0:T(8,128)(2,1)S(1)} %get-tuple-element.26), channel_id=1, source_target_pairs={{0,8},{8,0},{16,24},{24,16},{1,9},{9,1},{17,25},{25,17},{2,10},{10... | collective-permute-start | bytes 196616 | tf_op jit(solution)/shard_map/ppermute | solution.py:399
  23.6 1.5 %collective-permute-start.6 = (bf16[64,512]{1,0:T(8,128)(2,1)S(1)}, bf16[64,512]{1,0:T(8,128)(2,1)S(1)}, u32[]{:S(2)}, u32[]{:S(2)}) collective-permute-start(bf16[64,512]{1,0:T(8,128)(2,1)S(1)} %get-tuple-element.28), channel_id=1, source_target_pairs={{0,16},{8,24},{16,0},{24,8},{1,17},{9,25},{17,1},{25,9},{2,18},{10... | collective-permute-start | bytes 196616 | tf_op jit(solution)/shard_map/ppermute | solution.py:399
  25.1 0.5 collective-permute-start.7
  25.6 0.8 %collective-permute-done.5 = bf16[64,512]{1,0:T(8,128)(2,1)S(1)} collective-permute-done((bf16[64,512]{1,0:T(8,128)(2,1)S(1)}, bf16[64,512]{1,0:T(8,128)(2,1)S(1)}, u32[]{:S(2)}, u32[]{:S(2)}) %collective-permute-start.5) | collective-permute-done | bytes 65568 | tf_op jit(solution)/shard_map/ppermute | solution.py:399
  26.4 1.5 %collective-permute-done.6 = bf16[64,512]{1,0:T(8,128)(2,1)S(1)} collective-permute-done((bf16[64,512]{1,0:T(8,128)(2,1)S(1)}, bf16[64,512]{1,0:T(8,128)(2,1)S(1)}, u32[]{:S(2)}, u32[]{:S(2)}) %collective-permute-start.6) | collective-permute-done | bytes 65568 | tf_op jit(solution)/shard_map/ppermute | solution.py:399
  27.9 2.4 %collective-permute-done.7 = bf16[64,512]{1,0:T(8,128)(2,1)S(1)} collective-permute-done((bf16[64,512]{1,0:T(8,128)(2,1)S(1)}, bf16[64,512]{1,0:T(8,128)(2,1)S(1)}, u32[]{:S(2)}, u32[]{:S(2)}) %collective-permute-start.7) | collective-permute-done | bytes 65568 | tf_op jit(solution)/shard_map/ppermute | solution.py:399
  30.3 1.1 %collective-permute-start.10 = (bf16[64,512]{1,0:T(8,128)(2,1)S(1)}, bf16[64,512]{1,0:T(8,128)(2,1)S(1)}, u32[]{:S(2)}, u32[]{:S(2)}) collective-permute-start(bf16[64,512]{1,0:T(8,128)(2,1)S(1)} %fusion.1), channel_id=1, source_target_pairs={{0,6},{1,7},{2,4},{3,5},{4,2},{5,3},{6,0},{7,1},{8,14},{9,15},{10,... | collective-permute-start | bytes 196616 | tf_op jit(solution)/shard_map/ppermute | solution.py:399
  31.4 0.0 collective-permute-start.8
  31.4 3.4 %collective-permute-start.9 = (bf16[64,512]{1,0:T(8,128)(2,1)S(1)}, bf16[64,512]{1,0:T(8,128)(2,1)S(1)}, u32[]{:S(2)}, u32[]{:S(2)}) collective-permute-start(bf16[64,512]{1,0:T(8,128)(2,1)S(1)} %fusion.1), channel_id=1, source_target_pairs={{0,4},{1,5},{2,6},{3,7},{4,0},{5,1},{6,2},{7,3},{8,12},{9,13},{10,... | collective-permute-start | bytes 196616 | tf_op jit(solution)/shard_map/ppermute | solution.py:399
  34.8 1.7 %collective-permute-done.10 = bf16[64,512]{1,0:T(8,128)(2,1)S(1)} collective-permute-done((bf16[64,512]{1,0:T(8,128)(2,1)S(1)}, bf16[64,512]{1,0:T(8,128)(2,1)S(1)}, u32[]{:S(2)}, u32[]{:S(2)}) %collective-permute-start.10) | collective-permute-done | bytes 65568 | tf_op jit(solution)/shard_map/ppermute | solution.py:399
  36.5 0.0 collective-permute-done.8
  36.5 0.7 %collective-permute-done.9 = bf16[64,512]{1,0:T(8,128)(2,1)S(1)} collective-permute-done((bf16[64,512]{1,0:T(8,128)(2,1)S(1)}, bf16[64,512]{1,0:T(8,128)(2,1)S(1)}, u32[]{:S(2)}, u32[]{:S(2)}) %collective-permute-start.9) | collective-permute-done | bytes 65568 | tf_op jit(solution)/shard_map/ppermute | solution.py:399
  37.2 0.6 %collective-permute-start.11 = (bf16[64,512]{1,0:T(8,128)(2,1)S(1)}, bf16[64,512]{1,0:T(8,128)(2,1)S(1)}, u32[]{:S(2)}, u32[]{:S(2)}) collective-permute-start(bf16[64,512]{1,0:T(8,128)(2,1)S(1)} %add_convert_fusion.1), channel_id=1, source_target_pairs={{0,8},{8,0},{16,24},{24,16},{1,9},{9,1},{17,25},{25,17},{2,10},{10... | collective-permute-start | bytes 196616 | tf_op jit(solution)/shard_map/ppermute | solution.py:399
  37.8 0.5 %collective-permute-start.12 = (bf16[64,512]{1,0:T(8,128)(2,1)S(1)}, bf16[64,512]{1,0:T(8,128)(2,1)S(1)}, u32[]{:S(2)}, u32[]{:S(2)}) collective-permute-start(bf16[64,512]{1,0:T(8,128)(2,1)S(1)} %add_convert_fusion.1), channel_id=1, source_target_pairs={{0,16},{8,24},{16,0},{24,8},{1,17},{9,25},{17,1},{25,9},{2,18},{10... | collective-permute-start | bytes 196616 | tf_op jit(solution)/shard_map/ppermute | solution.py:399
  38.3 2.5 %collective-permute-start.13 = (bf16[64,512]{1,0:T(8,128)(2,1)S(1)}, bf16[64,512]{1,0:T(8,128)(2,1)S(1)}, u32[]{:S(2)}, u32[]{:S(2)}) collective-permute-start(bf16[64,512]{1,0:T(8,128)(2,1)S(1)} %add_convert_fusion.1), channel_id=1, source_target_pairs={{0,24},{8,16},{16,8},{24,0},{1,25},{9,17},{17,9},{25,1},{2,26},{10... | collective-permute-start | bytes 196616 | tf_op jit(solution)/shard_map/ppermute | solution.py:399
  40.8 0.8 %collective-permute-done.11 = bf16[64,512]{1,0:T(8,128)(2,1)S(1)} collective-permute-done((bf16[64,512]{1,0:T(8,128)(2,1)S(1)}, bf16[64,512]{1,0:T(8,128)(2,1)S(1)}, u32[]{:S(2)}, u32[]{:S(2)}) %collective-permute-start.11) | collective-permute-done | bytes 65568 | tf_op jit(solution)/shard_map/ppermute | solution.py:399
  41.5 0.5 %collective-permute-done.12 = bf16[64,512]{1,0:T(8,128)(2,1)S(1)} collective-permute-done((bf16[64,512]{1,0:T(8,128)(2,1)S(1)}, bf16[64,512]{1,0:T(8,128)(2,1)S(1)}, u32[]{:S(2)}, u32[]{:S(2)}) %collective-permute-start.12) | collective-permute-done | bytes 65568 | tf_op jit(solution)/shard_map/ppermute | solution.py:399
  42.1 1.4 %collective-permute-done.13 = bf16[64,512]{1,0:T(8,128)(2,1)S(1)} collective-permute-done((bf16[64,512]{1,0:T(8,128)(2,1)S(1)}, bf16[64,512]{1,0:T(8,128)(2,1)S(1)}, u32[]{:S(2)}, u32[]{:S(2)}) %collective-permute-start.13) | collective-permute-done | bytes 65568 | tf_op jit(solution)/shard_map/ppermute | solution.py:399
  43.5 0.1 collective-permute-start.14
  43.6 1.5 %collective-permute-done.14 = bf16[256,512]{1,0:T(8,128)(2,1)S(1)} collective-permute-done((bf16[256,512]{1,0:T(8,128)(2,1)S(1)}, bf16[256,512]{1,0:T(8,128)(2,1)S(1)}, u32[]{:S(2)}, u32[]{:S(2)}) %collective-permute-start.14) | collective-permute-done | bytes 262176 | tf_op jit(solution)/shard_map/ppermute | solution.py:399
  45.1 0.1 broadcast_select_fusion.1
  45.2 1.1 %maximum_convert_fusion = f32[512,512]{1,0:T(8,128)} fusion(bf16[256,512]{1,0:T(8,128)(2,1)S(1)} %get-tuple-element.21, bf16[256,512]{1,0:T(8,128)(2,1)S(1)} %get-tuple-element.20), kind=kLoop, calls=%fused_computation | loop fusion | flops 1048576 | bytes 1572864 | tf_op jit(solution)/shard_map/convert_element_type | solution.py:442
  (8 shorter events, 0.2 us)
Async XLA Ops:
  0.6 12.5 %copy-start.1 = (s32[1,307]{1,0:T(1,128)S(1)}, s32[1,307]{1,0:T(1,128)}, u32[]{:S(2)}) copy-start(s32[1,307]{1,0:T(1,128)} %pos_ref.1) | copy-start | bytes 3688
  0.6 12.5 %copy-start.2 = (s32[1,307]{1,0:T(1,128)S(1)}, s32[1,307]{1,0:T(1,128)}, u32[]{:S(2)}) copy-start(s32[1,307]{1,0:T(1,128)} %rep_ref.1) | copy-start | bytes 3688
  0.7 12.5 %copy-start = (bf16[512,512]{1,0:T(8,128)(2,1)S(1)}, bf16[512,512]{1,0:T(8,128)(2,1)}, u32[]{:S(2)}) copy-start(bf16[512,512]{1,0:T(8,128)(2,1)} %wout_ref.1) | copy-start | bytes 1572868
  0.7 1.5 %collective-permute-start = (s32[1,256]{1,0:T(1,128)}, s32[1,256]{1,0:T(1,128)S(1)}, u32[]{:S(2)}, u32[]{:S(2)}) collective-permute-start(s32[1,256]{1,0:T(1,128)} %param.14), channel_id=1, source_target_pairs={{0,1},{1,0},{2,3},{3,2},{4,5},{5,4},{6,7},{7,6},{8,9},{9,8},{10,11... | collective-permute-start | bytes 3080 | tf_op jit(solution)/shard_map/ppermute | solution.py:399
  2.2 8.1 %collective-permute-start.1 = (f32[2,256]{1,0:T(2,128)S(1)}, f32[2,256]{1,0:T(2,128)S(1)}, u32[]{:S(2)}, u32[]{:S(2)}) collective-permute-start(f32[2,256]{1,0:T(2,128)S(1)} %pad_maximum_fusion.1), channel_id=1, source_target_pairs={{0,2},{1,3},{2,0},{3,1},{4,6},{5,7},{6,4},{7,5},{8,10},{9,11},{10,... | collective-permute-start | bytes 6152 | tf_op jit(solution)/shard_map/ppermute | solution.py:399
  5.2 5.2 %collective-permute-start.2 = (f32[2,256]{1,0:T(2,128)S(1)}, f32[2,256]{1,0:T(2,128)S(1)}, u32[]{:S(2)}, u32[]{:S(2)}) collective-permute-start(f32[2,256]{1,0:T(2,128)S(1)} %pad_maximum_fusion.1), channel_id=1, source_target_pairs={{0,4},{1,5},{2,6},{3,7},{4,0},{5,1},{6,2},{7,3},{8,12},{9,13},{10,... | collective-permute-start | bytes 6152 | tf_op jit(solution)/shard_map/ppermute | solution.py:399
  7.8 5.4 %collective-permute-start.3 = (f32[2,256]{1,0:T(2,128)S(1)}, f32[2,256]{1,0:T(2,128)S(1)}, u32[]{:S(2)}, u32[]{:S(2)}) collective-permute-start(f32[2,256]{1,0:T(2,128)S(1)} %pad_maximum_fusion.1), channel_id=1, source_target_pairs={{0,6},{1,7},{2,4},{3,5},{4,2},{5,3},{6,0},{7,1},{8,14},{9,15},{10,... | collective-permute-start | bytes 6152 | tf_op jit(solution)/shard_map/ppermute | solution.py:399
  20.3 1.6 %collective-permute-start.4 = (bf16[256,512]{1,0:T(8,128)(2,1)S(1)}, bf16[256,512]{1,0:T(8,128)(2,1)S(1)}, u32[]{:S(2)}, u32[]{:S(2)}) collective-permute-start(bf16[256,512]{1,0:T(8,128)(2,1)S(1)} %get-tuple-element.19), channel_id=1, source_target_pairs={{0,1},{1,0},{2,3},{3,2},{4,5},{5,4},{6,7},{7,6},{8,9},{9,8},{10,11... | collective-permute-start | bytes 786440 | tf_op jit(solution)/shard_map/ppermute | solution.py:399
  22.0 4.3 %collective-permute-start.5 = (bf16[64,512]{1,0:T(8,128)(2,1)S(1)}, bf16[64,512]{1,0:T(8,128)(2,1)S(1)}, u32[]{:S(2)}, u32[]{:S(2)}) collective-permute-start(bf16[64,512]{1,0:T(8,128)(2,1)S(1)} %get-tuple-element.26), channel_id=1, source_target_pairs={{0,8},{8,0},{16,24},{24,16},{1,9},{9,1},{17,25},{25,17},{2,10},{10... | collective-permute-start | bytes 196616 | tf_op jit(solution)/shard_map/ppermute | solution.py:399
  23.6 4.3 %collective-permute-start.6 = (bf16[64,512]{1,0:T(8,128)(2,1)S(1)}, bf16[64,512]{1,0:T(8,128)(2,1)S(1)}, u32[]{:S(2)}, u32[]{:S(2)}) collective-permute-start(bf16[64,512]{1,0:T(8,128)(2,1)S(1)} %get-tuple-element.28), channel_id=1, source_target_pairs={{0,16},{8,24},{16,0},{24,8},{1,17},{9,25},{17,1},{25,9},{2,18},{10... | collective-permute-start | bytes 196616 | tf_op jit(solution)/shard_map/ppermute | solution.py:399
  25.1 5.2 %collective-permute-start.7 = (bf16[64,512]{1,0:T(8,128)(2,1)S(1)}, bf16[64,512]{1,0:T(8,128)(2,1)S(1)}, u32[]{:S(2)}, u32[]{:S(2)}) collective-permute-start(bf16[64,512]{1,0:T(8,128)(2,1)S(1)} %get-tuple-element.27), channel_id=1, source_target_pairs={{0,24},{8,16},{16,8},{24,0},{1,25},{9,17},{17,9},{25,1},{2,26},{10... | collective-permute-start | bytes 196616 | tf_op jit(solution)/shard_map/ppermute | solution.py:399
  30.3 6.1 %collective-permute-start.10 = (bf16[64,512]{1,0:T(8,128)(2,1)S(1)}, bf16[64,512]{1,0:T(8,128)(2,1)S(1)}, u32[]{:S(2)}, u32[]{:S(2)}) collective-permute-start(bf16[64,512]{1,0:T(8,128)(2,1)S(1)} %fusion.1), channel_id=1, source_target_pairs={{0,6},{1,7},{2,4},{3,5},{4,2},{5,3},{6,0},{7,1},{8,14},{9,15},{10,... | collective-permute-start | bytes 196616 | tf_op jit(solution)/shard_map/ppermute | solution.py:399
  31.4 5.1 %collective-permute-start.8 = (bf16[64,512]{1,0:T(8,128)(2,1)S(1)}, bf16[64,512]{1,0:T(8,128)(2,1)S(1)}, u32[]{:S(2)}, u32[]{:S(2)}) collective-permute-start(bf16[64,512]{1,0:T(8,128)(2,1)S(1)} %fusion.1), channel_id=1, source_target_pairs={{0,2},{1,3},{2,0},{3,1},{4,6},{5,7},{6,4},{7,5},{8,10},{9,11},{10,... | collective-permute-start | bytes 196616 | tf_op jit(solution)/shard_map/ppermute | solution.py:399
  31.4 5.7 %collective-permute-start.9 = (bf16[64,512]{1,0:T(8,128)(2,1)S(1)}, bf16[64,512]{1,0:T(8,128)(2,1)S(1)}, u32[]{:S(2)}, u32[]{:S(2)}) collective-permute-start(bf16[64,512]{1,0:T(8,128)(2,1)S(1)} %fusion.1), channel_id=1, source_target_pairs={{0,4},{1,5},{2,6},{3,7},{4,0},{5,1},{6,2},{7,3},{8,12},{9,13},{10,... | collective-permute-start | bytes 196616 | tf_op jit(solution)/shard_map/ppermute | solution.py:399
  37.2 4.3 %collective-permute-start.11 = (bf16[64,512]{1,0:T(8,128)(2,1)S(1)}, bf16[64,512]{1,0:T(8,128)(2,1)S(1)}, u32[]{:S(2)}, u32[]{:S(2)}) collective-permute-start(bf16[64,512]{1,0:T(8,128)(2,1)S(1)} %add_convert_fusion.1), channel_id=1, source_target_pairs={{0,8},{8,0},{16,24},{24,16},{1,9},{9,1},{17,25},{25,17},{2,10},{10... | collective-permute-start | bytes 196616 | tf_op jit(solution)/shard_map/ppermute | solution.py:399
  37.8 4.3 %collective-permute-start.12 = (bf16[64,512]{1,0:T(8,128)(2,1)S(1)}, bf16[64,512]{1,0:T(8,128)(2,1)S(1)}, u32[]{:S(2)}, u32[]{:S(2)}) collective-permute-start(bf16[64,512]{1,0:T(8,128)(2,1)S(1)} %add_convert_fusion.1), channel_id=1, source_target_pairs={{0,16},{8,24},{16,0},{24,8},{1,17},{9,25},{17,1},{25,9},{2,18},{10... | collective-permute-start | bytes 196616 | tf_op jit(solution)/shard_map/ppermute | solution.py:399
  38.3 5.2 %collective-permute-start.13 = (bf16[64,512]{1,0:T(8,128)(2,1)S(1)}, bf16[64,512]{1,0:T(8,128)(2,1)S(1)}, u32[]{:S(2)}, u32[]{:S(2)}) collective-permute-start(bf16[64,512]{1,0:T(8,128)(2,1)S(1)} %add_convert_fusion.1), channel_id=1, source_target_pairs={{0,24},{8,16},{16,8},{24,0},{1,25},{9,17},{17,9},{25,1},{2,26},{10... | collective-permute-start | bytes 196616 | tf_op jit(solution)/shard_map/ppermute | solution.py:399
  43.5 1.6 %collective-permute-start.14 = (bf16[256,512]{1,0:T(8,128)(2,1)S(1)}, bf16[256,512]{1,0:T(8,128)(2,1)S(1)}, u32[]{:S(2)}, u32[]{:S(2)}) collective-permute-start(bf16[256,512]{1,0:T(8,128)(2,1)S(1)} %bitcast.28), channel_id=1, source_target_pairs={{0,1},{1,0},{2,3},{3,2},{4,5},{5,4},{6,7},{7,6},{8,9},{9,8},{10,11... | collective-permute-start | bytes 786440 | tf_op jit(solution)/shard_map/ppermute | solution.py:399

commit v4 on v3

--- a/solution.py
+++ b/solution.py
@@ -44,8 +44,9 @@
 
 
 def tables_kernel(*refs):
-    count = 10
-    sources, outs, buffers, sem = refs[:count], refs[count:-count - 1], refs[-count - 1 : -1], refs[-1]
+    count = 13
+    sources, outs, buffers = refs[:count], refs[count : count + 7], refs[count + 7 : 2 * count + 7]
+    pos_s, rep_s, sem = refs[2 * count + 7 :]
     copies = [
         pltpu.make_async_copy(source, buffer, sem.at[i])
         for i, (source, buffer) in enumerate(zip(sources, buffers))
@@ -54,8 +55,29 @@
         copy.start()
     for copy in copies:
         copy.wait()
-    emb_ref, scale_ref, win_ref, inc_ref, cw_ref, cb_ref, dtb_ref, rate_ref, gain_ref, head_ref = buffers
-    conv_out, gate_out, step_out, decay_out, gain_out, head_out = outs
+    (
+        emb_ref, scale_ref, win_ref, inc_ref, cw_ref, cb_ref, dtb_ref, rate_ref, gain_ref, head_ref,
+        tok_ref, pos_ref, rep_ref,
+    ) = buffers
+    conv_out, gate_out, step_out, decay_out, gain_out, head_out, val_out = outs
+
+    masks, wide, blocks = pos_ref.shape[1], pos_s.shape[1], val_out.shape[0]
+    pos_s[...] = jnp.full_like(pos_s, -1)
+    rep_s[...] = jnp.zeros_like(rep_s)
+    pos_s[:, :masks] = pos_ref[...]
+    rep_s[:, :masks] = rep_ref[...]
+    pos = pos_s[...]
+    block_hit = lax.broadcasted_iota(jnp.int32, (blocks, wide), 0) == (pos >> 7)
+    put = jnp.where(block_hit, (rep_s[...] + 1).astype(F32), 0.0).astype(BF16)
+    lane_hit = (lax.broadcasted_iota(jnp.int32, (SPAN, wide), 0) == (pos & 127)) & (pos >= 0)
+    val_out[...] = mm(put, lane_hit.astype(F32).astype(BF16), NT)
+    length = tok_ref.shape[1]
+    nb = length // SPAN
+    first = lax.axis_index("seq") * nb
+    val = jnp.concatenate([val_out[pl.ds(first + b, 1), :] for b in range(nb)], axis=1)
+    ids = jnp.where(val > 0.5, val - 1.0, tok_ref[...].astype(F32))
+    hot = (lax.broadcasted_iota(jnp.int32, (8, length), 0).astype(F32) == ids).astype(F32)
+    hot = jnp.concatenate([hot, hot], axis=0).astype(BF16)
     emb = emb_ref[...].astype(F32)
     none = jnp.zeros((2, emb.shape[1]), F32)
     rows = jnp.concatenate(
@@ -72,7 +94,7 @@
     mixed = projected[:, INNER:]
     for strand in range(2):
         high, low = split_two(gate_t[:, strand * 8 : strand * 8 + 8])
-        gate_out[strand * INNER : (strand + 1) * INNER, :] = jnp.concatenate([high, low], axis=1)
+        gate_out[strand * INNER : (strand + 1) * INNER, :] = mm(jnp.concatenate([high, low], axis=1), hot)
     for side in range(2):
         for strand in range(2):
             param = side ^ strand
@@ -105,15 +127,12 @@
 
 def layer_kernel(
     n, length, masked_total,
-    tok_ref, pos_ref, rep_ref, conv_ref, gate_ref, step_ref, decay_ref, gain_ref, headt_ref, wout_ref,
+    tok_ref, conv_ref, gate_ref, step_ref, decay_ref, gain_ref, headt_ref, val_s, wout_ref,
     layer_out, send_out, keep_out,
-    pos_s, rep_s, ids_s, val_s, step_s, log_s, cum_s, tot_s, own_s, from_s, near_s, far_s, farb_s, state_s, y_s, comb_s,
+    ids_s, step_s, log_s, cum_s, tot_s, own_s, from_s, near_s, far_s, farb_s, state_s, y_s, comb_s,
 ):
     me = lax.axis_index("seq")
     nb = length // SPAN
-    blocks = n * nb
-    masks = pos_ref.shape[1]
-    wide = pos_s.shape[1]
     unrolled = n <= 16
     rows = 2 * nb * 8
 
@@ -124,15 +143,6 @@
         else:
             pl.loop(0, count)(body)
 
-    pos_s[...] = jnp.full_like(pos_s, -1)
-    rep_s[...] = jnp.zeros_like(rep_s)
-    pos_s[:, :masks] = pos_ref[...]
-    rep_s[:, :masks] = rep_ref[...]
-    pos = pos_s[...]
-    block_hit = lax.broadcasted_iota(jnp.int32, (blocks, wide), 0) == (pos >> 7)
-    put = jnp.where(block_hit, (rep_s[...] + 1).astype(F32), 0.0).astype(BF16)
-    lane_hit = (lax.broadcasted_iota(jnp.int32, (SPAN, wide), 0) == (pos & 127)) & (pos >= 0)
-    val_s[...] = mm(put, lane_hit.astype(F32).astype(BF16), NT)
     nothing = jnp.full((1, length), -1.0, F32)
     ids_s[0:1, :] = nothing
     ids_s[n + 1 : n + 2, :] = nothing
@@ -254,10 +264,10 @@
             row8 = across(weight, strand)
             base = strand * CONVW
             for c in range(4):
-                half = mm(conv_ref[side, base + c * 128 : base + (c + 1) * 128, :], hot)
+                half = mm(conv_ref[side, base + c * 128 : base + (c + 1) * 128, :], hot).astype(BF16)
                 far_s[strand, c * 128 : (c + 1) * 128, at] = per_head(
-                    silu_half(half), row8, 2 * c
-                ).astype(BF16)
+                    silu_half(half), row8.astype(BF16), 2 * c
+                )
             b_t = silu_half(mm(conv_ref[side, base + INNER : base + INNER + STATE, :], hot))
             farb_s[strand, :STATE, at] = jnp.where(side == 0, b_t, 0.0).astype(BF16)
             farb_s[strand, STATE:, at] = jnp.where(side == 0, 0.0, b_t).astype(BF16)
@@ -348,8 +358,6 @@
                         y = y + near_s[strand, side, hs, at] * here[h : h + 1]
                 y_s[strand, hs, at] = y
 
-    hot0 = (sub8 == ids_s[pl.ds(me + 1, 1), :]).astype(F32)
-    hot0 = jnp.concatenate([hot0, hot0], axis=0).astype(BF16)
     for h in range(HEADS):
         hs = slice(h * HEADDIM, (h + 1) * HEADDIM)
         gain = gain_ref[hs, :]
@@ -357,7 +365,7 @@
         total = None
         for strand in range(2):
             at = strand * INNER + h * HEADDIM
-            g = y_s[strand, hs, :] * mm(gate_ref[at : at + HEADDIM, :], hot0)
+            g = y_s[strand, hs, :] * gate_ref[at : at + HEADDIM, :]
             mean_sq = jnp.mean(g * g, axis=0, keepdims=True)
             out = (g * lax.rsqrt(mean_sq + EPSILON) * gain).astype(BF16).astype(F32)
             total = out if total is None else total + out
@@ -462,29 +470,32 @@
     weights = (
         token_embedding_matrix, entry_scale_vector[None], input_projection_weight,
         increment_coefficients.T, conv_w, conv_b, dt_bias, decay_rate, gain_out[None], w_head.T,
+        tokens, mask_pos, replace_ids,
     )
+    masks = mask_pos.shape[1]
+    wide = -(-masks // 128) * 128
     tables = pl.pallas_call(
         tables_kernel,
         in_specs=[pl.BlockSpec(memory_space=pltpu.HBM)] * len(weights),
         scratch_shapes=[pltpu.VMEM(w.shape, w.dtype) for w in weights]
+        + [pltpu.VMEM((1, wide), jnp.int32)] * 2
         + [pltpu.SemaphoreType.DMA((len(weights),))],
         out_shape=(
             pltpu.VMEM((2, 2 * CONVW, 16 * KW), BF16),
-            pltpu.VMEM((2 * INNER, 16), BF16),
+            pltpu.VMEM((2 * INNER, length), F32),
             pltpu.VMEM((2, 2, HEADS, 8), F32),
             pltpu.VMEM((2, 2, HEADS, 8), F32),
             pltpu.VMEM((INNER, 128), F32),
             pltpu.VMEM((8, width), BF16),
+            pltpu.VMEM((n * nb, SPAN), F32),
         ),
         compiler_params=pltpu.CompilerParams(vmem_limit_bytes=32 << 20),
         cost_estimate=pl.CostEstimate(flops=20_000_000, bytes_accessed=3_000_000, transcendentals=10_000),
         name="tables",
     )(*[pltpu.with_memory_space_constraint(w, pltpu.HBM) for w in weights])
-    masks = mask_pos.shape[1]
-    wide = -(-masks // 128) * 128
     slots = n + 1
     spots = n - 1 if n <= 16 else 1
-    operands = (gathered, mask_pos, replace_ids, *tables, w_out)
+    operands = (gathered, *tables, w_out)
     layer_out, send, keep = pl.pallas_call(
         functools.partial(layer_kernel, n, length, lax.axis_size("dp") * masks),
         out_shape=(
@@ -493,10 +504,7 @@
             pltpu.VMEM((INNER // 2, width), BF16),
         ),
         scratch_shapes=[
-            pltpu.VMEM((1, wide), jnp.int32),
-            pltpu.VMEM((1, wide), jnp.int32),
             pltpu.VMEM((n + 2, length), F32),
-            pltpu.VMEM((n * nb, SPAN), F32),
             pltpu.VMEM((slots, rows, SPAN), F32),
             pltpu.VMEM((slots, rows, SPAN), F32),
             pltpu.VMEM((slots, rows, SPAN), F32),

time: 46.5 us -> 46.1 us (level)
  no operation moved by 1% of the time
where the time goes in v4:
time: 46.1 us; the launch traced here: 45.9 us
  starting transfers between devices  17.8 us (39%)
  waiting for transfers between devices  15.9 us (34%)
  Pallas kernels  9.36 us (20%)
  other arithmetic  2.06 us (4%)
  between operations  0.77 us (2%)
    ppermute x15, starting transfers between devices, swap(): lax.ppermute(value, axis, [(i, i ^ k) for i in range(lax.axis_size(axis))])  17.8 us
    ppermute x15, waiting for transfers between devices, swap(): lax.ppermute(value, axis, [(i, i ^ k) for i in range(lax.axis_size(axis))])  15.9 us
    pallas_call x1, Pallas kernels, per_device(): pl.pallas_call(functools.partial(layer_kernel, n, length, lax.axis_size('...  6.68 us
    pallas_call x1, Pallas kernels, per_device(): pl.pallas_call(tables_kernel, in_specs=[pl.BlockSpec(memory_space=pltpu.H...  2.68 us
    convert_element_type x1, other arithmetic, sum_all(): return jnp.concatenate([low, high], axis=0).astype(F32)  1.1 us
  transfers between devices with their start and end apart: 15, of which 12 were waited for; matrix products, arithmetic and copies ran while one was open for 1% of the time, Pallas kernels for 6%

profile of v4, /device:TPU:0, one launch (start us, length us, event | category | flops | bytes accessed | tf_op | source)
XLA Modules:
  0.0 45.9 jit_solution(9255672413185030055)
XLA Ops:
  0.6 0.0 copy-start
  0.6 0.5 %collective-permute-start = (s32[1,256]{1,0:T(1,128)}, s32[1,256]{1,0:T(1,128)S(1)}, u32[]{:S(2)}, u32[]{:S(2)}) collective-permute-start(s32[1,256]{1,0:T(1,128)} %refs_10_.1), channel_id=1, source_target_pairs={{0,1},{1,0},{2,3},{3,2},{4,5},{5,4},{6,7},{7,6},{8,9},{9,8},{10,11... | collective-permute-start | bytes 3080 | tf_op jit(solution)/shard_map/ppermute | solution.py:407
  1.2 0.7 %convert_element_type.51 = f32[1,256]{1,0:T(1,128)S(1)} convert(s32[1,256]{1,0:T(1,128)} %refs_10_.1) | non-fusion elementwise | flops 256 | bytes 2048 | tf_op jit(solution)/shard_map/convert_element_type | solution.py:463
  1.8 0.3 collective-permute-done
  2.2 3.0 %collective-permute-start.1 = (f32[2,256]{1,0:T(2,128)S(1)}, f32[2,256]{1,0:T(2,128)S(1)}, u32[]{:S(2)}, u32[]{:S(2)}) collective-permute-start(f32[2,256]{1,0:T(2,128)S(1)} %pad_maximum_fusion.1), channel_id=1, source_target_pairs={{0,2},{1,3},{2,0},{3,1},{4,6},{5,7},{6,4},{7,5},{8,10},{9,11},{10,... | collective-permute-start | bytes 6152 | tf_op jit(solution)/shard_map/ppermute | solution.py:407
  5.2 2.6 %collective-permute-start.2 = (f32[2,256]{1,0:T(2,128)S(1)}, f32[2,256]{1,0:T(2,128)S(1)}, u32[]{:S(2)}, u32[]{:S(2)}) collective-permute-start(f32[2,256]{1,0:T(2,128)S(1)} %pad_maximum_fusion.1), channel_id=1, source_target_pairs={{0,4},{1,5},{2,6},{3,7},{4,0},{5,1},{6,2},{7,3},{8,12},{9,13},{10,... | collective-permute-start | bytes 6152 | tf_op jit(solution)/shard_map/ppermute | solution.py:407
  7.7 0.0 collective-permute-start.3
  7.7 2.7 %tables.1 = (bf16[2,1280,64]{2,1,0:T(8,128)(2,1)S(1)}, f32[1024,256]{1,0:T(8,128)S(1)}, f32[2,2,8,8]{3,2,1,0:T(8,128)S(1)}, f32[2,2,8,8]{3,2,1,0:T(8,128)S(1)}, ...) custom-call(bf16[6,512]{1,0:T(8,128)(2,1)} %refs_0_.1, f32[1,512]{1,0:T(1,128)} %bitcast.31, ...), custom_call_target="tpu_custom_call" | custom-call | flops 20000000 | bytes 3000000 | tf_op jit(solution)/shard_map/tables/pallas_call | solution.py:477
  10.4 0.0 collective-permute-done.1
  10.5 0.0 collective-permute-done.2
  10.5 2.7 %collective-permute-done.3 = f32[2,256]{1,0:T(2,128)S(1)} collective-permute-done((f32[2,256]{1,0:T(2,128)S(1)}, f32[2,256]{1,0:T(2,128)S(1)}, u32[]{:S(2)}, u32[]{:S(2)}) %collective-permute-start.3) | collective-permute-done | bytes 2080 | tf_op jit(solution)/shard_map/ppermute | solution.py:407
  13.2 0.0 copy-done
  13.2 6.7 %layer.1 = (bf16[256,512]{1,0:T(8,128)(2,1)}, bf16[256,512]{1,0:T(8,128)(2,1)S(1)}, bf16[256,512]{1,0:T(8,128)(2,1)S(1)}) custom-call(f32[8,256]{1,0:T(8,128)S(1)} %concatenate.11.tok_ref, bf16[2,1280,64]{2,1,0:T(8,128)(2,1)S(1)} %get-tuple-element.12.conv_ref, f32[1024,256]{1,0:T(8,128)S(1)} %get-tuple-element.13.gate_ref, ...), custom_call_target="tpu_custom_call" | custom-call | flops 2000000000 | bytes 4000000 | tf_op jit(solution)/shard_map/layer/pallas_call | solution.py:499
  19.8 0.1 collective-permute-start.4
  19.9 1.5 %collective-permute-done.4 = bf16[256,512]{1,0:T(8,128)(2,1)S(1)} collective-permute-done((bf16[256,512]{1,0:T(8,128)(2,1)S(1)}, bf16[256,512]{1,0:T(8,128)(2,1)S(1)}, u32[]{:S(2)}, u32[]{:S(2)}) %collective-permute-start.4) | collective-permute-done | bytes 262176 | tf_op jit(solution)/shard_map/ppermute | solution.py:407
  21.4 0.1 add_convert_fusion
  21.5 1.6 %collective-permute-start.5 = (bf16[64,512]{1,0:T(8,128)(2,1)S(1)}, bf16[64,512]{1,0:T(8,128)(2,1)S(1)}, u32[]{:S(2)}, u32[]{:S(2)}) collective-permute-start(bf16[64,512]{1,0:T(8,128)(2,1)S(1)} %get-tuple-element.28), channel_id=1, source_target_pairs={{0,8},{8,0},{16,24},{24,16},{1,9},{9,1},{17,25},{25,17},{2,10},{10... | collective-permute-start | bytes 196616 | tf_op jit(solution)/shard_map/ppermute | solution.py:407
  23.1 1.5 %collective-permute-start.6 = (bf16[64,512]{1,0:T(8,128)(2,1)S(1)}, bf16[64,512]{1,0:T(8,128)(2,1)S(1)}, u32[]{:S(2)}, u32[]{:S(2)}) collective-permute-start(bf16[64,512]{1,0:T(8,128)(2,1)S(1)} %get-tuple-element.30), channel_id=1, source_target_pairs={{0,16},{8,24},{16,0},{24,8},{1,17},{9,25},{17,1},{25,9},{2,18},{10... | collective-permute-start | bytes 196616 | tf_op jit(solution)/shard_map/ppermute | solution.py:407
  24.6 0.5 %collective-permute-start.7 = (bf16[64,512]{1,0:T(8,128)(2,1)S(1)}, bf16[64,512]{1,0:T(8,128)(2,1)S(1)}, u32[]{:S(2)}, u32[]{:S(2)}) collective-permute-start(bf16[64,512]{1,0:T(8,128)(2,1)S(1)} %get-tuple-element.29), channel_id=1, source_target_pairs={{0,24},{8,16},{16,8},{24,0},{1,25},{9,17},{17,9},{25,1},{2,26},{10... | collective-permute-start | bytes 196616 | tf_op jit(solution)/shard_map/ppermute | solution.py:407
  25.1 0.8 %collective-permute-done.5 = bf16[64,512]{1,0:T(8,128)(2,1)S(1)} collective-permute-done((bf16[64,512]{1,0:T(8,128)(2,1)S(1)}, bf16[64,512]{1,0:T(8,128)(2,1)S(1)}, u32[]{:S(2)}, u32[]{:S(2)}) %collective-permute-start.5) | collective-permute-done | bytes 65568 | tf_op jit(solution)/shard_map/ppermute | solution.py:407
  25.9 1.5 %collective-permute-done.6 = bf16[64,512]{1,0:T(8,128)(2,1)S(1)} collective-permute-done((bf16[64,512]{1,0:T(8,128)(2,1)S(1)}, bf16[64,512]{1,0:T(8,128)(2,1)S(1)}, u32[]{:S(2)}, u32[]{:S(2)}) %collective-permute-start.6) | collective-permute-done | bytes 65568 | tf_op jit(solution)/shard_map/ppermute | solution.py:407
  27.4 2.4 %collective-permute-done.7 = bf16[64,512]{1,0:T(8,128)(2,1)S(1)} collective-permute-done((bf16[64,512]{1,0:T(8,128)(2,1)S(1)}, bf16[64,512]{1,0:T(8,128)(2,1)S(1)}, u32[]{:S(2)}, u32[]{:S(2)}) %collective-permute-start.7) | collective-permute-done | bytes 65568 | tf_op jit(solution)/shard_map/ppermute | solution.py:407
  29.8 1.2 %collective-permute-start.10 = (bf16[64,512]{1,0:T(8,128)(2,1)S(1)}, bf16[64,512]{1,0:T(8,128)(2,1)S(1)}, u32[]{:S(2)}, u32[]{:S(2)}) collective-permute-start(bf16[64,512]{1,0:T(8,128)(2,1)S(1)} %fusion.1), channel_id=1, source_target_pairs={{0,6},{1,7},{2,4},{3,5},{4,2},{5,3},{6,0},{7,1},{8,14},{9,15},{10,... | collective-permute-start | bytes 196616 | tf_op jit(solution)/shard_map/ppermute | solution.py:407
  31.1 0.0 collective-permute-start.8
  31.1 3.2 %collective-permute-start.9 = (bf16[64,512]{1,0:T(8,128)(2,1)S(1)}, bf16[64,512]{1,0:T(8,128)(2,1)S(1)}, u32[]{:S(2)}, u32[]{:S(2)}) collective-permute-start(bf16[64,512]{1,0:T(8,128)(2,1)S(1)} %fusion.1), channel_id=1, source_target_pairs={{0,4},{1,5},{2,6},{3,7},{4,0},{5,1},{6,2},{7,3},{8,12},{9,13},{10,... | collective-permute-start | bytes 196616 | tf_op jit(solution)/shard_map/ppermute | solution.py:407
  34.3 1.8 %collective-permute-done.10 = bf16[64,512]{1,0:T(8,128)(2,1)S(1)} collective-permute-done((bf16[64,512]{1,0:T(8,128)(2,1)S(1)}, bf16[64,512]{1,0:T(8,128)(2,1)S(1)}, u32[]{:S(2)}, u32[]{:S(2)}) %collective-permute-start.10) | collective-permute-done | bytes 65568 | tf_op jit(solution)/shard_map/ppermute | solution.py:407
  36.0 0.0 collective-permute-done.8
  36.0 0.7 %collective-permute-done.9 = bf16[64,512]{1,0:T(8,128)(2,1)S(1)} collective-permute-done((bf16[64,512]{1,0:T(8,128)(2,1)S(1)}, bf16[64,512]{1,0:T(8,128)(2,1)S(1)}, u32[]{:S(2)}, u32[]{:S(2)}) %collective-permute-start.9) | collective-permute-done | bytes 65568 | tf_op jit(solution)/shard_map/ppermute | solution.py:407
  36.8 0.6 %collective-permute-start.11 = (bf16[64,512]{1,0:T(8,128)(2,1)S(1)}, bf16[64,512]{1,0:T(8,128)(2,1)S(1)}, u32[]{:S(2)}, u32[]{:S(2)}) collective-permute-start(bf16[64,512]{1,0:T(8,128)(2,1)S(1)} %add_convert_fusion.1), channel_id=1, source_target_pairs={{0,8},{8,0},{16,24},{24,16},{1,9},{9,1},{17,25},{25,17},{2,10},{10... | collective-permute-start | bytes 196616 | tf_op jit(solution)/shard_map/ppermute | solution.py:407
  37.4 0.5 %collective-permute-start.12 = (bf16[64,512]{1,0:T(8,128)(2,1)S(1)}, bf16[64,512]{1,0:T(8,128)(2,1)S(1)}, u32[]{:S(2)}, u32[]{:S(2)}) collective-permute-start(bf16[64,512]{1,0:T(8,128)(2,1)S(1)} %add_convert_fusion.1), channel_id=1, source_target_pairs={{0,16},{8,24},{16,0},{24,8},{1,17},{9,25},{17,1},{25,9},{2,18},{10... | collective-permute-start | bytes 196616 | tf_op jit(solution)/shard_map/ppermute | solution.py:407
  37.9 2.4 %collective-permute-start.13 = (bf16[64,512]{1,0:T(8,128)(2,1)S(1)}, bf16[64,512]{1,0:T(8,128)(2,1)S(1)}, u32[]{:S(2)}, u32[]{:S(2)}) collective-permute-start(bf16[64,512]{1,0:T(8,128)(2,1)S(1)} %add_convert_fusion.1), channel_id=1, source_target_pairs={{0,24},{8,16},{16,8},{24,0},{1,25},{9,17},{17,9},{25,1},{2,26},{10... | collective-permute-start | bytes 196616 | tf_op jit(solution)/shard_map/ppermute | solution.py:407
  40.3 0.8 %collective-permute-done.11 = bf16[64,512]{1,0:T(8,128)(2,1)S(1)} collective-permute-done((bf16[64,512]{1,0:T(8,128)(2,1)S(1)}, bf16[64,512]{1,0:T(8,128)(2,1)S(1)}, u32[]{:S(2)}, u32[]{:S(2)}) %collective-permute-start.11) | collective-permute-done | bytes 65568 | tf_op jit(solution)/shard_map/ppermute | solution.py:407
  41.1 0.5 %collective-permute-done.12 = bf16[64,512]{1,0:T(8,128)(2,1)S(1)} collective-permute-done((bf16[64,512]{1,0:T(8,128)(2,1)S(1)}, bf16[64,512]{1,0:T(8,128)(2,1)S(1)}, u32[]{:S(2)}, u32[]{:S(2)}) %collective-permute-start.12) | collective-permute-done | bytes 65568 | tf_op jit(solution)/shard_map/ppermute | solution.py:407
  41.6 1.4 %collective-permute-done.13 = bf16[64,512]{1,0:T(8,128)(2,1)S(1)} collective-permute-done((bf16[64,512]{1,0:T(8,128)(2,1)S(1)}, bf16[64,512]{1,0:T(8,128)(2,1)S(1)}, u32[]{:S(2)}, u32[]{:S(2)}) %collective-permute-start.13) | collective-permute-done | bytes 65568 | tf_op jit(solution)/shard_map/ppermute | solution.py:407
  43.1 0.1 collective-permute-start.14
  43.2 1.5 %collective-permute-done.14 = bf16[256,512]{1,0:T(8,128)(2,1)S(1)} collective-permute-done((bf16[256,512]{1,0:T(8,128)(2,1)S(1)}, bf16[256,512]{1,0:T(8,128)(2,1)S(1)}, u32[]{:S(2)}, u32[]{:S(2)}) %collective-permute-start.14) | collective-permute-done | bytes 262176 | tf_op jit(solution)/shard_map/ppermute | solution.py:407
  44.7 0.1 broadcast_select_fusion.1
  44.8 1.1 %maximum_convert_fusion = f32[512,512]{1,0:T(8,128)} fusion(bf16[256,512]{1,0:T(8,128)(2,1)S(1)} %get-tuple-element.23, bf16[256,512]{1,0:T(8,128)(2,1)S(1)} %get-tuple-element.22), kind=kLoop, calls=%fused_computation | loop fusion | flops 1048576 | bytes 1572864 | tf_op jit(solution)/shard_map/convert_element_type | solution.py:450
  (8 shorter events, 0.2 us)
Async XLA Ops:
  0.6 12.5 %copy-start = (bf16[512,512]{1,0:T(8,128)(2,1)S(1)}, bf16[512,512]{1,0:T(8,128)(2,1)}, u32[]{:S(2)}) copy-start(bf16[512,512]{1,0:T(8,128)(2,1)} %wout_ref.1) | copy-start | bytes 1572868
  0.6 1.5 %collective-permute-start = (s32[1,256]{1,0:T(1,128)}, s32[1,256]{1,0:T(1,128)S(1)}, u32[]{:S(2)}, u32[]{:S(2)}) collective-permute-start(s32[1,256]{1,0:T(1,128)} %refs_10_.1), channel_id=1, source_target_pairs={{0,1},{1,0},{2,3},{3,2},{4,5},{5,4},{6,7},{7,6},{8,9},{9,8},{10,11... | collective-permute-start | bytes 3080 | tf_op jit(solution)/shard_map/ppermute | solution.py:407
  2.2 8.2 %collective-permute-start.1 = (f32[2,256]{1,0:T(2,128)S(1)}, f32[2,256]{1,0:T(2,128)S(1)}, u32[]{:S(2)}, u32[]{:S(2)}) collective-permute-start(f32[2,256]{1,0:T(2,128)S(1)} %pad_maximum_fusion.1), channel_id=1, source_target_pairs={{0,2},{1,3},{2,0},{3,1},{4,6},{5,7},{6,4},{7,5},{8,10},{9,11},{10,... | collective-permute-start | bytes 6152 | tf_op jit(solution)/shard_map/ppermute | solution.py:407
  5.2 5.3 %collective-permute-start.2 = (f32[2,256]{1,0:T(2,128)S(1)}, f32[2,256]{1,0:T(2,128)S(1)}, u32[]{:S(2)}, u32[]{:S(2)}) collective-permute-start(f32[2,256]{1,0:T(2,128)S(1)} %pad_maximum_fusion.1), channel_id=1, source_target_pairs={{0,4},{1,5},{2,6},{3,7},{4,0},{5,1},{6,2},{7,3},{8,12},{9,13},{10,... | collective-permute-start | bytes 6152 | tf_op jit(solution)/shard_map/ppermute | solution.py:407
  7.7 5.4 %collective-permute-start.3 = (f32[2,256]{1,0:T(2,128)S(1)}, f32[2,256]{1,0:T(2,128)S(1)}, u32[]{:S(2)}, u32[]{:S(2)}) collective-permute-start(f32[2,256]{1,0:T(2,128)S(1)} %pad_maximum_fusion.1), channel_id=1, source_target_pairs={{0,6},{1,7},{2,4},{3,5},{4,2},{5,3},{6,0},{7,1},{8,14},{9,15},{10,... | collective-permute-start | bytes 6152 | tf_op jit(solution)/shard_map/ppermute | solution.py:407
  19.8 1.6 %collective-permute-start.4 = (bf16[256,512]{1,0:T(8,128)(2,1)S(1)}, bf16[256,512]{1,0:T(8,128)(2,1)S(1)}, u32[]{:S(2)}, u32[]{:S(2)}) collective-permute-start(bf16[256,512]{1,0:T(8,128)(2,1)S(1)} %get-tuple-element.21), channel_id=1, source_target_pairs={{0,1},{1,0},{2,3},{3,2},{4,5},{5,4},{6,7},{7,6},{8,9},{9,8},{10,11... | collective-permute-start | bytes 786440 | tf_op jit(solution)/shard_map/ppermute | solution.py:407
  21.5 4.3 %collective-permute-start.5 = (bf16[64,512]{1,0:T(8,128)(2,1)S(1)}, bf16[64,512]{1,0:T(8,128)(2,1)S(1)}, u32[]{:S(2)}, u32[]{:S(2)}) collective-permute-start(bf16[64,512]{1,0:T(8,128)(2,1)S(1)} %get-tuple-element.28), channel_id=1, source_target_pairs={{0,8},{8,0},{16,24},{24,16},{1,9},{9,1},{17,25},{25,17},{2,10},{10... | collective-permute-start | bytes 196616 | tf_op jit(solution)/shard_map/ppermute | solution.py:407
  23.1 4.3 %collective-permute-start.6 = (bf16[64,512]{1,0:T(8,128)(2,1)S(1)}, bf16[64,512]{1,0:T(8,128)(2,1)S(1)}, u32[]{:S(2)}, u32[]{:S(2)}) collective-permute-start(bf16[64,512]{1,0:T(8,128)(2,1)S(1)} %get-tuple-element.30), channel_id=1, source_target_pairs={{0,16},{8,24},{16,0},{24,8},{1,17},{9,25},{17,1},{25,9},{2,18},{10... | collective-permute-start | bytes 196616 | tf_op jit(solution)/shard_map/ppermute | solution.py:407
  24.6 5.2 %collective-permute-start.7 = (bf16[64,512]{1,0:T(8,128)(2,1)S(1)}, bf16[64,512]{1,0:T(8,128)(2,1)S(1)}, u32[]{:S(2)}, u32[]{:S(2)}) collective-permute-start(bf16[64,512]{1,0:T(8,128)(2,1)S(1)} %get-tuple-element.29), channel_id=1, source_target_pairs={{0,24},{8,16},{16,8},{24,0},{1,25},{9,17},{17,9},{25,1},{2,26},{10... | collective-permute-start | bytes 196616 | tf_op jit(solution)/shard_map/ppermute | solution.py:407
  29.8 6.2 %collective-permute-start.10 = (bf16[64,512]{1,0:T(8,128)(2,1)S(1)}, bf16[64,512]{1,0:T(8,128)(2,1)S(1)}, u32[]{:S(2)}, u32[]{:S(2)}) collective-permute-start(bf16[64,512]{1,0:T(8,128)(2,1)S(1)} %fusion.1), channel_id=1, source_target_pairs={{0,6},{1,7},{2,4},{3,5},{4,2},{5,3},{6,0},{7,1},{8,14},{9,15},{10,... | collective-permute-start | bytes 196616 | tf_op jit(solution)/shard_map/ppermute | solution.py:407
  31.1 5.0 %collective-permute-start.8 = (bf16[64,512]{1,0:T(8,128)(2,1)S(1)}, bf16[64,512]{1,0:T(8,128)(2,1)S(1)}, u32[]{:S(2)}, u32[]{:S(2)}) collective-permute-start(bf16[64,512]{1,0:T(8,128)(2,1)S(1)} %fusion.1), channel_id=1, source_target_pairs={{0,2},{1,3},{2,0},{3,1},{4,6},{5,7},{6,4},{7,5},{8,10},{9,11},{10,... | collective-permute-start | bytes 196616 | tf_op jit(solution)/shard_map/ppermute | solution.py:407
  31.1 5.7 %collective-permute-start.9 = (bf16[64,512]{1,0:T(8,128)(2,1)S(1)}, bf16[64,512]{1,0:T(8,128)(2,1)S(1)}, u32[]{:S(2)}, u32[]{:S(2)}) collective-permute-start(bf16[64,512]{1,0:T(8,128)(2,1)S(1)} %fusion.1), channel_id=1, source_target_pairs={{0,4},{1,5},{2,6},{3,7},{4,0},{5,1},{6,2},{7,3},{8,12},{9,13},{10,... | collective-permute-start | bytes 196616 | tf_op jit(solution)/shard_map/ppermute | solution.py:407
  36.8 4.3 %collective-permute-start.11 = (bf16[64,512]{1,0:T(8,128)(2,1)S(1)}, bf16[64,512]{1,0:T(8,128)(2,1)S(1)}, u32[]{:S(2)}, u32[]{:S(2)}) collective-permute-start(bf16[64,512]{1,0:T(8,128)(2,1)S(1)} %add_convert_fusion.1), channel_id=1, source_target_pairs={{0,8},{8,0},{16,24},{24,16},{1,9},{9,1},{17,25},{25,17},{2,10},{10... | collective-permute-start | bytes 196616 | tf_op jit(solution)/shard_map/ppermute | solution.py:407
  37.4 4.3 %collective-permute-start.12 = (bf16[64,512]{1,0:T(8,128)(2,1)S(1)}, bf16[64,512]{1,0:T(8,128)(2,1)S(1)}, u32[]{:S(2)}, u32[]{:S(2)}) collective-permute-start(bf16[64,512]{1,0:T(8,128)(2,1)S(1)} %add_convert_fusion.1), channel_id=1, source_target_pairs={{0,16},{8,24},{16,0},{24,8},{1,17},{9,25},{17,1},{25,9},{2,18},{10... | collective-permute-start | bytes 196616 | tf_op jit(solution)/shard_map/ppermute | solution.py:407
  37.9 5.2 %collective-permute-start.13 = (bf16[64,512]{1,0:T(8,128)(2,1)S(1)}, bf16[64,512]{1,0:T(8,128)(2,1)S(1)}, u32[]{:S(2)}, u32[]{:S(2)}) collective-permute-start(bf16[64,512]{1,0:T(8,128)(2,1)S(1)} %add_convert_fusion.1), channel_id=1, source_target_pairs={{0,24},{8,16},{16,8},{24,0},{1,25},{9,17},{17,9},{25,1},{2,26},{10... | collective-permute-start | bytes 196616 | tf_op jit(solution)/shard_map/ppermute | solution.py:407
  43.1 1.6 %collective-permute-start.14 = (bf16[256,512]{1,0:T(8,128)(2,1)S(1)}, bf16[256,512]{1,0:T(8,128)(2,1)S(1)}, u32[]{:S(2)}, u32[]{:S(2)}) collective-permute-start(bf16[256,512]{1,0:T(8,128)(2,1)S(1)} %bitcast.28), channel_id=1, source_target_pairs={{0,1},{1,0},{2,3},{3,2},{4,5},{5,4},{6,7},{7,6},{8,9},{9,8},{10,11... | collective-permute-start | bytes 786440 | tf_op jit(solution)/shard_map/ppermute | solution.py:407

commit v5 on v4

--- a/solution.py
+++ b/solution.py
@@ -263,11 +263,8 @@
         for strand in range(2):
             row8 = across(weight, strand)
             base = strand * CONVW
-            for c in range(4):
-                half = mm(conv_ref[side, base + c * 128 : base + (c + 1) * 128, :], hot).astype(BF16)
-                far_s[strand, c * 128 : (c + 1) * 128, at] = per_head(
-                    silu_half(half), row8.astype(BF16), 2 * c
-                )
+            half = mm(conv_ref[side, base : base + INNER, :], hot).astype(BF16)
+            far_s[strand, :, at] = per_head(silu_half(half), row8.astype(BF16), 0)
             b_t = silu_half(mm(conv_ref[side, base + INNER : base + INNER + STATE, :], hot))
             farb_s[strand, :STATE, at] = jnp.where(side == 0, b_t, 0.0).astype(BF16)
             farb_s[strand, STATE:, at] = jnp.where(side == 0, 0.0, b_t).astype(BF16)
@@ -304,8 +301,8 @@
             hot, steps, cums, tots, _ = sides[side]
             row8 = across(steps, strand)
             for c in range(4):
-                half = mm(conv_ref[side, base + c * 128 : base + (c + 1) * 128, :], hot)
-                x = per_head(silu_half(half), row8, 2 * c).astype(BF16)
+                half = mm(conv_ref[side, base + c * 128 : base + (c + 1) * 128, :], hot).astype(BF16)
+                x = per_head(silu_half(half), row8.astype(BF16), 2 * c)
                 for b in range(nb):
                     to = (b * 2 + side) * SPAN
                     own_s[strand, c * 128 : (c + 1) * 128, to : to + SPAN] = x[:, b * SPAN : (b + 1) * SPAN]

time: 46.1 us -> 46.1 us (level)
  no operation moved by 1% of the time
where the time goes in v5:
time: 46.1 us; the launch traced here: 45.9 us
  starting transfers between devices  17.8 us (39%)
  waiting for transfers between devices  15.9 us (34%)
  Pallas kernels  9.33 us (20%)
  other arithmetic  2.06 us (4%)
  between operations  0.77 us (2%)
    ppermute x15, starting transfers between devices, swap(): lax.ppermute(value, axis, [(i, i ^ k) for i in range(lax.axis_size(axis))])  17.8 us
    ppermute x15, waiting for transfers between devices, swap(): lax.ppermute(value, axis, [(i, i ^ k) for i in range(lax.axis_size(axis))])  15.9 us
    pallas_call x1, Pallas kernels, per_device(): pl.pallas_call(functools.partial(layer_kernel, n, length, lax.axis_size('...  6.65 us
    pallas_call x1, Pallas kernels, per_device(): pl.pallas_call(tables_kernel, in_specs=[pl.BlockSpec(memory_space=pltpu.H...  2.68 us
    convert_element_type x1, other arithmetic, sum_all(): return jnp.concatenate([low, high], axis=0).astype(F32)  1.1 us
  transfers between devices with their start and end apart: 15, of which 12 were waited for; matrix products, arithmetic and copies ran while one was open for 1% of the time, Pallas kernels for 6%

profile of v5, /device:TPU:0, one launch (start us, length us, event | category | flops | bytes accessed | tf_op | source)
XLA Modules:
  0.0 45.9 jit_solution(8451685470985228223)
XLA Ops:
  0.6 0.0 copy-start
  0.6 0.5 %collective-permute-start = (s32[1,256]{1,0:T(1,128)}, s32[1,256]{1,0:T(1,128)S(1)}, u32[]{:S(2)}, u32[]{:S(2)}) collective-permute-start(s32[1,256]{1,0:T(1,128)} %refs_10_.1), channel_id=1, source_target_pairs={{0,1},{1,0},{2,3},{3,2},{4,5},{5,4},{6,7},{7,6},{8,9},{9,8},{10,11... | collective-permute-start | bytes 3080 | tf_op jit(solution)/shard_map/ppermute | solution.py:404
  1.2 0.7 %convert_element_type.51 = f32[1,256]{1,0:T(1,128)S(1)} convert(s32[1,256]{1,0:T(1,128)} %refs_10_.1) | non-fusion elementwise | flops 256 | bytes 2048 | tf_op jit(solution)/shard_map/convert_element_type | solution.py:460
  1.8 0.3 collective-permute-done
  2.2 3.0 %collective-permute-start.1 = (f32[2,256]{1,0:T(2,128)S(1)}, f32[2,256]{1,0:T(2,128)S(1)}, u32[]{:S(2)}, u32[]{:S(2)}) collective-permute-start(f32[2,256]{1,0:T(2,128)S(1)} %pad_maximum_fusion.1), channel_id=1, source_target_pairs={{0,2},{1,3},{2,0},{3,1},{4,6},{5,7},{6,4},{7,5},{8,10},{9,11},{10,... | collective-permute-start | bytes 6152 | tf_op jit(solution)/shard_map/ppermute | solution.py:404
  5.2 2.6 %collective-permute-start.2 = (f32[2,256]{1,0:T(2,128)S(1)}, f32[2,256]{1,0:T(2,128)S(1)}, u32[]{:S(2)}, u32[]{:S(2)}) collective-permute-start(f32[2,256]{1,0:T(2,128)S(1)} %pad_maximum_fusion.1), channel_id=1, source_target_pairs={{0,4},{1,5},{2,6},{3,7},{4,0},{5,1},{6,2},{7,3},{8,12},{9,13},{10,... | collective-permute-start | bytes 6152 | tf_op jit(solution)/shard_map/ppermute | solution.py:404
  7.7 0.0 collective-permute-start.3
  7.7 2.7 %tables.1 = (bf16[2,1280,64]{2,1,0:T(8,128)(2,1)S(1)}, f32[1024,256]{1,0:T(8,128)S(1)}, f32[2,2,8,8]{3,2,1,0:T(8,128)S(1)}, f32[2,2,8,8]{3,2,1,0:T(8,128)S(1)}, ...) custom-call(bf16[6,512]{1,0:T(8,128)(2,1)} %refs_0_.1, f32[1,512]{1,0:T(1,128)} %bitcast.31, ...), custom_call_target="tpu_custom_call" | custom-call | flops 20000000 | bytes 3000000 | tf_op jit(solution)/shard_map/tables/pallas_call | solution.py:474
  10.4 0.0 collective-permute-done.1
  10.5 0.0 collective-permute-done.2
  10.5 2.7 %collective-permute-done.3 = f32[2,256]{1,0:T(2,128)S(1)} collective-permute-done((f32[2,256]{1,0:T(2,128)S(1)}, f32[2,256]{1,0:T(2,128)S(1)}, u32[]{:S(2)}, u32[]{:S(2)}) %collective-permute-start.3) | collective-permute-done | bytes 2080 | tf_op jit(solution)/shard_map/ppermute | solution.py:404
  13.2 0.0 copy-done
  13.2 6.6 %layer.1 = (bf16[256,512]{1,0:T(8,128)(2,1)}, bf16[256,512]{1,0:T(8,128)(2,1)S(1)}, bf16[256,512]{1,0:T(8,128)(2,1)S(1)}) custom-call(f32[8,256]{1,0:T(8,128)S(1)} %concatenate.11.tok_ref, bf16[2,1280,64]{2,1,0:T(8,128)(2,1)S(1)} %get-tuple-element.12.conv_ref, f32[1024,256]{1,0:T(8,128)S(1)} %get-tuple-element.13.gate_ref, ...), custom_call_target="tpu_custom_call" | custom-call | flops 2000000000 | bytes 4000000 | tf_op jit(solution)/shard_map/layer/pallas_call | solution.py:496
  19.8 0.1 collective-permute-start.4
  19.9 1.5 %collective-permute-done.4 = bf16[256,512]{1,0:T(8,128)(2,1)S(1)} collective-permute-done((bf16[256,512]{1,0:T(8,128)(2,1)S(1)}, bf16[256,512]{1,0:T(8,128)(2,1)S(1)}, u32[]{:S(2)}, u32[]{:S(2)}) %collective-permute-start.4) | collective-permute-done | bytes 262176 | tf_op jit(solution)/shard_map/ppermute | solution.py:404
  21.4 0.1 add_convert_fusion
  21.5 1.6 %collective-permute-start.5 = (bf16[64,512]{1,0:T(8,128)(2,1)S(1)}, bf16[64,512]{1,0:T(8,128)(2,1)S(1)}, u32[]{:S(2)}, u32[]{:S(2)}) collective-permute-start(bf16[64,512]{1,0:T(8,128)(2,1)S(1)} %get-tuple-element.28), channel_id=1, source_target_pairs={{0,8},{8,0},{16,24},{24,16},{1,9},{9,1},{17,25},{25,17},{2,10},{10... | collective-permute-start | bytes 196616 | tf_op jit(solution)/shard_map/ppermute | solution.py:404
  23.1 1.5 %collective-permute-start.6 = (bf16[64,512]{1,0:T(8,128)(2,1)S(1)}, bf16[64,512]{1,0:T(8,128)(2,1)S(1)}, u32[]{:S(2)}, u32[]{:S(2)}) collective-permute-start(bf16[64,512]{1,0:T(8,128)(2,1)S(1)} %get-tuple-element.30), channel_id=1, source_target_pairs={{0,16},{8,24},{16,0},{24,8},{1,17},{9,25},{17,1},{25,9},{2,18},{10... | collective-permute-start | bytes 196616 | tf_op jit(solution)/shard_map/ppermute | solution.py:404
  24.6 0.5 %collective-permute-start.7 = (bf16[64,512]{1,0:T(8,128)(2,1)S(1)}, bf16[64,512]{1,0:T(8,128)(2,1)S(1)}, u32[]{:S(2)}, u32[]{:S(2)}) collective-permute-start(bf16[64,512]{1,0:T(8,128)(2,1)S(1)} %get-tuple-element.29), channel_id=1, source_target_pairs={{0,24},{8,16},{16,8},{24,0},{1,25},{9,17},{17,9},{25,1},{2,26},{10... | collective-permute-start | bytes 196616 | tf_op jit(solution)/shard_map/ppermute | solution.py:404
  25.1 0.8 %collective-permute-done.5 = bf16[64,512]{1,0:T(8,128)(2,1)S(1)} collective-permute-done((bf16[64,512]{1,0:T(8,128)(2,1)S(1)}, bf16[64,512]{1,0:T(8,128)(2,1)S(1)}, u32[]{:S(2)}, u32[]{:S(2)}) %collective-permute-start.5) | collective-permute-done | bytes 65568 | tf_op jit(solution)/shard_map/ppermute | solution.py:404
  25.9 1.5 %collective-permute-done.6 = bf16[64,512]{1,0:T(8,128)(2,1)S(1)} collective-permute-done((bf16[64,512]{1,0:T(8,128)(2,1)S(1)}, bf16[64,512]{1,0:T(8,128)(2,1)S(1)}, u32[]{:S(2)}, u32[]{:S(2)}) %collective-permute-start.6) | collective-permute-done | bytes 65568 | tf_op jit(solution)/shard_map/ppermute | solution.py:404
  27.3 2.4 %collective-permute-done.7 = bf16[64,512]{1,0:T(8,128)(2,1)S(1)} collective-permute-done((bf16[64,512]{1,0:T(8,128)(2,1)S(1)}, bf16[64,512]{1,0:T(8,128)(2,1)S(1)}, u32[]{:S(2)}, u32[]{:S(2)}) %collective-permute-start.7) | collective-permute-done | bytes 65568 | tf_op jit(solution)/shard_map/ppermute | solution.py:404
  29.8 1.2 %collective-permute-start.10 = (bf16[64,512]{1,0:T(8,128)(2,1)S(1)}, bf16[64,512]{1,0:T(8,128)(2,1)S(1)}, u32[]{:S(2)}, u32[]{:S(2)}) collective-permute-start(bf16[64,512]{1,0:T(8,128)(2,1)S(1)} %fusion.1), channel_id=1, source_target_pairs={{0,6},{1,7},{2,4},{3,5},{4,2},{5,3},{6,0},{7,1},{8,14},{9,15},{10,... | collective-permute-start | bytes 196616 | tf_op jit(solution)/shard_map/ppermute | solution.py:404
  31.0 0.0 collective-permute-start.8
  31.0 3.2 %collective-permute-start.9 = (bf16[64,512]{1,0:T(8,128)(2,1)S(1)}, bf16[64,512]{1,0:T(8,128)(2,1)S(1)}, u32[]{:S(2)}, u32[]{:S(2)}) collective-permute-start(bf16[64,512]{1,0:T(8,128)(2,1)S(1)} %fusion.1), channel_id=1, source_target_pairs={{0,4},{1,5},{2,6},{3,7},{4,0},{5,1},{6,2},{7,3},{8,12},{9,13},{10,... | collective-permute-start | bytes 196616 | tf_op jit(solution)/shard_map/ppermute | solution.py:404
  34.3 1.8 %collective-permute-done.10 = bf16[64,512]{1,0:T(8,128)(2,1)S(1)} collective-permute-done((bf16[64,512]{1,0:T(8,128)(2,1)S(1)}, bf16[64,512]{1,0:T(8,128)(2,1)S(1)}, u32[]{:S(2)}, u32[]{:S(2)}) %collective-permute-start.10) | collective-permute-done | bytes 65568 | tf_op jit(solution)/shard_map/ppermute | solution.py:404
  36.0 0.0 collective-permute-done.8
  36.0 0.7 %collective-permute-done.9 = bf16[64,512]{1,0:T(8,128)(2,1)S(1)} collective-permute-done((bf16[64,512]{1,0:T(8,128)(2,1)S(1)}, bf16[64,512]{1,0:T(8,128)(2,1)S(1)}, u32[]{:S(2)}, u32[]{:S(2)}) %collective-permute-start.9) | collective-permute-done | bytes 65568 | tf_op jit(solution)/shard_map/ppermute | solution.py:404
  36.7 0.6 %collective-permute-start.11 = (bf16[64,512]{1,0:T(8,128)(2,1)S(1)}, bf16[64,512]{1,0:T(8,128)(2,1)S(1)}, u32[]{:S(2)}, u32[]{:S(2)}) collective-permute-start(bf16[64,512]{1,0:T(8,128)(2,1)S(1)} %add_convert_fusion.1), channel_id=1, source_target_pairs={{0,8},{8,0},{16,24},{24,16},{1,9},{9,1},{17,25},{25,17},{2,10},{10... | collective-permute-start | bytes 196616 | tf_op jit(solution)/shard_map/ppermute | solution.py:404
  37.3 0.5 %collective-permute-start.12 = (bf16[64,512]{1,0:T(8,128)(2,1)S(1)}, bf16[64,512]{1,0:T(8,128)(2,1)S(1)}, u32[]{:S(2)}, u32[]{:S(2)}) collective-permute-start(bf16[64,512]{1,0:T(8,128)(2,1)S(1)} %add_convert_fusion.1), channel_id=1, source_target_pairs={{0,16},{8,24},{16,0},{24,8},{1,17},{9,25},{17,1},{25,9},{2,18},{10... | collective-permute-start | bytes 196616 | tf_op jit(solution)/shard_map/ppermute | solution.py:404
  37.9 2.4 %collective-permute-start.13 = (bf16[64,512]{1,0:T(8,128)(2,1)S(1)}, bf16[64,512]{1,0:T(8,128)(2,1)S(1)}, u32[]{:S(2)}, u32[]{:S(2)}) collective-permute-start(bf16[64,512]{1,0:T(8,128)(2,1)S(1)} %add_convert_fusion.1), channel_id=1, source_target_pairs={{0,24},{8,16},{16,8},{24,0},{1,25},{9,17},{17,9},{25,1},{2,26},{10... | collective-permute-start | bytes 196616 | tf_op jit(solution)/shard_map/ppermute | solution.py:404
  40.3 0.8 %collective-permute-done.11 = bf16[64,512]{1,0:T(8,128)(2,1)S(1)} collective-permute-done((bf16[64,512]{1,0:T(8,128)(2,1)S(1)}, bf16[64,512]{1,0:T(8,128)(2,1)S(1)}, u32[]{:S(2)}, u32[]{:S(2)}) %collective-permute-start.11) | collective-permute-done | bytes 65568 | tf_op jit(solution)/shard_map/ppermute | solution.py:404
  41.1 0.5 %collective-permute-done.12 = bf16[64,512]{1,0:T(8,128)(2,1)S(1)} collective-permute-done((bf16[64,512]{1,0:T(8,128)(2,1)S(1)}, bf16[64,512]{1,0:T(8,128)(2,1)S(1)}, u32[]{:S(2)}, u32[]{:S(2)}) %collective-permute-start.12) | collective-permute-done | bytes 65568 | tf_op jit(solution)/shard_map/ppermute | solution.py:404
  41.6 1.4 %collective-permute-done.13 = bf16[64,512]{1,0:T(8,128)(2,1)S(1)} collective-permute-done((bf16[64,512]{1,0:T(8,128)(2,1)S(1)}, bf16[64,512]{1,0:T(8,128)(2,1)S(1)}, u32[]{:S(2)}, u32[]{:S(2)}) %collective-permute-start.13) | collective-permute-done | bytes 65568 | tf_op jit(solution)/shard_map/ppermute | solution.py:404
  43.1 0.1 collective-permute-start.14
  43.2 1.5 %collective-permute-done.14 = bf16[256,512]{1,0:T(8,128)(2,1)S(1)} collective-permute-done((bf16[256,512]{1,0:T(8,128)(2,1)S(1)}, bf16[256,512]{1,0:T(8,128)(2,1)S(1)}, u32[]{:S(2)}, u32[]{:S(2)}) %collective-permute-start.14) | collective-permute-done | bytes 262176 | tf_op jit(solution)/shard_map/ppermute | solution.py:404
  44.7 0.1 broadcast_select_fusion.1
  44.8 1.1 %maximum_convert_fusion = f32[512,512]{1,0:T(8,128)} fusion(bf16[256,512]{1,0:T(8,128)(2,1)S(1)} %get-tuple-element.23, bf16[256,512]{1,0:T(8,128)(2,1)S(1)} %get-tuple-element.22), kind=kLoop, calls=%fused_computation | loop fusion | flops 1048576 | bytes 1572864 | tf_op jit(solution)/shard_map/convert_element_type | solution.py:447
  (8 shorter events, 0.2 us)
Async XLA Ops:
  0.6 12.5 %copy-start = (bf16[512,512]{1,0:T(8,128)(2,1)S(1)}, bf16[512,512]{1,0:T(8,128)(2,1)}, u32[]{:S(2)}) copy-start(bf16[512,512]{1,0:T(8,128)(2,1)} %wout_ref.1) | copy-start | bytes 1572868
  0.6 1.5 %collective-permute-start = (s32[1,256]{1,0:T(1,128)}, s32[1,256]{1,0:T(1,128)S(1)}, u32[]{:S(2)}, u32[]{:S(2)}) collective-permute-start(s32[1,256]{1,0:T(1,128)} %refs_10_.1), channel_id=1, source_target_pairs={{0,1},{1,0},{2,3},{3,2},{4,5},{5,4},{6,7},{7,6},{8,9},{9,8},{10,11... | collective-permute-start | bytes 3080 | tf_op jit(solution)/shard_map/ppermute | solution.py:404
  2.2 8.2 %collective-permute-start.1 = (f32[2,256]{1,0:T(2,128)S(1)}, f32[2,256]{1,0:T(2,128)S(1)}, u32[]{:S(2)}, u32[]{:S(2)}) collective-permute-start(f32[2,256]{1,0:T(2,128)S(1)} %pad_maximum_fusion.1), channel_id=1, source_target_pairs={{0,2},{1,3},{2,0},{3,1},{4,6},{5,7},{6,4},{7,5},{8,10},{9,11},{10,... | collective-permute-start | bytes 6152 | tf_op jit(solution)/shard_map/ppermute | solution.py:404
  5.2 5.3 %collective-permute-start.2 = (f32[2,256]{1,0:T(2,128)S(1)}, f32[2,256]{1,0:T(2,128)S(1)}, u32[]{:S(2)}, u32[]{:S(2)}) collective-permute-start(f32[2,256]{1,0:T(2,128)S(1)} %pad_maximum_fusion.1), channel_id=1, source_target_pairs={{0,4},{1,5},{2,6},{3,7},{4,0},{5,1},{6,2},{7,3},{8,12},{9,13},{10,... | collective-permute-start | bytes 6152 | tf_op jit(solution)/shard_map/ppermute | solution.py:404
  7.7 5.4 %collective-permute-start.3 = (f32[2,256]{1,0:T(2,128)S(1)}, f32[2,256]{1,0:T(2,128)S(1)}, u32[]{:S(2)}, u32[]{:S(2)}) collective-permute-start(f32[2,256]{1,0:T(2,128)S(1)} %pad_maximum_fusion.1), channel_id=1, source_target_pairs={{0,6},{1,7},{2,4},{3,5},{4,2},{5,3},{6,0},{7,1},{8,14},{9,15},{10,... | collective-permute-start | bytes 6152 | tf_op jit(solution)/shard_map/ppermute | solution.py:404
  19.8 1.6 %collective-permute-start.4 = (bf16[256,512]{1,0:T(8,128)(2,1)S(1)}, bf16[256,512]{1,0:T(8,128)(2,1)S(1)}, u32[]{:S(2)}, u32[]{:S(2)}) collective-permute-start(bf16[256,512]{1,0:T(8,128)(2,1)S(1)} %get-tuple-element.21), channel_id=1, source_target_pairs={{0,1},{1,0},{2,3},{3,2},{4,5},{5,4},{6,7},{7,6},{8,9},{9,8},{10,11... | collective-permute-start | bytes 786440 | tf_op jit(solution)/shard_map/ppermute | solution.py:404
  21.5 4.3 %collective-permute-start.5 = (bf16[64,512]{1,0:T(8,128)(2,1)S(1)}, bf16[64,512]{1,0:T(8,128)(2,1)S(1)}, u32[]{:S(2)}, u32[]{:S(2)}) collective-permute-start(bf16[64,512]{1,0:T(8,128)(2,1)S(1)} %get-tuple-element.28), channel_id=1, source_target_pairs={{0,8},{8,0},{16,24},{24,16},{1,9},{9,1},{17,25},{25,17},{2,10},{10... | collective-permute-start | bytes 196616 | tf_op jit(solution)/shard_map/ppermute | solution.py:404
  23.1 4.3 %collective-permute-start.6 = (bf16[64,512]{1,0:T(8,128)(2,1)S(1)}, bf16[64,512]{1,0:T(8,128)(2,1)S(1)}, u32[]{:S(2)}, u32[]{:S(2)}) collective-permute-start(bf16[64,512]{1,0:T(8,128)(2,1)S(1)} %get-tuple-element.30), channel_id=1, source_target_pairs={{0,16},{8,24},{16,0},{24,8},{1,17},{9,25},{17,1},{25,9},{2,18},{10... | collective-permute-start | bytes 196616 | tf_op jit(solution)/shard_map/ppermute | solution.py:404
  24.6 5.2 %collective-permute-start.7 = (bf16[64,512]{1,0:T(8,128)(2,1)S(1)}, bf16[64,512]{1,0:T(8,128)(2,1)S(1)}, u32[]{:S(2)}, u32[]{:S(2)}) collective-permute-start(bf16[64,512]{1,0:T(8,128)(2,1)S(1)} %get-tuple-element.29), channel_id=1, source_target_pairs={{0,24},{8,16},{16,8},{24,0},{1,25},{9,17},{17,9},{25,1},{2,26},{10... | collective-permute-start | bytes 196616 | tf_op jit(solution)/shard_map/ppermute | solution.py:404
  29.8 6.2 %collective-permute-start.10 = (bf16[64,512]{1,0:T(8,128)(2,1)S(1)}, bf16[64,512]{1,0:T(8,128)(2,1)S(1)}, u32[]{:S(2)}, u32[]{:S(2)}) collective-permute-start(bf16[64,512]{1,0:T(8,128)(2,1)S(1)} %fusion.1), channel_id=1, source_target_pairs={{0,6},{1,7},{2,4},{3,5},{4,2},{5,3},{6,0},{7,1},{8,14},{9,15},{10,... | collective-permute-start | bytes 196616 | tf_op jit(solution)/shard_map/ppermute | solution.py:404
  31.0 5.0 %collective-permute-start.8 = (bf16[64,512]{1,0:T(8,128)(2,1)S(1)}, bf16[64,512]{1,0:T(8,128)(2,1)S(1)}, u32[]{:S(2)}, u32[]{:S(2)}) collective-permute-start(bf16[64,512]{1,0:T(8,128)(2,1)S(1)} %fusion.1), channel_id=1, source_target_pairs={{0,2},{1,3},{2,0},{3,1},{4,6},{5,7},{6,4},{7,5},{8,10},{9,11},{10,... | collective-permute-start | bytes 196616 | tf_op jit(solution)/shard_map/ppermute | solution.py:404
  31.0 5.7 %collective-permute-start.9 = (bf16[64,512]{1,0:T(8,128)(2,1)S(1)}, bf16[64,512]{1,0:T(8,128)(2,1)S(1)}, u32[]{:S(2)}, u32[]{:S(2)}) collective-permute-start(bf16[64,512]{1,0:T(8,128)(2,1)S(1)} %fusion.1), channel_id=1, source_target_pairs={{0,4},{1,5},{2,6},{3,7},{4,0},{5,1},{6,2},{7,3},{8,12},{9,13},{10,... | collective-permute-start | bytes 196616 | tf_op jit(solution)/shard_map/ppermute | solution.py:404
  36.7 4.3 %collective-permute-start.11 = (bf16[64,512]{1,0:T(8,128)(2,1)S(1)}, bf16[64,512]{1,0:T(8,128)(2,1)S(1)}, u32[]{:S(2)}, u32[]{:S(2)}) collective-permute-start(bf16[64,512]{1,0:T(8,128)(2,1)S(1)} %add_convert_fusion.1), channel_id=1, source_target_pairs={{0,8},{8,0},{16,24},{24,16},{1,9},{9,1},{17,25},{25,17},{2,10},{10... | collective-permute-start | bytes 196616 | tf_op jit(solution)/shard_map/ppermute | solution.py:404
  37.3 4.3 %collective-permute-start.12 = (bf16[64,512]{1,0:T(8,128)(2,1)S(1)}, bf16[64,512]{1,0:T(8,128)(2,1)S(1)}, u32[]{:S(2)}, u32[]{:S(2)}) collective-permute-start(bf16[64,512]{1,0:T(8,128)(2,1)S(1)} %add_convert_fusion.1), channel_id=1, source_target_pairs={{0,16},{8,24},{16,0},{24,8},{1,17},{9,25},{17,1},{25,9},{2,18},{10... | collective-permute-start | bytes 196616 | tf_op jit(solution)/shard_map/ppermute | solution.py:404
  37.9 5.2 %collective-permute-start.13 = (bf16[64,512]{1,0:T(8,128)(2,1)S(1)}, bf16[64,512]{1,0:T(8,128)(2,1)S(1)}, u32[]{:S(2)}, u32[]{:S(2)}) collective-permute-start(bf16[64,512]{1,0:T(8,128)(2,1)S(1)} %add_convert_fusion.1), channel_id=1, source_target_pairs={{0,24},{8,16},{16,8},{24,0},{1,25},{9,17},{17,9},{25,1},{2,26},{10... | collective-permute-start | bytes 196616 | tf_op jit(solution)/shard_map/ppermute | solution.py:404
  43.1 1.6 %collective-permute-start.14 = (bf16[256,512]{1,0:T(8,128)(2,1)S(1)}, bf16[256,512]{1,0:T(8,128)(2,1)S(1)}, u32[]{:S(2)}, u32[]{:S(2)}) collective-permute-start(bf16[256,512]{1,0:T(8,128)(2,1)S(1)} %bitcast.28), channel_id=1, source_target_pairs={{0,1},{1,0},{2,3},{3,2},{4,5},{5,4},{6,7},{7,6},{8,9},{9,8},{10,11... | collective-permute-start | bytes 786440 | tf_op jit(solution)/shard_map/ppermute | solution.py:404

commit v6 on v4

--- a/solution.py
+++ b/solution.py
@@ -128,7 +128,7 @@
 def layer_kernel(
     n, length, masked_total,
     tok_ref, conv_ref, gate_ref, step_ref, decay_ref, gain_ref, headt_ref, val_s, wout_ref,
-    layer_out, send_out, keep_out,
+    layer_hbm, send_out, keep_out, layer_out, sem,
     ids_s, step_s, log_s, cum_s, tot_s, own_s, from_s, near_s, far_s, farb_s, state_s, y_s, comb_s,
 ):
     me = lax.axis_index("seq")
@@ -375,6 +375,8 @@
     comb = jnp.transpose(comb_t.astype(F32)).astype(BF16)
     layer = mm(comb, wout_ref[...]).astype(BF16)
     layer_out[...] = layer
+    write = pltpu.make_async_copy(layer_out, layer_hbm, sem)
+    write.start()
     layer = layer.astype(F32)
     sigma = 0.5 + 0.5 * jnp.tanh(0.5 * layer)
     act_high, act_low = split_two(layer * sigma)
@@ -401,6 +403,7 @@
     keep_out[...] = mm(
         comb_s[pl.ds(pl.multiple_of(core * half, half), half), :], grad_layer
     ).astype(BF16)
+    write.wait()
 
 
 def swap(value, axis, k):
@@ -503,7 +506,14 @@
             pltpu.VMEM((INNER // 2, width), BF16),
             pltpu.VMEM((INNER // 2, width), BF16),
         ),
+        out_specs=(
+            pl.BlockSpec(memory_space=pltpu.HBM),
+            pl.BlockSpec(memory_space=pltpu.VMEM),
+            pl.BlockSpec(memory_space=pltpu.VMEM),
+        ),
         scratch_shapes=[
+            pltpu.VMEM((length, width), BF16),
+            pltpu.SemaphoreType.DMA,
             pltpu.VMEM((n + 2, length), F32),
             pltpu.VMEM((slots, rows, SPAN), F32),
             pltpu.VMEM((slots, rows, SPAN), F32),

time: 46.1 us -> 46.2 us (level)
  no operation moved by 1% of the time
where the time goes in v6:
time: 46.2 us; the launch traced here: 46 us
  starting transfers between devices  17.8 us (39%)
  waiting for transfers between devices  15.9 us (34%)
  Pallas kernels  9.47 us (20%)
  other arithmetic  2.06 us (4%)
  between operations  0.77 us (2%)
    ppermute x15, starting transfers between devices, swap(): lax.ppermute(value, axis, [(i, i ^ k) for i in range(lax.axis_size(axis))])  17.8 us
    ppermute x15, waiting for transfers between devices, swap(): lax.ppermute(value, axis, [(i, i ^ k) for i in range(lax.axis_size(axis))])  15.9 us
    pallas_call x1, Pallas kernels, per_device(): pl.pallas_call(functools.partial(layer_kernel, n, length, lax.axis_size('...  6.79 us
    pallas_call x1, Pallas kernels, per_device(): pl.pallas_call(tables_kernel, in_specs=[pl.BlockSpec(memory_space=pltpu.H...  2.68 us
    convert_element_type x1, other arithmetic, sum_all(): return jnp.concatenate([low, high], axis=0).astype(F32)  1.1 us
  transfers between devices with their start and end apart: 15, of which 12 were waited for; matrix products, arithmetic and copies ran while one was open for 1% of the time, Pallas kernels for 6%

profile of v6, /device:TPU:0, one launch (start us, length us, event | category | flops | bytes accessed | tf_op | source)
XLA Modules:
  0.0 46.0 jit_solution(17765736218386106109)
XLA Ops:
  0.6 0.0 copy-start
  0.6 0.5 %collective-permute-start = (s32[1,256]{1,0:T(1,128)}, s32[1,256]{1,0:T(1,128)S(1)}, u32[]{:S(2)}, u32[]{:S(2)}) collective-permute-start(s32[1,256]{1,0:T(1,128)} %refs_10_.1), channel_id=1, source_target_pairs={{0,1},{1,0},{2,3},{3,2},{4,5},{5,4},{6,7},{7,6},{8,9},{9,8},{10,11... | collective-permute-start | bytes 3080 | tf_op jit(solution)/shard_map/ppermute | solution.py:410
  1.2 0.7 %convert_element_type.51 = f32[1,256]{1,0:T(1,128)S(1)} convert(s32[1,256]{1,0:T(1,128)} %refs_10_.1) | non-fusion elementwise | flops 256 | bytes 2048 | tf_op jit(solution)/shard_map/convert_element_type | solution.py:466
  1.8 0.3 collective-permute-done
  2.2 3.0 %collective-permute-start.1 = (f32[2,256]{1,0:T(2,128)S(1)}, f32[2,256]{1,0:T(2,128)S(1)}, u32[]{:S(2)}, u32[]{:S(2)}) collective-permute-start(f32[2,256]{1,0:T(2,128)S(1)} %pad_maximum_fusion.1), channel_id=1, source_target_pairs={{0,2},{1,3},{2,0},{3,1},{4,6},{5,7},{6,4},{7,5},{8,10},{9,11},{10,... | collective-permute-start | bytes 6152 | tf_op jit(solution)/shard_map/ppermute | solution.py:410
  5.2 2.6 %collective-permute-start.2 = (f32[2,256]{1,0:T(2,128)S(1)}, f32[2,256]{1,0:T(2,128)S(1)}, u32[]{:S(2)}, u32[]{:S(2)}) collective-permute-start(f32[2,256]{1,0:T(2,128)S(1)} %pad_maximum_fusion.1), channel_id=1, source_target_pairs={{0,4},{1,5},{2,6},{3,7},{4,0},{5,1},{6,2},{7,3},{8,12},{9,13},{10,... | collective-permute-start | bytes 6152 | tf_op jit(solution)/shard_map/ppermute | solution.py:410
  7.7 0.0 collective-permute-start.3
  7.7 2.7 %tables.1 = (bf16[2,1280,64]{2,1,0:T(8,128)(2,1)S(1)}, f32[1024,256]{1,0:T(8,128)S(1)}, f32[2,2,8,8]{3,2,1,0:T(8,128)S(1)}, f32[2,2,8,8]{3,2,1,0:T(8,128)S(1)}, ...) custom-call(bf16[6,512]{1,0:T(8,128)(2,1)} %refs_0_.1, f32[1,512]{1,0:T(1,128)} %bitcast.31, ...), custom_call_target="tpu_custom_call" | custom-call | flops 20000000 | bytes 3000000 | tf_op jit(solution)/shard_map/tables/pallas_call | solution.py:480
  10.4 0.0 collective-permute-done.1
  10.5 0.0 collective-permute-done.2
  10.5 2.7 %collective-permute-done.3 = f32[2,256]{1,0:T(2,128)S(1)} collective-permute-done((f32[2,256]{1,0:T(2,128)S(1)}, f32[2,256]{1,0:T(2,128)S(1)}, u32[]{:S(2)}, u32[]{:S(2)}) %collective-permute-start.3) | collective-permute-done | bytes 2080 | tf_op jit(solution)/shard_map/ppermute | solution.py:410
  13.2 0.0 copy-done
  13.2 6.8 %layer.1 = (bf16[256,512]{1,0:T(8,128)(2,1)}, bf16[256,512]{1,0:T(8,128)(2,1)S(1)}, bf16[256,512]{1,0:T(8,128)(2,1)S(1)}) custom-call(f32[8,256]{1,0:T(8,128)S(1)} %concatenate.11.tok_ref, bf16[2,1280,64]{2,1,0:T(8,128)(2,1)S(1)} %get-tuple-element.12.conv_ref, f32[1024,256]{1,0:T(8,128)S(1)} %get-tuple-element.13.gate_ref, ...), custom_call_target="tpu_custom_call" | custom-call | flops 2000000000 | bytes 4000000 | tf_op jit(solution)/shard_map/layer/pallas_call | solution.py:502
  20.0 0.1 collective-permute-start.4
  20.1 1.5 %collective-permute-done.4 = bf16[256,512]{1,0:T(8,128)(2,1)S(1)} collective-permute-done((bf16[256,512]{1,0:T(8,128)(2,1)S(1)}, bf16[256,512]{1,0:T(8,128)(2,1)S(1)}, u32[]{:S(2)}, u32[]{:S(2)}) %collective-permute-start.4) | collective-permute-done | bytes 262176 | tf_op jit(solution)/shard_map/ppermute | solution.py:410
  21.6 0.1 add_convert_fusion
  21.7 1.6 %collective-permute-start.5 = (bf16[64,512]{1,0:T(8,128)(2,1)S(1)}, bf16[64,512]{1,0:T(8,128)(2,1)S(1)}, u32[]{:S(2)}, u32[]{:S(2)}) collective-permute-start(bf16[64,512]{1,0:T(8,128)(2,1)S(1)} %get-tuple-element.28), channel_id=1, source_target_pairs={{0,8},{8,0},{16,24},{24,16},{1,9},{9,1},{17,25},{25,17},{2,10},{10... | collective-permute-start | bytes 196616 | tf_op jit(solution)/shard_map/ppermute | solution.py:410
  23.2 1.5 %collective-permute-start.6 = (bf16[64,512]{1,0:T(8,128)(2,1)S(1)}, bf16[64,512]{1,0:T(8,128)(2,1)S(1)}, u32[]{:S(2)}, u32[]{:S(2)}) collective-permute-start(bf16[64,512]{1,0:T(8,128)(2,1)S(1)} %get-tuple-element.30), channel_id=1, source_target_pairs={{0,16},{8,24},{16,0},{24,8},{1,17},{9,25},{17,1},{25,9},{2,18},{10... | collective-permute-start | bytes 196616 | tf_op jit(solution)/shard_map/ppermute | solution.py:410
  24.7 0.5 %collective-permute-start.7 = (bf16[64,512]{1,0:T(8,128)(2,1)S(1)}, bf16[64,512]{1,0:T(8,128)(2,1)S(1)}, u32[]{:S(2)}, u32[]{:S(2)}) collective-permute-start(bf16[64,512]{1,0:T(8,128)(2,1)S(1)} %get-tuple-element.29), channel_id=1, source_target_pairs={{0,24},{8,16},{16,8},{24,0},{1,25},{9,17},{17,9},{25,1},{2,26},{10... | collective-permute-start | bytes 196616 | tf_op jit(solution)/shard_map/ppermute | solution.py:410
  25.2 0.8 %collective-permute-done.5 = bf16[64,512]{1,0:T(8,128)(2,1)S(1)} collective-permute-done((bf16[64,512]{1,0:T(8,128)(2,1)S(1)}, bf16[64,512]{1,0:T(8,128)(2,1)S(1)}, u32[]{:S(2)}, u32[]{:S(2)}) %collective-permute-start.5) | collective-permute-done | bytes 65568 | tf_op jit(solution)/shard_map/ppermute | solution.py:410
  26.0 1.5 %collective-permute-done.6 = bf16[64,512]{1,0:T(8,128)(2,1)S(1)} collective-permute-done((bf16[64,512]{1,0:T(8,128)(2,1)S(1)}, bf16[64,512]{1,0:T(8,128)(2,1)S(1)}, u32[]{:S(2)}, u32[]{:S(2)}) %collective-permute-start.6) | collective-permute-done | bytes 65568 | tf_op jit(solution)/shard_map/ppermute | solution.py:410
  27.5 2.4 %collective-permute-done.7 = bf16[64,512]{1,0:T(8,128)(2,1)S(1)} collective-permute-done((bf16[64,512]{1,0:T(8,128)(2,1)S(1)}, bf16[64,512]{1,0:T(8,128)(2,1)S(1)}, u32[]{:S(2)}, u32[]{:S(2)}) %collective-permute-start.7) | collective-permute-done | bytes 65568 | tf_op jit(solution)/shard_map/ppermute | solution.py:410
  29.9 1.2 %collective-permute-start.10 = (bf16[64,512]{1,0:T(8,128)(2,1)S(1)}, bf16[64,512]{1,0:T(8,128)(2,1)S(1)}, u32[]{:S(2)}, u32[]{:S(2)}) collective-permute-start(bf16[64,512]{1,0:T(8,128)(2,1)S(1)} %fusion.1), channel_id=1, source_target_pairs={{0,6},{1,7},{2,4},{3,5},{4,2},{5,3},{6,0},{7,1},{8,14},{9,15},{10,... | collective-permute-start | bytes 196616 | tf_op jit(solution)/shard_map/ppermute | solution.py:410
  31.2 0.0 collective-permute-start.8
  31.2 3.2 %collective-permute-start.9 = (bf16[64,512]{1,0:T(8,128)(2,1)S(1)}, bf16[64,512]{1,0:T(8,128)(2,1)S(1)}, u32[]{:S(2)}, u32[]{:S(2)}) collective-permute-start(bf16[64,512]{1,0:T(8,128)(2,1)S(1)} %fusion.1), channel_id=1, source_target_pairs={{0,4},{1,5},{2,6},{3,7},{4,0},{5,1},{6,2},{7,3},{8,12},{9,13},{10,... | collective-permute-start | bytes 196616 | tf_op jit(solution)/shard_map/ppermute | solution.py:410
  34.4 1.8 %collective-permute-done.10 = bf16[64,512]{1,0:T(8,128)(2,1)S(1)} collective-permute-done((bf16[64,512]{1,0:T(8,128)(2,1)S(1)}, bf16[64,512]{1,0:T(8,128)(2,1)S(1)}, u32[]{:S(2)}, u32[]{:S(2)}) %collective-permute-start.10) | collective-permute-done | bytes 65568 | tf_op jit(solution)/shard_map/ppermute | solution.py:410
  36.2 0.0 collective-permute-done.8
  36.2 0.7 %collective-permute-done.9 = bf16[64,512]{1,0:T(8,128)(2,1)S(1)} collective-permute-done((bf16[64,512]{1,0:T(8,128)(2,1)S(1)}, bf16[64,512]{1,0:T(8,128)(2,1)S(1)}, u32[]{:S(2)}, u32[]{:S(2)}) %collective-permute-start.9) | collective-permute-done | bytes 65568 | tf_op jit(solution)/shard_map/ppermute | solution.py:410
  36.9 0.6 %collective-permute-start.11 = (bf16[64,512]{1,0:T(8,128)(2,1)S(1)}, bf16[64,512]{1,0:T(8,128)(2,1)S(1)}, u32[]{:S(2)}, u32[]{:S(2)}) collective-permute-start(bf16[64,512]{1,0:T(8,128)(2,1)S(1)} %add_convert_fusion.1), channel_id=1, source_target_pairs={{0,8},{8,0},{16,24},{24,16},{1,9},{9,1},{17,25},{25,17},{2,10},{10... | collective-permute-start | bytes 196616 | tf_op jit(solution)/shard_map/ppermute | solution.py:410
  37.5 0.5 %collective-permute-start.12 = (bf16[64,512]{1,0:T(8,128)(2,1)S(1)}, bf16[64,512]{1,0:T(8,128)(2,1)S(1)}, u32[]{:S(2)}, u32[]{:S(2)}) collective-permute-start(bf16[64,512]{1,0:T(8,128)(2,1)S(1)} %add_convert_fusion.1), channel_id=1, source_target_pairs={{0,16},{8,24},{16,0},{24,8},{1,17},{9,25},{17,1},{25,9},{2,18},{10... | collective-permute-start | bytes 196616 | tf_op jit(solution)/shard_map/ppermute | solution.py:410
  38.0 2.4 %collective-permute-start.13 = (bf16[64,512]{1,0:T(8,128)(2,1)S(1)}, bf16[64,512]{1,0:T(8,128)(2,1)S(1)}, u32[]{:S(2)}, u32[]{:S(2)}) collective-permute-start(bf16[64,512]{1,0:T(8,128)(2,1)S(1)} %add_convert_fusion.1), channel_id=1, source_target_pairs={{0,24},{8,16},{16,8},{24,0},{1,25},{9,17},{17,9},{25,1},{2,26},{10... | collective-permute-start | bytes 196616 | tf_op jit(solution)/shard_map/ppermute | solution.py:410
  40.4 0.8 %collective-permute-done.11 = bf16[64,512]{1,0:T(8,128)(2,1)S(1)} collective-permute-done((bf16[64,512]{1,0:T(8,128)(2,1)S(1)}, bf16[64,512]{1,0:T(8,128)(2,1)S(1)}, u32[]{:S(2)}, u32[]{:S(2)}) %collective-permute-start.11) | collective-permute-done | bytes 65568 | tf_op jit(solution)/shard_map/ppermute | solution.py:410
  41.2 0.5 %collective-permute-done.12 = bf16[64,512]{1,0:T(8,128)(2,1)S(1)} collective-permute-done((bf16[64,512]{1,0:T(8,128)(2,1)S(1)}, bf16[64,512]{1,0:T(8,128)(2,1)S(1)}, u32[]{:S(2)}, u32[]{:S(2)}) %collective-permute-start.12) | collective-permute-done | bytes 65568 | tf_op jit(solution)/shard_map/ppermute | solution.py:410
  41.7 1.4 %collective-permute-done.13 = bf16[64,512]{1,0:T(8,128)(2,1)S(1)} collective-permute-done((bf16[64,512]{1,0:T(8,128)(2,1)S(1)}, bf16[64,512]{1,0:T(8,128)(2,1)S(1)}, u32[]{:S(2)}, u32[]{:S(2)}) %collective-permute-start.13) | collective-permute-done | bytes 65568 | tf_op jit(solution)/shard_map/ppermute | solution.py:410
  43.2 0.1 collective-permute-start.14
  43.3 1.5 %collective-permute-done.14 = bf16[256,512]{1,0:T(8,128)(2,1)S(1)} collective-permute-done((bf16[256,512]{1,0:T(8,128)(2,1)S(1)}, bf16[256,512]{1,0:T(8,128)(2,1)S(1)}, u32[]{:S(2)}, u32[]{:S(2)}) %collective-permute-start.14) | collective-permute-done | bytes 262176 | tf_op jit(solution)/shard_map/ppermute | solution.py:410
  44.8 0.1 broadcast_select_fusion.1
  44.9 1.1 %maximum_convert_fusion = f32[512,512]{1,0:T(8,128)} fusion(bf16[256,512]{1,0:T(8,128)(2,1)S(1)} %get-tuple-element.23, bf16[256,512]{1,0:T(8,128)(2,1)S(1)} %get-tuple-element.22), kind=kLoop, calls=%fused_computation | loop fusion | flops 1048576 | bytes 1572864 | tf_op jit(solution)/shard_map/convert_element_type | solution.py:453
  (8 shorter events, 0.2 us)
Async XLA Ops:
  0.6 12.5 %copy-start = (bf16[512,512]{1,0:T(8,128)(2,1)S(1)}, bf16[512,512]{1,0:T(8,128)(2,1)}, u32[]{:S(2)}) copy-start(bf16[512,512]{1,0:T(8,128)(2,1)} %wout_ref.1) | copy-start | bytes 1572868
  0.6 1.5 %collective-permute-start = (s32[1,256]{1,0:T(1,128)}, s32[1,256]{1,0:T(1,128)S(1)}, u32[]{:S(2)}, u32[]{:S(2)}) collective-permute-start(s32[1,256]{1,0:T(1,128)} %refs_10_.1), channel_id=1, source_target_pairs={{0,1},{1,0},{2,3},{3,2},{4,5},{5,4},{6,7},{7,6},{8,9},{9,8},{10,11... | collective-permute-start | bytes 3080 | tf_op jit(solution)/shard_map/ppermute | solution.py:410
  2.2 8.2 %collective-permute-start.1 = (f32[2,256]{1,0:T(2,128)S(1)}, f32[2,256]{1,0:T(2,128)S(1)}, u32[]{:S(2)}, u32[]{:S(2)}) collective-permute-start(f32[2,256]{1,0:T(2,128)S(1)} %pad_maximum_fusion.1), channel_id=1, source_target_pairs={{0,2},{1,3},{2,0},{3,1},{4,6},{5,7},{6,4},{7,5},{8,10},{9,11},{10,... | collective-permute-start | bytes 6152 | tf_op jit(solution)/shard_map/ppermute | solution.py:410
  5.2 5.3 %collective-permute-start.2 = (f32[2,256]{1,0:T(2,128)S(1)}, f32[2,256]{1,0:T(2,128)S(1)}, u32[]{:S(2)}, u32[]{:S(2)}) collective-permute-start(f32[2,256]{1,0:T(2,128)S(1)} %pad_maximum_fusion.1), channel_id=1, source_target_pairs={{0,4},{1,5},{2,6},{3,7},{4,0},{5,1},{6,2},{7,3},{8,12},{9,13},{10,... | collective-permute-start | bytes 6152 | tf_op jit(solution)/shard_map/ppermute | solution.py:410
  7.7 5.4 %collective-permute-start.3 = (f32[2,256]{1,0:T(2,128)S(1)}, f32[2,256]{1,0:T(2,128)S(1)}, u32[]{:S(2)}, u32[]{:S(2)}) collective-permute-start(f32[2,256]{1,0:T(2,128)S(1)} %pad_maximum_fusion.1), channel_id=1, source_target_pairs={{0,6},{1,7},{2,4},{3,5},{4,2},{5,3},{6,0},{7,1},{8,14},{9,15},{10,... | collective-permute-start | bytes 6152 | tf_op jit(solution)/shard_map/ppermute | solution.py:410
  20.0 1.6 %collective-permute-start.4 = (bf16[256,512]{1,0:T(8,128)(2,1)S(1)}, bf16[256,512]{1,0:T(8,128)(2,1)S(1)}, u32[]{:S(2)}, u32[]{:S(2)}) collective-permute-start(bf16[256,512]{1,0:T(8,128)(2,1)S(1)} %get-tuple-element.21), channel_id=1, source_target_pairs={{0,1},{1,0},{2,3},{3,2},{4,5},{5,4},{6,7},{7,6},{8,9},{9,8},{10,11... | collective-permute-start | bytes 786440 | tf_op jit(solution)/shard_map/ppermute | solution.py:410
  21.7 4.3 %collective-permute-start.5 = (bf16[64,512]{1,0:T(8,128)(2,1)S(1)}, bf16[64,512]{1,0:T(8,128)(2,1)S(1)}, u32[]{:S(2)}, u32[]{:S(2)}) collective-permute-start(bf16[64,512]{1,0:T(8,128)(2,1)S(1)} %get-tuple-element.28), channel_id=1, source_target_pairs={{0,8},{8,0},{16,24},{24,16},{1,9},{9,1},{17,25},{25,17},{2,10},{10... | collective-permute-start | bytes 196616 | tf_op jit(solution)/shard_map/ppermute | solution.py:410
  23.2 4.3 %collective-permute-start.6 = (bf16[64,512]{1,0:T(8,128)(2,1)S(1)}, bf16[64,512]{1,0:T(8,128)(2,1)S(1)}, u32[]{:S(2)}, u32[]{:S(2)}) collective-permute-start(bf16[64,512]{1,0:T(8,128)(2,1)S(1)} %get-tuple-element.30), channel_id=1, source_target_pairs={{0,16},{8,24},{16,0},{24,8},{1,17},{9,25},{17,1},{25,9},{2,18},{10... | collective-permute-start | bytes 196616 | tf_op jit(solution)/shard_map/ppermute | solution.py:410
  24.7 5.2 %collective-permute-start.7 = (bf16[64,512]{1,0:T(8,128)(2,1)S(1)}, bf16[64,512]{1,0:T(8,128)(2,1)S(1)}, u32[]{:S(2)}, u32[]{:S(2)}) collective-permute-start(bf16[64,512]{1,0:T(8,128)(2,1)S(1)} %get-tuple-element.29), channel_id=1, source_target_pairs={{0,24},{8,16},{16,8},{24,0},{1,25},{9,17},{17,9},{25,1},{2,26},{10... | collective-permute-start | bytes 196616 | tf_op jit(solution)/shard_map/ppermute | solution.py:410
  29.9 6.2 %collective-permute-start.10 = (bf16[64,512]{1,0:T(8,128)(2,1)S(1)}, bf16[64,512]{1,0:T(8,128)(2,1)S(1)}, u32[]{:S(2)}, u32[]{:S(2)}) collective-permute-start(bf16[64,512]{1,0:T(8,128)(2,1)S(1)} %fusion.1), channel_id=1, source_target_pairs={{0,6},{1,7},{2,4},{3,5},{4,2},{5,3},{6,0},{7,1},{8,14},{9,15},{10,... | collective-permute-start | bytes 196616 | tf_op jit(solution)/shard_map/ppermute | solution.py:410
  31.2 5.0 %collective-permute-start.8 = (bf16[64,512]{1,0:T(8,128)(2,1)S(1)}, bf16[64,512]{1,0:T(8,128)(2,1)S(1)}, u32[]{:S(2)}, u32[]{:S(2)}) collective-permute-start(bf16[64,512]{1,0:T(8,128)(2,1)S(1)} %fusion.1), channel_id=1, source_target_pairs={{0,2},{1,3},{2,0},{3,1},{4,6},{5,7},{6,4},{7,5},{8,10},{9,11},{10,... | collective-permute-start | bytes 196616 | tf_op jit(solution)/shard_map/ppermute | solution.py:410
  31.2 5.7 %collective-permute-start.9 = (bf16[64,512]{1,0:T(8,128)(2,1)S(1)}, bf16[64,512]{1,0:T(8,128)(2,1)S(1)}, u32[]{:S(2)}, u32[]{:S(2)}) collective-permute-start(bf16[64,512]{1,0:T(8,128)(2,1)S(1)} %fusion.1), channel_id=1, source_target_pairs={{0,4},{1,5},{2,6},{3,7},{4,0},{5,1},{6,2},{7,3},{8,12},{9,13},{10,... | collective-permute-start | bytes 196616 | tf_op jit(solution)/shard_map/ppermute | solution.py:410
  36.9 4.3 %collective-permute-start.11 = (bf16[64,512]{1,0:T(8,128)(2,1)S(1)}, bf16[64,512]{1,0:T(8,128)(2,1)S(1)}, u32[]{:S(2)}, u32[]{:S(2)}) collective-permute-start(bf16[64,512]{1,0:T(8,128)(2,1)S(1)} %add_convert_fusion.1), channel_id=1, source_target_pairs={{0,8},{8,0},{16,24},{24,16},{1,9},{9,1},{17,25},{25,17},{2,10},{10... | collective-permute-start | bytes 196616 | tf_op jit(solution)/shard_map/ppermute | solution.py:410
  37.5 4.3 %collective-permute-start.12 = (bf16[64,512]{1,0:T(8,128)(2,1)S(1)}, bf16[64,512]{1,0:T(8,128)(2,1)S(1)}, u32[]{:S(2)}, u32[]{:S(2)}) collective-permute-start(bf16[64,512]{1,0:T(8,128)(2,1)S(1)} %add_convert_fusion.1), channel_id=1, source_target_pairs={{0,16},{8,24},{16,0},{24,8},{1,17},{9,25},{17,1},{25,9},{2,18},{10... | collective-permute-start | bytes 196616 | tf_op jit(solution)/shard_map/ppermute | solution.py:410
  38.0 5.2 %collective-permute-start.13 = (bf16[64,512]{1,0:T(8,128)(2,1)S(1)}, bf16[64,512]{1,0:T(8,128)(2,1)S(1)}, u32[]{:S(2)}, u32[]{:S(2)}) collective-permute-start(bf16[64,512]{1,0:T(8,128)(2,1)S(1)} %add_convert_fusion.1), channel_id=1, source_target_pairs={{0,24},{8,16},{16,8},{24,0},{1,25},{9,17},{17,9},{25,1},{2,26},{10... | collective-permute-start | bytes 196616 | tf_op jit(solution)/shard_map/ppermute | solution.py:410
  43.2 1.6 %collective-permute-start.14 = (bf16[256,512]{1,0:T(8,128)(2,1)S(1)}, bf16[256,512]{1,0:T(8,128)(2,1)S(1)}, u32[]{:S(2)}, u32[]{:S(2)}) collective-permute-start(bf16[256,512]{1,0:T(8,128)(2,1)S(1)} %bitcast.28), channel_id=1, source_target_pairs={{0,1},{1,0},{2,3},{3,2},{4,5},{5,4},{6,7},{7,6},{8,9},{9,8},{10,11... | collective-permute-start | bytes 786440 | tf_op jit(solution)/shard_map/ppermute | solution.py:410
